TPU v7x, 32 devices: a whole 2x2x4 slice. The times are simulated.
32 devices in a mesh: hst: 16 (over z, y, core), local: 2 (over x).
Axes of the slice: x: 2, y: 2, z: 4, core: 2. Of those that a mesh axis runs over, the one named last changes fastest.
Arguments:
- gate_act: bfloat16 [2048, 11008], P('hst', 'local'), may hold values from -6 to 6
- up_act: bfloat16 [2048, 11008], P('hst', 'local'), may hold values from -6 to 6
- cotangent: bfloat16 [2048, 4096], P('hst', 'local'), may hold values from -6 to 6
- down_weight: bfloat16 [11008, 4096], P('local', 'hst'), may hold values from -0.0546875 to 0.0546875
Outputs:
- output: bfloat16 [2048, 4096], P('hst', 'local')
- gate_delta: bfloat16 [2048, 11008], P('hst', 'local')
- up_delta: bfloat16 [2048, 11008], P('hst', 'local')
- down_grad: float32 [11008, 4096], P('local', 'hst')
All inputs are finite; a program needn't handle non-finite values.
Results may differ from a plain program's by a relative error of at most 0.005.
Values may be sent and summed in bfloat16 or wider, within the bound.
No kernel may reach another device: no remote copies, remote signals or barrier semaphores. Data moves between devices by JAX's collectives and lax.ppermute only.
A program may use at most 320 MiB of HBM per device.

v0:
```python
import jax
import jax.numpy as jnp
from jax import lax
from jax.sharding import PartitionSpec as P

QUAD = 4
ORDER = (0, 2, 1, 3)
KEEP_COLS = (((1,), (1,)), ((), ()))
SUM_ROWS = (((0,), (0,)), ((), ()))


def after(value, *others):
    return lax.optimization_barrier((value,) + others)[0] if others else value


def slot_of(near):
    return [((near ^ block) & 1) << 1 | (near ^ block) >> 1 for block in range(QUAD)]


def picked(view, places, axis):
    return jnp.concatenate(
        [lax.dynamic_slice_in_dim(view, place, 1, axis=axis) for place in places], axis=axis
    )


def solution(mesh):
    n_hst, n_local = mesh.shape["hst"], mesh.shape["local"]
    n_far = n_hst // QUAD
    last_hop = n_far - 1

    def swap(value, bit):
        return lax.ppermute(value, "hst", [(h, h ^ bit) for h in range(n_hst)])

    def shift(value, step):
        pairs = [(h, (h + step * QUAD) % n_hst) for h in range(n_hst)]
        return lax.ppermute(value, "hst", pairs)

    def far_permute(value, pairs):
        pairs = [(s * QUAD + q, t * QUAD + q) for s, t in pairs for q in range(QUAD)]
        return lax.ppermute(value, "hst", pairs)

    def both_ways(up, down, sources):
        return (
            far_permute(up, [(z, z + 1) for z in sources]),
            far_permute(down, [(n_far - 1 - z, n_far - 2 - z) for z in sources]),
        )

    def local_shift(value, step):
        return lax.ppermute(value, "local", [(i, (i + step) % n_local) for i in range(n_local)])

    def on_device(gate_act, up_act, cotangent, down_weight):
        h = lax.axis_index("hst")
        x = lax.axis_index("local")
        far, near = h // QUAD, h % QUAD
        tokens, half = cotangent.shape
        width = down_weight.shape[1]
        columns = QUAD * width
        hidden_units = gate_act.shape[1]
        per_half = half // columns
        middle = 128 * ((hidden_units // 128 + 1) // 2)
        bounds = [(0, middle), (middle, hidden_units)]

        fence = []

        def move(send, value, *args):
            return send(after(value, *fence), *args)

        gate_all, up_all = gate_act.astype(jnp.float32), up_act.astype(jnp.float32)
        hidden = (gate_all * jax.nn.sigmoid(gate_all) * up_all).astype(jnp.bfloat16)
        lower = far < n_far // 2

        above, below, travel = {}, {}, {}

        def gather_hop(j):
            up, down = (below[j - 1], above[j - 1]) if j > 1 else (hidden, hidden)
            if j == last_hop:
                one = after(jnp.where(lower, down, up), *fence)
                ends = [(n_far - 2, n_far - 1), (1, 0)]
                below[j] = above[j] = far_permute(one, ends)
                return [below[j]]
            up, down = after(up, *fence), after(down, *fence)
            below[j], above[j] = both_ways(up, down, range(j - 1, n_far - 1))
            return [below[j], above[j]]

        def reduce_hop(f, j):
            d = n_far - j
            up_term, down_term = terms[f][d], terms[f][n_far - d]
            if j == 1:
                one = after(jnp.where(lower, up_term, down_term).astype(jnp.bfloat16), *fence)
                one = far_permute(one, [(0, 1), (n_far - 1, n_far - 2)])
                none = jnp.zeros_like(one)
                travel[f] = jnp.where(lower, one, none), jnp.where(lower, none, one)
                return [one]
            up, down = travel[f]
            up_term = (up_term + up.astype(jnp.float32)).astype(jnp.bfloat16)
            down_term = (down_term + down.astype(jnp.float32)).astype(jnp.bfloat16)
            up_term, down_term = after(up_term, *fence), after(down_term, *fence)
            travel[f] = both_ways(up_term, down_term, range(0, j))
            return list(travel[f])

        def weight_columns(f, other):
            lo, hi = bounds[f]
            pair = jnp.concatenate([down_weight[lo:hi], other], axis=1)
            return jnp.concatenate([pair, move(swap, pair, 1)], axis=1)

        def reduce_terms(f):
            dots = lax.dot_general(
                cot_rows, weights[f], KEEP_COLS, preferred_element_type=jnp.float32
            )
            return [dots[e * tokens : (e + 1) * tokens] for e in range(n_far)]

        weights, terms = {}, {}

        parts = [cotangent] + [local_shift(cotangent, n_local - s) for s in range(1, n_local)]
        weight_side = swap(down_weight[:middle], 2)
        waits = gather_hop(1)
        cot_slots = jnp.concatenate(parts, axis=1).reshape(tokens, n_far, QUAD, width)
        cot_slots = picked(cot_slots, [near ^ k for k in ORDER], 2).reshape(tokens, n_far, columns)

        def cot_for(step):
            place = (far + step) % n_far
            start = (place // per_half - x) % n_local * per_half + place % per_half
            return lax.dynamic_index_in_dim(cot_slots, start, axis=1, keepdims=False)

        came = []
        for e in range(1, n_far):
            came.append(shift(after(cot_for(n_far - e), *came[: max(0, e - 2)]), n_far - e))
        cot_rows = jnp.concatenate([cot_for(0)] + came, axis=0)
        fence = waits + came + [weight_side]

        for j in range(2, n_far):
            waits = gather_hop(j)
            if j == 2:
                weights[0] = weight_columns(0, weight_side)
                weight_side = move(swap, down_weight[middle:], 2)
                terms[0] = reduce_terms(0)
                waits.append(weight_side)
            waits += reduce_hop(0, j - 1)
            if j == 3:
                weights[1] = weight_columns(1, weight_side)
                terms[1] = reduce_terms(1)
            if j > 2:
                waits += reduce_hop(1, j - 2)
            fence = waits

        gather_fence, fence = fence, []
        waits = reduce_hop(0, last_hop)
        fence = gather_fence
        waits += reduce_hop(1, last_hop - 1)
        slots = [after(hidden, *fence)]
        for e in range(1, n_far):
            above_e, below_e = after(above[e], *fence), after(below[n_far - e], *fence)
            slots.append(jnp.where(far + e < n_far, above_e, below_e))
        rows = jnp.concatenate(slots, axis=0)
        give, keep = (
            lax.dot_general(rows, part, SUM_ROWS, preferred_element_type=jnp.float32)
            for part in (cot_rows[:, 2 * width :], cot_rows[:, : 2 * width])
        )
        theirs = swap(give.astype(jnp.bfloat16), 1)
        give = (keep[:, width:] + theirs[:, width:].astype(jnp.float32)).astype(jnp.bfloat16)
        other_grad = swap(give, 2)
        for part in travel:
            travel[part] = tuple(after(value, give) for value in travel[part])
        grad = keep[:, :width] + theirs[:, :width].astype(jnp.float32)
        down_grad = grad + other_grad.astype(jnp.float32)

        fence = waits + [give]
        waits = reduce_hop(1, last_hop)
        rows = after(rows, *fence)
        out_sum = 0.0
        for f, (lo, hi) in enumerate(bounds):
            out_sum += jnp.dot(rows[:, lo:hi], weights[f], preferred_element_type=jnp.float32)
        out_terms = after(out_sum.astype(jnp.bfloat16), *waits)
        outs = [out_terms[:tokens]]
        for e in range(1, n_far):
            term = out_terms[e * tokens : (e + 1) * tokens]
            outs.append(shift(after(term, *outs[1 : max(1, e - 1)]), e))
        up_parts, gate_parts = [], []
        for f in range(2):
            up, down = travel[f]
            hidden_grad = terms[f][0] + up.astype(jnp.float32) + down.astype(jnp.float32)
            lo, hi = bounds[f]
            gate_wide = gate_act[:, lo:hi].astype(jnp.float32)
            up_wide = up_act[:, lo:hi].astype(jnp.float32)
            sigmoid_gate = jax.nn.sigmoid(gate_wide)
            up_parts.append((hidden_grad * gate_wide * sigmoid_gate).astype(jnp.bfloat16))
            gate_parts.append(
                (
                    hidden_grad * up_wide * sigmoid_gate * (1.0 + gate_wide * (1.0 - sigmoid_gate))
                ).astype(jnp.bfloat16)
            )

        out_slots = jnp.concatenate(outs, axis=1)

        def half_of(step):
            first = (x + step) % n_local * per_half
            starts = [(far - first - q) % n_far * columns for q in range(per_half)]
            return jnp.concatenate(
                [lax.dynamic_slice_in_dim(out_slots, s, columns, axis=1) for s in starts], axis=1
            )

        sides = [local_shift(half_of(step), step) for step in range(1, n_local)]
        output = half_of(0).astype(jnp.float32)
        for side in sides:
            output = output + side.astype(jnp.float32)
        output = output.astype(jnp.bfloat16).reshape(tokens, per_half, QUAD, width)
        return (
            picked(output, slot_of(near), 2).reshape(tokens, half),
            jnp.concatenate(gate_parts, axis=1),
            jnp.concatenate(up_parts, axis=1),
            down_grad,
        )

    specs = (P("hst", "local"), P("hst", "local"), P("hst", "local"), P("local", "hst"))
    return jax.shard_map(
        on_device, mesh=mesh, in_specs=specs, out_specs=specs, check_vma=False
    )
```

profile of v0, /device:TPU:8, one launch (start us, length us, event | category | flops | bytes accessed | tf_op | source)
XLA Modules:
  0.0 275.1 jit_solution(14899690448521542728)
XLA Ops:
  5.3 1.9 fusion.8
  7.2 2.3 collective-permute-start
  9.6 3.5 %collective-permute-start.1 = (bf16[128,5504]{1,0:T(8,128)(2,1)}, bf16[128,5504]{1,0:T(8,128)(2,1)}, u32[]{:S(2)}, u32[]{:S(2)}) collective-permute-start(bf16[128,5504]{1,0:T(8,128)(2,1)} %fusion.8), channel_id=1, source_target_pairs={{0,8},{2,10},{4,12},{6,14},{8,16},{10,18},{12,20},{14,22},{16,24},... | collective-permute-start | bytes 4227080 | tf_op jit(solution)/shard_map/ppermute | solution.py:40
  15.5 2.2 constant_dynamic-slice_fusion.15
  17.7 2.4 pad_maximum_fusion.14
  20.6 2.2 constant_dynamic-slice_fusion.8
  23.2 2.9 %collective-permute-start.4 = (bf16[128,1024]{1,0:T(8,128)(2,1)S(1)}, bf16[128,1024]{1,0:T(8,128)(2,1)S(1)}, u32[]{:S(2)}, u32[]{:S(2)}) collective-permute-start(bf16[128,1024]{1,0:T(8,128)(2,1)S(1)} %bitcast.17), channel_id=1, source_target_pairs={{0,16},{2,18},{4,20},{6,22},{8,24},{10,26},{12,28},{14,30},{16,0},... | collective-permute-start | bytes 786440 | tf_op jit(solution)/shard_map/ppermute | solution.py:36
  26.2 33.8 %collective-permute-done.3 = bf16[128,1024]{1,0:T(8,128)(2,1)S(1)} collective-permute-done((bf16[128,1024]{1,0:T(8,128)(2,1)S(1)}, bf16[128,1024]{1,0:T(8,128)(2,1)S(1)}, u32[]{:S(2)}, u32[]{:S(2)}) %collective-permute-start.3) | collective-permute-done | bytes 262176 | tf_op jit(solution)/shard_map/ppermute | solution.py:36
  60.0 3.1 %pad_maximum_fusion.3 = bf16[2816,512]{1,0:T(8,128)(2,1)} fusion(bf16[2816,256]{1,0:T(8,128)(2,1)} %collective-permute-done.6, bf16[2816,256]{1,0:T(8,128)(2,1)S(1)} %slice.80), kind=kLoop, calls=%fused_computation.10 | loop fusion | flops 5767168 | bytes 5767168 | tf_op jit(solution)/shard_map/concatenate | solution.py:103
  63.1 3.2 %collective-permute-done.5 = bf16[128,1024]{1,0:T(8,128)(2,1)S(1)} collective-permute-done((bf16[128,1024]{1,0:T(8,128)(2,1)S(1)}, bf16[128,1024]{1,0:T(8,128)(2,1)S(1)}, u32[]{:S(2)}, u32[]{:S(2)}) %collective-permute-start.5) | collective-permute-done | bytes 262176 | tf_op jit(solution)/shard_map/ppermute | solution.py:36
  68.7 1.9 collective-permute-start.7
  70.6 4.3 %collective-permute-start.8 = (bf16[128,5504]{1,0:T(8,128)(2,1)}, bf16[128,5504]{1,0:T(8,128)(2,1)S(1)}, u32[]{:S(2)}, u32[]{:S(2)}) collective-permute-start(bf16[128,5504]{1,0:T(8,128)(2,1)} %collective-permute-done.1), channel_id=1, source_target_pairs={{8,16},{10,18},{12,20},{14,22},{16,24},{18,26},{20,28},{22,30},{9,... | collective-permute-start | bytes 4227080 | tf_op jit(solution)/shard_map/ppermute | solution.py:40
  75.5 5.3 %fusion.11 = f32[512,2816]{1,0:T(8,128)S(1)} fusion(bf16[2816,512]{1,0:T(8,128)(2,1)} %collective-permute-done.10, bf16[2816,256]{1,0:T(8,128)(2,1)} %collective-permute-done.6, bf16[2816,256]{1,0:T(8,128)(2,1)S(1)} %slice.80, bf16[128,1024]{1,0:T(8,128)(2,1)S(1)} %copy-done.22, bf16[128,1024]{1,0:T(8,128)(2,1)} %copy-done.19, ...), kind=kOutput, calls=%fused_computation.21 | convolution fusion | flops 2974285824 | bytes 12582912 | tf_op jit(solution)/shard_map/dot_general | solution.py:107
  82.2 24.7 %collective-permute-done.9 = bf16[2688,256]{1,0:T(8,128)(2,1)S(1)} collective-permute-done((bf16[2688,256]{1,0:T(8,128)(2,1)S(1)}, bf16[2688,256]{1,0:T(8,128)(2,1)S(1)}, u32[]{:S(2)}, u32[]{:S(2)}) %collective-permute-start.9) | collective-permute-done | bytes 1376288 | tf_op jit(solution)/shard_map/ppermute | solution.py:32
  108.9 2.5 collective-permute-start.12
  112.8 3.3 %collective-permute-start.13 = (bf16[128,2816]{1,0:T(8,128)(2,1)}, bf16[128,2816]{1,0:T(8,128)(2,1)}, u32[]{:S(2)}, u32[]{:S(2)}) collective-permute-start(bf16[128,2816]{1,0:T(8,128)(2,1)} %get-tuple-element.39), channel_id=1, source_target_pairs={{0,8},{2,10},{4,12},{6,14},{8,16},{10,18},{12,20},{14,22},{1,9},{3... | collective-permute-start | bytes 2162696 | tf_op jit(solution)/shard_map/ppermute | solution.py:40
  117.4 3.2 %fusion.12 = f32[512,2688]{1,0:T(8,128)S(1)} fusion(bf16[2688,512]{1,0:T(8,128)(2,1)S(1)} %collective-permute-done.15, bf16[2688,256]{1,0:T(8,128)(2,1)S(1)} %collective-permute-done.9, bf16[2688,256]{1,0:T(8,128)(2,1)S(1)} %slice.81, bf16[128,1024]{1,0:T(8,128)(2,1)S(1)} %copy-done.22, bf16[128,1024]{1,0:T(8,128)(2,1)S(1)} %copy-done.20, ...), kind=kOutput, calls=%fused_computation.22 | convolution fusion | flops 2839281664 | bytes 12058624 | tf_op jit(solution)/shard_map/dot_general | solution.py:107
  120.6 2.4 copy-done.2
  126.5 7.5 %collective-permute-done.13 = bf16[128,2816]{1,0:T(8,128)(2,1)} collective-permute-done((bf16[128,2816]{1,0:T(8,128)(2,1)}, bf16[128,2816]{1,0:T(8,128)(2,1)}, u32[]{:S(2)}, u32[]{:S(2)}) %collective-permute-start.13) | collective-permute-done | bytes 720928 | tf_op jit(solution)/shard_map/ppermute | solution.py:40
  134.0 2.0 collective-permute-done.14
  136.0 5.4 %collective-permute-done.12 = bf16[128,5504]{1,0:T(8,128)(2,1)} collective-permute-done((bf16[128,5504]{1,0:T(8,128)(2,1)}, bf16[128,5504]{1,0:T(8,128)(2,1)}, u32[]{:S(2)}, u32[]{:S(2)}) %collective-permute-start.12) | collective-permute-done | bytes 1409056 | tf_op jit(solution)/shard_map/ppermute | solution.py:40
  141.3 6.6 %collective-permute-done.16 = bf16[128,2688]{1,0:T(8,128)(2,1)} collective-permute-done((bf16[128,2688]{1,0:T(8,128)(2,1)}, bf16[128,2688]{1,0:T(8,128)(2,1)}, u32[]{:S(2)}, u32[]{:S(2)}) %collective-permute-start.16) | collective-permute-done | bytes 688160 | tf_op jit(solution)/shard_map/ppermute | solution.py:40
  148.2 3.0 %broadcast_select_fusion.2 = (bf16[128,5504]{1,0:T(8,128)(2,1)S(1)}, bf16[128,5504]{1,0:T(8,128)(2,1)S(1)}) fusion(bf16[128,5504]{1,0:T(8,128)(2,1)} %collective-permute-done, bf16[128,5504]{1,0:T(8,128)(2,1)} %collective-permute-done.12, pred[]{:T(512)S(6)} %lt.161, bf16[128,5504]{1,0:T(8,128)(2,1)} %collective-permute-done.1, pred[]{:T(512)S(6)} %lt.163), kind=kLoop, calls=%fused_computation.49 | loop fusion | flops 1409024 | bytes 7045122 | tf_op jit(solution)/shard_map/jit(_where)/select_n | solution.py:153
  151.2 6.7 %convolution_convert_fusion = bf16[5504,512]{1,0:T(8,128)(2,1)} fusion(bf16[512,1024]{1,0:T(8,128)(2,1)S(1)} %pad_maximum_fusion.15, bf16[128,5504]{1,0:T(8,128)(2,1)S(1)} %get-tuple-element.73, bf16[128,5504]{1,0:T(8,128)(2,1)S(1)} %broadcast_select_fusion.1, bf16[128,5504]{1,0:T(8,128)(2,1)S(1)} %get-tuple-element.72, bf16[128,5504]{1,0:T(8,128)(2,1)} %fusion.8), kind=kOutput, calls=%fused_computation | convolution fusion | flops 2911043584 | bytes 11796480 | tf_op jit(solution)/shard_map/dot_general | solution.py:156
  157.9 3.6 %add_convert_fusion.1 = (bf16[128,2816]{1,0:T(8,128)(2,1)}, bf16[128,2816]{1,0:T(8,128)(2,1)}) fusion(bf16[128,2816]{1,0:T(8,128)(2,1)} %collective-permute-done.14, f32[512,2816]{1,0:T(8,128)} %copy-done.1, bf16[128,2816]{1,0:T(8,128)(2,1)} %collective-permute-done.13), kind=kLoop, calls=%fused_computation.40 | loop fusion | flops 2162688 | bytes 5767168 | tf_op jit(solution)/shard_map/convert_element_type | solution.py:96
  161.5 4.6 %collective-permute-start.17 = (bf16[128,2816]{1,0:T(8,128)(2,1)}, bf16[128,2816]{1,0:T(8,128)(2,1)}, u32[]{:S(2)}, u32[]{:S(2)}) collective-permute-start(bf16[128,2816]{1,0:T(8,128)(2,1)} %get-tuple-element.69), channel_id=1, source_target_pairs={{0,8},{2,10},{4,12},{6,14},{8,16},{10,18},{12,20},{14,22},{16,24},... | collective-permute-start | bytes 2162696 | tf_op jit(solution)/shard_map/ppermute | solution.py:40
  166.1 2.4 collective-permute-start.18
  168.4 2.6 add_convert_fusion.7
  171.1 3.5 %collective-permute-start.19 = (bf16[128,2688]{1,0:T(8,128)(2,1)}, bf16[128,2688]{1,0:T(8,128)(2,1)}, u32[]{:S(2)}, u32[]{:S(2)}) collective-permute-start(bf16[128,2688]{1,0:T(8,128)(2,1)} %get-tuple-element.49), channel_id=1, source_target_pairs={{0,8},{2,10},{4,12},{6,14},{8,16},{10,18},{12,20},{14,22},{1,9},{3... | collective-permute-start | bytes 2064392 | tf_op jit(solution)/shard_map/ppermute | solution.py:40
  175.9 3.1 %pad_maximum_fusion.1 = bf16[512,5504]{1,0:T(8,128)(2,1)S(1)} fusion(bf16[128,5504]{1,0:T(8,128)(2,1)S(1)} %copy-done.12, bf16[128,5504]{1,0:T(8,128)(2,1)S(1)} %copy-done.10, bf16[128,5504]{1,0:T(8,128)(2,1)S(1)} %get-tuple-element.72, bf16[128,5504]{1,0:T(8,128)(2,1)} %fusion.8), kind=kLoop, calls=%fused_computation.6 | loop fusion | flops 22544384 | bytes 11272192 | tf_op jit(solution)/shard_map/concatenate | solution.py:154
  179.0 5.1 %fusion.34 = f32[5504,512]{1,0:T(8,128)S(1)} fusion(bf16[512,1024]{1,0:T(8,128)(2,1)} %copy-done.17, bf16[128,5504]{1,0:T(8,128)(2,1)} %copy-done.11, bf16[128,5504]{1,0:T(8,128)(2,1)S(1)} %copy-done.10, bf16[128,5504]{1,0:T(8,128)(2,1)S(1)} %get-tuple-element.72, bf16[128,5504]{1,0:T(8,128)(2,1)} %fusion.8), kind=kOutput, calls=%fused_computation.72 | convolution fusion | flops 2908225536 | bytes 17432576 | tf_op jit(solution)/shard_map/dot_general | solution.py:156
  184.1 6.5 %fusion.1 = bf16[5504,256]{1,0:T(8,128)(2,1)} fusion(f32[5504,512]{1,0:T(8,128)S(1)} %fusion.34, bf16[5504,512]{1,0:T(8,128)(2,1)} %collective-permute-done.21), kind=kLoop, calls=%fused_computation.5 | loop fusion | flops 4227072 | bytes 11272192 | tf_op jit(solution)/shard_map/convert_element_type | solution.py:160
  191.1 6.1 %collective-permute-done.19 = bf16[128,2688]{1,0:T(8,128)(2,1)} collective-permute-done((bf16[128,2688]{1,0:T(8,128)(2,1)}, bf16[128,2688]{1,0:T(8,128)(2,1)}, u32[]{:S(2)}, u32[]{:S(2)}) %collective-permute-start.19) | collective-permute-done | bytes 688160 | tf_op jit(solution)/shard_map/ppermute | solution.py:40
  197.2 4.1 %collective-permute-done.20 = bf16[128,2688]{1,0:T(8,128)(2,1)} collective-permute-done((bf16[128,2688]{1,0:T(8,128)(2,1)S(1)}, bf16[128,2688]{1,0:T(8,128)(2,1)}, u32[]{:S(2)}, u32[]{:S(2)}) %collective-permute-start.20) | collective-permute-done | bytes 688160 | tf_op jit(solution)/shard_map/ppermute | solution.py:40
  202.8 2.4 collective-permute-start.22
  205.3 3.7 %collective-permute-start.23 = (bf16[128,2688]{1,0:T(8,128)(2,1)S(1)}, bf16[128,2688]{1,0:T(8,128)(2,1)S(1)}, u32[]{:S(2)}, u32[]{:S(2)}) collective-permute-start(bf16[128,2688]{1,0:T(8,128)(2,1)S(1)} %get-tuple-element.55), channel_id=1, source_target_pairs={{24,16},{26,18},{28,20},{30,22},{16,8},{18,10},{20,12},{22,14},{8,... | collective-permute-start | bytes 2064392 | tf_op jit(solution)/shard_map/ppermute | solution.py:40
  209.0 3.2 %fusion.9 = f32[512,1024]{1,0:T(8,128)S(1)} fusion(bf16[512,5504]{1,0:T(8,128)(2,1)S(1)} %pad_maximum_fusion.1, bf16[2688,512]{1,0:T(8,128)(2,1)S(1)} %copy-done.24, bf16[2688,256]{1,0:T(8,128)(2,1)S(1)} %copy-done.16, bf16[2688,256]{1,0:T(8,128)(2,1)S(1)} %copy-done.14), kind=kOutput, calls=%fused_computation.19 | convolution fusion | flops 2835087360 | bytes 10354688 | tf_op jit(solution)/shard_map/dot_general | solution.py:172
  212.2 5.5 %add_convert_fusion = bf16[512,1024]{1,0:T(8,128)(2,1)S(1)} fusion(f32[512,1024]{1,0:T(8,128)S(1)} %fusion.9, bf16[2816,512]{1,0:T(8,128)(2,1)} %collective-permute-done.10, bf16[2816,256]{1,0:T(8,128)(2,1)} %collective-permute-done.6, bf16[2816,256]{1,0:T(8,128)(2,1)S(1)} %slice.80, bf16[512,5504]{1,0:T(8,128)(2,1)S(1)} %pad_maximum_fusion.1), kind=kOutput, calls=%fused_computation.26 | convolution fusion | flops 2971140096 | bytes 11796480 | tf_op jit(solution)/shard_map/dot_general | solution.py:172
  217.7 4.0 %collective-permute-done.22 = bf16[128,2688]{1,0:T(8,128)(2,1)S(1)} collective-permute-done((bf16[128,2688]{1,0:T(8,128)(2,1)S(1)}, bf16[128,2688]{1,0:T(8,128)(2,1)S(1)}, u32[]{:S(2)}, u32[]{:S(2)}) %collective-permute-start.22) | collective-permute-done | bytes 688160 | tf_op jit(solution)/shard_map/ppermute | solution.py:40
  221.7 2.2 collective-permute-done.23
  224.4 2.7 fusion.22
  227.1 3.6 %collective-permute-start.25 = (bf16[128,1024]{1,0:T(8,128)(2,1)S(1)}, bf16[128,1024]{1,0:T(8,128)(2,1)S(1)}, u32[]{:S(2)}, u32[]{:S(2)}) collective-permute-start(bf16[128,1024]{1,0:T(8,128)(2,1)S(1)} %get-tuple-element.80), channel_id=1, source_target_pairs={{0,16},{2,18},{4,20},{6,22},{8,24},{10,26},{12,28},{14,30},{16,0},... | collective-permute-start | bytes 786440 | tf_op jit(solution)/shard_map/ppermute | solution.py:36
  230.7 2.6 collective-permute-done.24
  233.3 3.4 %collective-permute-start.26 = (bf16[128,1024]{1,0:T(8,128)(2,1)S(1)}, bf16[128,1024]{1,0:T(8,128)(2,1)S(1)}, u32[]{:S(2)}, u32[]{:S(2)}) collective-permute-start(bf16[128,1024]{1,0:T(8,128)(2,1)S(1)} %get-tuple-element.57), channel_id=1, source_target_pairs={{0,24},{2,26},{4,28},{6,30},{8,0},{10,2},{12,4},{14,6},{16,8},{18,... | collective-permute-start | bytes 786440 | tf_op jit(solution)/shard_map/ppermute | solution.py:36
  237.6 8.3 %collective-permute-done.25 = bf16[128,1024]{1,0:T(8,128)(2,1)S(1)} collective-permute-done((bf16[128,1024]{1,0:T(8,128)(2,1)S(1)}, bf16[128,1024]{1,0:T(8,128)(2,1)S(1)}, u32[]{:S(2)}, u32[]{:S(2)}) %collective-permute-start.25) | collective-permute-done | bytes 262176 | tf_op jit(solution)/shard_map/ppermute | solution.py:36
  245.9 3.4 %collective-permute-done.26 = bf16[128,1024]{1,0:T(8,128)(2,1)S(1)} collective-permute-done((bf16[128,1024]{1,0:T(8,128)(2,1)S(1)}, bf16[128,1024]{1,0:T(8,128)(2,1)S(1)}, u32[]{:S(2)}, u32[]{:S(2)}) %collective-permute-start.26) | collective-permute-done | bytes 262176 | tf_op jit(solution)/shard_map/ppermute | solution.py:36
  252.1 11.5 %collective-permute-done.27 = bf16[128,2048]{1,0:T(8,128)(2,1)S(1)} collective-permute-done((bf16[128,2048]{1,0:T(8,128)(2,1)S(1)}, bf16[128,2048]{1,0:T(8,128)(2,1)S(1)}, u32[]{:S(2)}, u32[]{:S(2)}) %collective-permute-start.27) | collective-permute-done | bytes 524320 | tf_op jit(solution)/shard_map/ppermute | solution.py:49
  267.6 7.5 %fusion = f32[5504,256]{1,0:T(8,128)} fusion(f32[5504,512]{1,0:T(8,128)} %copy-done, bf16[5504,256]{1,0:T(8,128)(2,1)} %collective-permute-done.28, bf16[5504,512]{1,0:T(8,128)(2,1)} %collective-permute-done.21), kind=kLoop, calls=%fused_computation.3 | loop fusion | flops 5636096 | bytes 16908288 | tf_op jit(solution)/shard_map/add | solution.py:165
  (111 shorter events, 31.8 us)
Async XLA Ops:
  0.7 13.9 %collective-permute-start.2 = (bf16[128,2048]{1,0:T(8,128)(2,1)}, bf16[128,2048]{1,0:T(8,128)(2,1)S(1)}, u32[]{:S(2)}, u32[]{:S(2)}) collective-permute-start(bf16[128,2048]{1,0:T(8,128)(2,1)} %param.6), channel_id=1, source_target_pairs={{0,1},{1,0},{2,3},{3,2},{4,5},{5,4},{6,7},{7,6},{8,9},{9,8},{10,11... | collective-permute-start | bytes 1572872 | tf_op jit(solution)/shard_map/ppermute | solution.py:49
  3.7 10.9 %copy-start.18 = (bf16[128,2048]{1,0:T(8,128)(2,1)S(1)}, bf16[128,2048]{1,0:T(8,128)(2,1)}, u32[]{:S(2)}) copy-start(bf16[128,2048]{1,0:T(8,128)(2,1)} %param.6) | copy-start | bytes 1572868
  3.7 56.3 %collective-permute-start.6 = (bf16[2816,256]{1,0:T(8,128)(2,1)S(1)}, bf16[2816,256]{1,0:T(8,128)(2,1)}, u32[]{:S(2)}, u32[]{:S(2)}) collective-permute-start(bf16[2816,256]{1,0:T(8,128)(2,1)S(1)} %slice.80), channel_id=1, source_target_pairs={{0,4},{2,6},{4,0},{6,2},{8,12},{10,14},{12,8},{14,10},{16,20},{18,... | collective-permute-start | bytes 4325384 | tf_op jit(solution)/shard_map/ppermute | solution.py:32
  7.2 59.9 %collective-permute-start = (bf16[128,5504]{1,0:T(8,128)(2,1)}, bf16[128,5504]{1,0:T(8,128)(2,1)}, u32[]{:S(2)}, u32[]{:S(2)}) collective-permute-start(bf16[128,5504]{1,0:T(8,128)(2,1)} %fusion.8), channel_id=1, source_target_pairs={{24,16},{26,18},{28,20},{30,22},{16,8},{18,10},{20,12},{22,14},{8,... | collective-permute-start | bytes 4227080 | tf_op jit(solution)/shard_map/ppermute | solution.py:40
  9.6 57.5 %collective-permute-start.1 = (bf16[128,5504]{1,0:T(8,128)(2,1)}, bf16[128,5504]{1,0:T(8,128)(2,1)}, u32[]{:S(2)}, u32[]{:S(2)}) collective-permute-start(bf16[128,5504]{1,0:T(8,128)(2,1)} %fusion.8), channel_id=1, source_target_pairs={{0,8},{2,10},{4,12},{6,14},{8,16},{10,18},{12,20},{14,22},{16,24},... | collective-permute-start | bytes 4227080 | tf_op jit(solution)/shard_map/ppermute | solution.py:40
  22.8 37.1 %collective-permute-start.3 = (bf16[128,1024]{1,0:T(8,128)(2,1)S(1)}, bf16[128,1024]{1,0:T(8,128)(2,1)S(1)}, u32[]{:S(2)}, u32[]{:S(2)}) collective-permute-start(bf16[128,1024]{1,0:T(8,128)(2,1)S(1)} %bitcast.19), channel_id=1, source_target_pairs={{0,24},{2,26},{4,28},{6,30},{8,0},{10,2},{12,4},{14,6},{16,8},{18,... | collective-permute-start | bytes 786440 | tf_op jit(solution)/shard_map/ppermute | solution.py:36
  23.2 40.0 %collective-permute-start.4 = (bf16[128,1024]{1,0:T(8,128)(2,1)S(1)}, bf16[128,1024]{1,0:T(8,128)(2,1)S(1)}, u32[]{:S(2)}, u32[]{:S(2)}) collective-permute-start(bf16[128,1024]{1,0:T(8,128)(2,1)S(1)} %bitcast.17), channel_id=1, source_target_pairs={{0,16},{2,18},{4,20},{6,22},{8,24},{10,26},{12,28},{14,30},{16,0},... | collective-permute-start | bytes 786440 | tf_op jit(solution)/shard_map/ppermute | solution.py:36
  60.0 6.4 %collective-permute-start.5 = (bf16[128,1024]{1,0:T(8,128)(2,1)S(1)}, bf16[128,1024]{1,0:T(8,128)(2,1)S(1)}, u32[]{:S(2)}, u32[]{:S(2)}) collective-permute-start(bf16[128,1024]{1,0:T(8,128)(2,1)S(1)} %bitcast.18), channel_id=1, source_target_pairs={{0,8},{2,10},{4,12},{6,14},{8,16},{10,18},{12,20},{14,22},{16,24},... | collective-permute-start | bytes 786440 | tf_op jit(solution)/shard_map/ppermute | solution.py:36
  67.1 8.4 %collective-permute-start.10 = (bf16[2816,512]{1,0:T(8,128)(2,1)}, bf16[2816,512]{1,0:T(8,128)(2,1)}, u32[]{:S(2)}, u32[]{:S(2)}) collective-permute-start(bf16[2816,512]{1,0:T(8,128)(2,1)} %pad_maximum_fusion.3), channel_id=1, source_target_pairs={{0,2},{2,0},{4,6},{6,4},{8,10},{10,8},{12,14},{14,12},{16,18},{18,... | collective-permute-start | bytes 8650760 | tf_op jit(solution)/shard_map/ppermute | solution.py:32
  67.1 8.4 %copy-start.22 = (bf16[128,1024]{1,0:T(8,128)(2,1)S(1)}, bf16[128,1024]{1,0:T(8,128)(2,1)}, u32[]{:S(2)}) copy-start(bf16[128,1024]{1,0:T(8,128)(2,1)} %copy-done.21) | copy-start | bytes 786436
  68.6 48.8 %copy-start.13 = (bf16[2688,256]{1,0:T(8,128)(2,1)}, bf16[2688,256]{1,0:T(8,128)(2,1)S(1)}, u32[]{:S(2)}) copy-start(bf16[2688,256]{1,0:T(8,128)(2,1)S(1)} %slice.81) | copy-start | bytes 4128772
  68.7 38.5 %collective-permute-start.7 = (bf16[128,5504]{1,0:T(8,128)(2,1)}, bf16[128,5504]{1,0:T(8,128)(2,1)S(1)}, u32[]{:S(2)}, u32[]{:S(2)}) collective-permute-start(bf16[128,5504]{1,0:T(8,128)(2,1)} %collective-permute-done), channel_id=1, source_target_pairs={{16,8},{18,10},{20,12},{22,14},{8,0},{10,2},{12,4},{14,6},{17,9},{... | collective-permute-start | bytes 4227080 | tf_op jit(solution)/shard_map/ppermute | solution.py:40
  70.6 36.6 %collective-permute-start.8 = (bf16[128,5504]{1,0:T(8,128)(2,1)}, bf16[128,5504]{1,0:T(8,128)(2,1)S(1)}, u32[]{:S(2)}, u32[]{:S(2)}) collective-permute-start(bf16[128,5504]{1,0:T(8,128)(2,1)} %collective-permute-done.1), channel_id=1, source_target_pairs={{8,16},{10,18},{12,20},{14,22},{16,24},{18,26},{20,28},{22,30},{9,... | collective-permute-start | bytes 4227080 | tf_op jit(solution)/shard_map/ppermute | solution.py:40
  74.9 32.1 %collective-permute-start.9 = (bf16[2688,256]{1,0:T(8,128)(2,1)S(1)}, bf16[2688,256]{1,0:T(8,128)(2,1)S(1)}, u32[]{:S(2)}, u32[]{:S(2)}) collective-permute-start(bf16[2688,256]{1,0:T(8,128)(2,1)S(1)} %slice.81), channel_id=1, source_target_pairs={{0,4},{2,6},{4,0},{6,2},{8,12},{10,14},{12,8},{14,10},{16,20},{18,... | collective-permute-start | bytes 4128776 | tf_op jit(solution)/shard_map/ppermute | solution.py:32
  80.8 30.6 %copy-start.1 = (f32[512,2816]{1,0:T(8,128)}, f32[512,2816]{1,0:T(8,128)S(1)}, u32[]{:S(2)}) copy-start(f32[512,2816]{1,0:T(8,128)S(1)} %fusion.11) | copy-start | bytes 17301508
  80.9 26.3 %collective-permute-start.11 = (bf16[128,2816]{1,0:T(8,128)(2,1)S(1)}, bf16[128,2816]{1,0:T(8,128)(2,1)S(1)}, u32[]{:S(2)}, u32[]{:S(2)}) collective-permute-start(bf16[128,2816]{1,0:T(8,128)(2,1)S(1)} %select_convert_fusion), channel_id=1, source_target_pairs={{0,8},{2,10},{4,12},{6,14},{24,16},{26,18},{28,20},{30,22},{1,9},{... | collective-permute-start | bytes 2162696 | tf_op jit(solution)/shard_map/ppermute | solution.py:40
  107.0 10.4 %copy-start.15 = (bf16[2688,256]{1,0:T(8,128)(2,1)}, bf16[2688,256]{1,0:T(8,128)(2,1)S(1)}, u32[]{:S(2)}) copy-start(bf16[2688,256]{1,0:T(8,128)(2,1)S(1)} %collective-permute-done.9) | copy-start | bytes 4128772
  107.2 10.2 %collective-permute-start.15 = (bf16[2688,512]{1,0:T(8,128)(2,1)S(1)}, bf16[2688,512]{1,0:T(8,128)(2,1)S(1)}, u32[]{:S(2)}, u32[]{:S(2)}) collective-permute-start(bf16[2688,512]{1,0:T(8,128)(2,1)S(1)} %pad_maximum_fusion.4), channel_id=1, source_target_pairs={{0,2},{2,0},{4,6},{6,4},{8,10},{10,8},{12,14},{14,12},{16,18},{18,... | collective-permute-start | bytes 8257544 | tf_op jit(solution)/shard_map/ppermute | solution.py:32
  108.9 8.5 %copy-start.20 = (bf16[128,1024]{1,0:T(8,128)(2,1)S(1)}, bf16[128,1024]{1,0:T(8,128)(2,1)}, u32[]{:S(2)}) copy-start(bf16[128,1024]{1,0:T(8,128)(2,1)} %copy-done.19) | copy-start | bytes 786436
  108.9 32.5 %collective-permute-start.12 = (bf16[128,5504]{1,0:T(8,128)(2,1)}, bf16[128,5504]{1,0:T(8,128)(2,1)}, u32[]{:S(2)}, u32[]{:S(2)}) collective-permute-start(bf16[128,5504]{1,0:T(8,128)(2,1)} %broadcast_select_fusion.3), channel_id=1, source_target_pairs={{16,24},{18,26},{20,28},{22,30},{8,0},{10,2},{12,4},{14,6},{17,25}... | collective-permute-start | bytes 4227080 | tf_op jit(solution)/shard_map/ppermute | solution.py:40
  112.8 21.2 %collective-permute-start.13 = (bf16[128,2816]{1,0:T(8,128)(2,1)}, bf16[128,2816]{1,0:T(8,128)(2,1)}, u32[]{:S(2)}, u32[]{:S(2)}) collective-permute-start(bf16[128,2816]{1,0:T(8,128)(2,1)} %get-tuple-element.39), channel_id=1, source_target_pairs={{0,8},{2,10},{4,12},{6,14},{8,16},{10,18},{12,20},{14,22},{1,9},{3... | collective-permute-start | bytes 2162696 | tf_op jit(solution)/shard_map/ppermute | solution.py:40
  116.1 19.9 %collective-permute-start.14 = (bf16[128,2816]{1,0:T(8,128)(2,1)}, bf16[128,2816]{1,0:T(8,128)(2,1)}, u32[]{:S(2)}, u32[]{:S(2)}) collective-permute-start(bf16[128,2816]{1,0:T(8,128)(2,1)} %get-tuple-element.40), channel_id=1, source_target_pairs={{24,16},{26,18},{28,20},{30,22},{16,8},{18,10},{20,12},{22,14},{25... | collective-permute-start | bytes 2162696 | tf_op jit(solution)/shard_map/ppermute | solution.py:40
  124.0 24.0 %collective-permute-start.16 = (bf16[128,2688]{1,0:T(8,128)(2,1)}, bf16[128,2688]{1,0:T(8,128)(2,1)}, u32[]{:S(2)}, u32[]{:S(2)}) collective-permute-start(bf16[128,2688]{1,0:T(8,128)(2,1)} %select_convert_fusion.1), channel_id=1, source_target_pairs={{0,8},{2,10},{4,12},{6,14},{24,16},{26,18},{28,20},{30,22},{1,9},{... | collective-permute-start | bytes 2064392 | tf_op jit(solution)/shard_map/ppermute | solution.py:40
  125.3 22.7 %copy-start.4 = (bf16[128,5504]{1,0:T(8,128)(2,1)S(1)}, bf16[128,5504]{1,0:T(8,128)(2,1)}, u32[]{:S(2)}) copy-start(bf16[128,5504]{1,0:T(8,128)(2,1)} %copy-done.3) | copy-start | bytes 4227076
  126.5 24.7 %copy-start.17 = (bf16[512,1024]{1,0:T(8,128)(2,1)}, bf16[512,1024]{1,0:T(8,128)(2,1)S(1)}, u32[]{:S(2)}) copy-start(bf16[512,1024]{1,0:T(8,128)(2,1)S(1)} %pad_maximum_fusion.15) | copy-start | bytes 3145732
  151.2 6.7 %copy-start.11 = (bf16[128,5504]{1,0:T(8,128)(2,1)}, bf16[128,5504]{1,0:T(8,128)(2,1)S(1)}, u32[]{:S(2)}) copy-start(bf16[128,5504]{1,0:T(8,128)(2,1)S(1)} %get-tuple-element.73) | copy-start | bytes 4227076
  157.9 26.2 %collective-permute-start.21 = (bf16[5504,512]{1,0:T(8,128)(2,1)}, bf16[5504,512]{1,0:T(8,128)(2,1)}, u32[]{:S(2)}, u32[]{:S(2)}) collective-permute-start(bf16[5504,512]{1,0:T(8,128)(2,1)} %convolution_convert_fusion), channel_id=1, source_target_pairs={{0,2},{2,0},{4,6},{6,4},{8,10},{10,8},{12,14},{14,12},{16,18},{18,... | collective-permute-start | bytes 16908296 | tf_op jit(solution)/shard_map/ppermute | solution.py:32
  161.5 14.4 %copy-start.10 = (bf16[128,5504]{1,0:T(8,128)(2,1)S(1)}, bf16[128,5504]{1,0:T(8,128)(2,1)}, u32[]{:S(2)}) copy-start(bf16[128,5504]{1,0:T(8,128)(2,1)} %copy-done.9) | copy-start | bytes 4227076
  161.5 14.4 %copy-start.12 = (bf16[128,5504]{1,0:T(8,128)(2,1)S(1)}, bf16[128,5504]{1,0:T(8,128)(2,1)}, u32[]{:S(2)}) copy-start(bf16[128,5504]{1,0:T(8,128)(2,1)} %copy-done.11) | copy-start | bytes 4227076
  161.5 29.7 %collective-permute-start.17 = (bf16[128,2816]{1,0:T(8,128)(2,1)}, bf16[128,2816]{1,0:T(8,128)(2,1)}, u32[]{:S(2)}, u32[]{:S(2)}) collective-permute-start(bf16[128,2816]{1,0:T(8,128)(2,1)} %get-tuple-element.69), channel_id=1, source_target_pairs={{0,8},{2,10},{4,12},{6,14},{8,16},{10,18},{12,20},{14,22},{16,24},... | collective-permute-start | bytes 2162696 | tf_op jit(solution)/shard_map/ppermute | solution.py:40
  166.1 25.1 %collective-permute-start.18 = (bf16[128,2816]{1,0:T(8,128)(2,1)}, bf16[128,2816]{1,0:T(8,128)(2,1)}, u32[]{:S(2)}, u32[]{:S(2)}) collective-permute-start(bf16[128,2816]{1,0:T(8,128)(2,1)} %get-tuple-element.68), channel_id=1, source_target_pairs={{24,16},{26,18},{28,20},{30,22},{16,8},{18,10},{20,12},{22,14},{8,... | collective-permute-start | bytes 2162696 | tf_op jit(solution)/shard_map/ppermute | solution.py:40
  171.1 26.2 %collective-permute-start.19 = (bf16[128,2688]{1,0:T(8,128)(2,1)}, bf16[128,2688]{1,0:T(8,128)(2,1)}, u32[]{:S(2)}, u32[]{:S(2)}) collective-permute-start(bf16[128,2688]{1,0:T(8,128)(2,1)} %get-tuple-element.49), channel_id=1, source_target_pairs={{0,8},{2,10},{4,12},{6,14},{8,16},{10,18},{12,20},{14,22},{1,9},{3... | collective-permute-start | bytes 2064392 | tf_op jit(solution)/shard_map/ppermute | solution.py:40
  174.5 26.7 %collective-permute-start.20 = (bf16[128,2688]{1,0:T(8,128)(2,1)S(1)}, bf16[128,2688]{1,0:T(8,128)(2,1)}, u32[]{:S(2)}, u32[]{:S(2)}) collective-permute-start(bf16[128,2688]{1,0:T(8,128)(2,1)S(1)} %get-tuple-element.50), channel_id=1, source_target_pairs={{24,16},{26,18},{28,20},{30,22},{16,8},{18,10},{20,12},{22,14},{25... | collective-permute-start | bytes 2064392 | tf_op jit(solution)/shard_map/ppermute | solution.py:40
  175.9 25.4 %slice-start = ((s8[5505024]{0:T(1024)(128)(4,1)}), s8[4194304]{0:T(1024)(128)(4,1)S(1)}, s32[]{:S(2)}) async-start(s8[5505024]{0:T(1024)(128)(4,1)} %bitcast.12), calls=%async_computation | async-start | bytes 8388608
  179.0 22.3 %slice-start.1 = ((s8[5505024]{0:T(1024)(128)(4,1)}), s8[1310720]{0:T(1024)(128)(4,1)S(1)}, s32[]{:S(2)}) async-start(s8[5505024]{0:T(1024)(128)(4,1)} %bitcast.12), calls=%async_computation.1 | async-start | bytes 2621440
  184.1 6.5 %copy-start = (f32[5504,512]{1,0:T(8,128)}, f32[5504,512]{1,0:T(8,128)S(1)}, u32[]{:S(2)}) copy-start(f32[5504,512]{1,0:T(8,128)S(1)} %fusion.34) | copy-start | bytes 33816580
  190.5 18.4 %copy-start.14 = (bf16[2688,256]{1,0:T(8,128)(2,1)S(1)}, bf16[2688,256]{1,0:T(8,128)(2,1)}, u32[]{:S(2)}) copy-start(bf16[2688,256]{1,0:T(8,128)(2,1)} %copy-done.13) | copy-start | bytes 4128772
  190.5 18.4 %copy-start.16 = (bf16[2688,256]{1,0:T(8,128)(2,1)S(1)}, bf16[2688,256]{1,0:T(8,128)(2,1)}, u32[]{:S(2)}) copy-start(bf16[2688,256]{1,0:T(8,128)(2,1)} %copy-done.15) | copy-start | bytes 4128772
  190.6 18.4 %copy-start.24 = (bf16[2688,512]{1,0:T(8,128)(2,1)S(1)}, bf16[2688,512]{1,0:T(8,128)(2,1)}, u32[]{:S(2)}) copy-start(bf16[2688,512]{1,0:T(8,128)(2,1)} %copy-done.23) | copy-start | bytes 8257540
  190.6 77.0 %collective-permute-start.28 = (bf16[5504,256]{1,0:T(8,128)(2,1)}, bf16[5504,256]{1,0:T(8,128)(2,1)}, u32[]{:S(2)}, u32[]{:S(2)}) collective-permute-start(bf16[5504,256]{1,0:T(8,128)(2,1)} %fusion.1), channel_id=1, source_target_pairs={{0,4},{2,6},{4,0},{6,2},{8,12},{10,14},{12,8},{14,10},{16,20},{18,... | collective-permute-start | bytes 8454152 | tf_op jit(solution)/shard_map/ppermute | solution.py:32
  202.8 18.9 %collective-permute-start.22 = (bf16[128,2688]{1,0:T(8,128)(2,1)S(1)}, bf16[128,2688]{1,0:T(8,128)(2,1)S(1)}, u32[]{:S(2)}, u32[]{:S(2)}) collective-permute-start(bf16[128,2688]{1,0:T(8,128)(2,1)S(1)} %get-tuple-element.53), channel_id=1, source_target_pairs={{0,8},{2,10},{4,12},{6,14},{8,16},{10,18},{12,20},{14,22},{16,24},... | collective-permute-start | bytes 2064392 | tf_op jit(solution)/shard_map/ppermute | solution.py:40
  205.3 18.7 %collective-permute-start.23 = (bf16[128,2688]{1,0:T(8,128)(2,1)S(1)}, bf16[128,2688]{1,0:T(8,128)(2,1)S(1)}, u32[]{:S(2)}, u32[]{:S(2)}) collective-permute-start(bf16[128,2688]{1,0:T(8,128)(2,1)S(1)} %get-tuple-element.55), channel_id=1, source_target_pairs={{24,16},{26,18},{28,20},{30,22},{16,8},{18,10},{20,12},{22,14},{8,... | collective-permute-start | bytes 2064392 | tf_op jit(solution)/shard_map/ppermute | solution.py:40
  212.2 12.2 %copy-start.8 = (bf16[128,5504]{1,0:T(8,128)(2,1)S(1)}, bf16[128,5504]{1,0:T(8,128)(2,1)}, u32[]{:S(2)}) copy-start(bf16[128,5504]{1,0:T(8,128)(2,1)} %param.4) | copy-start | bytes 4227076
  217.6 6.8 %copy-start.6 = (bf16[128,5504]{1,0:T(8,128)(2,1)S(1)}, bf16[128,5504]{1,0:T(8,128)(2,1)}, u32[]{:S(2)}) copy-start(bf16[128,5504]{1,0:T(8,128)(2,1)} %param.5) | copy-start | bytes 4227076
  224.1 9.3 %collective-permute-start.24 = (bf16[128,1024]{1,0:T(8,128)(2,1)S(1)}, bf16[128,1024]{1,0:T(8,128)(2,1)S(1)}, u32[]{:S(2)}, u32[]{:S(2)}) collective-permute-start(bf16[128,1024]{1,0:T(8,128)(2,1)S(1)} %get-tuple-element.81), channel_id=1, source_target_pairs={{0,8},{2,10},{4,12},{6,14},{8,16},{10,18},{12,20},{14,22},{16,24},... | collective-permute-start | bytes 786440 | tf_op jit(solution)/shard_map/ppermute | solution.py:36
  227.1 18.8 %collective-permute-start.25 = (bf16[128,1024]{1,0:T(8,128)(2,1)S(1)}, bf16[128,1024]{1,0:T(8,128)(2,1)S(1)}, u32[]{:S(2)}, u32[]{:S(2)}) collective-permute-start(bf16[128,1024]{1,0:T(8,128)(2,1)S(1)} %get-tuple-element.80), channel_id=1, source_target_pairs={{0,16},{2,18},{4,20},{6,22},{8,24},{10,26},{12,28},{14,30},{16,0},... | collective-permute-start | bytes 786440 | tf_op jit(solution)/shard_map/ppermute | solution.py:36
  233.3 16.0 %collective-permute-start.26 = (bf16[128,1024]{1,0:T(8,128)(2,1)S(1)}, bf16[128,1024]{1,0:T(8,128)(2,1)S(1)}, u32[]{:S(2)}, u32[]{:S(2)}) collective-permute-start(bf16[128,1024]{1,0:T(8,128)(2,1)S(1)} %get-tuple-element.57), channel_id=1, source_target_pairs={{0,24},{2,26},{4,28},{6,30},{8,0},{10,2},{12,4},{14,6},{16,8},{18,... | collective-permute-start | bytes 786440 | tf_op jit(solution)/shard_map/ppermute | solution.py:36
  249.5 14.0 %collective-permute-start.27 = (bf16[128,2048]{1,0:T(8,128)(2,1)S(1)}, bf16[128,2048]{1,0:T(8,128)(2,1)S(1)}, u32[]{:S(2)}, u32[]{:S(2)}) collective-permute-start(bf16[128,2048]{1,0:T(8,128)(2,1)S(1)} %pad_maximum_fusion.17), channel_id=1, source_target_pairs={{0,1},{1,0},{2,3},{3,2},{4,5},{5,4},{6,7},{7,6},{8,9},{9,8},{10,11... | collective-permute-start | bytes 1572872 | tf_op jit(solution)/shard_map/ppermute | solution.py:49
  (8 other events, 25.7 us)
where the time goes:
time: 276 us; the launch traced here: 275 us
  waiting for transfers between devices  127 us (46%)
  starting transfers between devices  55.1 us (20%)
  other arithmetic  47.9 us (17%)
  matrix products  28.9 us (10%)
  local copies, waits for them, and re-layouts  14.9 us (5%)
    ppermute x6, waiting for transfers between devices, shift(): return lax.ppermute(value, 'hst', pairs)  51.4 us
    ppermute x15, starting transfers between devices, far_permute(): return lax.ppermute(value, 'hst', pairs)  39.5 us
    ppermute x15, waiting for transfers between devices, far_permute(): return lax.ppermute(value, 'hst', pairs)  37.9 us
    ppermute x6, waiting for transfers between devices, swap(): return lax.ppermute(value, 'hst', [(h, h ^ bit) for h in range(n_hst)])  24.7 us
    ppermute x2, waiting for transfers between devices, local_shift(): lax.ppermute(value, 'local', [(i, (i + step) % n_local) for i in range(n_...  12.7 us
    dot_general x2, matrix products, on_device(): lax.dot_general(rows, part, SUM_ROWS, preferred_element_type=jnp.float32)  11.8 us
    ppermute x6, starting transfers between devices, shift(): return lax.ppermute(value, 'hst', pairs)  10.4 us
    convert_element_type x4, other arithmetic, reduce_hop(): down_term = (down_term + down.astype(jnp.float32)).astype(jnp.bfloat16)  9.13 us
  transfers between devices with their start and end apart: 29, of which 16 were waited for; matrix products, arithmetic and copies ran while one was open for 26% of the time, Pallas kernels for 0%

commit v1 on v0

--- a/solution.py
+++ b/solution.py
@@ -86,14 +86,15 @@
             d = n_far - j
             up_term, down_term = terms[f][d], terms[f][n_far - d]
             if j == 1:
-                one = after(jnp.where(lower, up_term, down_term).astype(jnp.bfloat16), *fence)
+                one = after(jnp.where(lower, up_term, down_term), *fence)
                 one = far_permute(one, [(0, 1), (n_far - 1, n_far - 2)])
                 none = jnp.zeros_like(one)
                 travel[f] = jnp.where(lower, one, none), jnp.where(lower, none, one)
                 return [one]
             up, down = travel[f]
-            up_term = (up_term + up.astype(jnp.float32)).astype(jnp.bfloat16)
-            down_term = (down_term + down.astype(jnp.float32)).astype(jnp.bfloat16)
+            up_term = (up_term.astype(jnp.float32) + up.astype(jnp.float32)).astype(jnp.bfloat16)
+            down_term = down_term.astype(jnp.float32) + down.astype(jnp.float32)
+            down_term = down_term.astype(jnp.bfloat16)
             up_term, down_term = after(up_term, *fence), after(down_term, *fence)
             travel[f] = both_ways(up_term, down_term, range(0, j))
             return list(travel[f])
@@ -106,7 +107,7 @@
         def reduce_terms(f):
             dots = lax.dot_general(
                 cot_rows, weights[f], KEEP_COLS, preferred_element_type=jnp.float32
-            )
+            ).astype(jnp.bfloat16)
             return [dots[e * tokens : (e + 1) * tokens] for e in range(n_far)]
 
         weights, terms = {}, {}
@@ -152,25 +153,27 @@
             above_e, below_e = after(above[e], *fence), after(below[n_far - e], *fence)
             slots.append(jnp.where(far + e < n_far, above_e, below_e))
         rows = jnp.concatenate(slots, axis=0)
-        give, keep = (
-            lax.dot_general(rows, part, SUM_ROWS, preferred_element_type=jnp.float32)
-            for part in (cot_rows[:, 2 * width :], cot_rows[:, : 2 * width])
-        )
-        theirs = swap(give.astype(jnp.bfloat16), 1)
-        give = (keep[:, width:] + theirs[:, width:].astype(jnp.float32)).astype(jnp.bfloat16)
+
+        def grad_terms(lo, hi):
+            part = cot_rows[:, lo * width : hi * width]
+            return lax.dot_general(rows, part, SUM_ROWS, preferred_element_type=jnp.float32)
+
+        theirs = swap(grad_terms(2, 4).astype(jnp.bfloat16), 1)
+        give = grad_terms(1, 2) + theirs[:, width:].astype(jnp.float32)
+        give = give.astype(jnp.bfloat16)
         other_grad = swap(give, 2)
         for part in travel:
             travel[part] = tuple(after(value, give) for value in travel[part])
-        grad = keep[:, :width] + theirs[:, :width].astype(jnp.float32)
-        down_grad = grad + other_grad.astype(jnp.float32)
-
-        fence = waits + [give]
-        waits = reduce_hop(1, last_hop)
-        rows = after(rows, *fence)
+        rows = after(rows, give)
+        down_grad = grad_terms(0, 1) + after(theirs, give)[:, :width].astype(jnp.float32)
+        down_grad = down_grad + other_grad.astype(jnp.float32)
         out_sum = 0.0
         for f, (lo, hi) in enumerate(bounds):
             out_sum += jnp.dot(rows[:, lo:hi], weights[f], preferred_element_type=jnp.float32)
         out_terms = after(out_sum.astype(jnp.bfloat16), *waits)
+
+        fence = waits + [give]
+        waits = reduce_hop(1, last_hop)
         outs = [out_terms[:tokens]]
         for e in range(1, n_far):
             term = out_terms[e * tokens : (e + 1) * tokens]
@@ -178,7 +181,8 @@
         up_parts, gate_parts = [], []
         for f in range(2):
             up, down = travel[f]
-            hidden_grad = terms[f][0] + up.astype(jnp.float32) + down.astype(jnp.float32)
+            hidden_grad = terms[f][0].astype(jnp.float32) + up.astype(jnp.float32)
+            hidden_grad += down.astype(jnp.float32)
             lo, hi = bounds[f]
             gate_wide = gate_act[:, lo:hi].astype(jnp.float32)
             up_wide = up_act[:, lo:hi].astype(jnp.float32)
@@ -202,7 +206,7 @@
         sides = [local_shift(half_of(step), step) for step in range(1, n_local)]
         output = half_of(0).astype(jnp.float32)
         for side in sides:
-            output = output + side.astype(jnp.float32)
+            output = output + after(side, down_grad).astype(jnp.float32)
         output = output.astype(jnp.bfloat16).reshape(tokens, per_half, QUAD, width)
         return (
             picked(output, slot_of(near), 2).reshape(tokens, half),

time: 276 us -> 265 us (0.960)
  other arithmetic: 47.9 us -> 29 us
  matrix products: 28.9 us -> 37 us
  waiting for transfers between devices: 127 us -> 132 us
  starting transfers between devices: 55.1 us -> 50.6 us
    ppermute x6, waiting for transfers between devices: 51.4 us -> 67.4 us  [shift(): return lax.ppermute(value, 'hst', pairs)]
    convert_element_type x7 -> x4, other arithmetic: 16.7 us -> 5.04 us  [the longest x3 4.72 us: reduce_hop(): down_term = down_term.astype(jnp.bfloat16)]
    ppermute x2, waiting for transfers between devices: 12.7 us -> 3.99 us  [local_shift(): lax.ppermute(value, 'local', [(i, (i + step) % n_local) for i in range(n_...]
    add x1 -> x0, other arithmetic: 7.52 us -> none  [on_device(): down_grad = grad + other_grad.astype(jnp.float32)]
    ppermute x6, starting transfers between devices: 10.4 us -> 3.58 us  [shift(): return lax.ppermute(value, 'hst', pairs)]
    dot_general x2 -> x3, matrix products: 11.8 us -> 17.8 us  [grad_terms(): lax.dot_general(rows, part, SUM_ROWS, preferred_element_type=jnp.float32)]
    ppermute x6, waiting for transfers between devices: 24.7 us -> 19.8 us  [swap(): return lax.ppermute(value, 'hst', [(h, h ^ bit) for h in range(n_hst)])]
    ppermute x15, waiting for transfers between devices: 37.9 us -> 40.7 us  [far_permute(): return lax.ppermute(value, 'hst', pairs)]
  transfers between devices with their start and end apart: 29 -> 29, of which waited for: 16 -> 14; matrix products, arithmetic and copies ran while one was open for 26% -> 24% of each run, Pallas kernels for 0% -> 0%
where the time goes in v1:
time: 265 us; the launch traced here: 264 us
  waiting for transfers between devices  132 us (50%)
  starting transfers between devices  50.6 us (19%)
  matrix products  37 us (14%)
  other arithmetic  29 us (11%)
  local copies, waits for them, and re-layouts  13.5 us (5%)
    ppermute x6, waiting for transfers between devices, shift(): return lax.ppermute(value, 'hst', pairs)  67.4 us
    ppermute x15, starting transfers between devices, far_permute(): return lax.ppermute(value, 'hst', pairs)  41 us
    ppermute x15, waiting for transfers between devices, far_permute(): return lax.ppermute(value, 'hst', pairs)  40.7 us
    ppermute x6, waiting for transfers between devices, swap(): return lax.ppermute(value, 'hst', [(h, h ^ bit) for h in range(n_hst)])  19.8 us
    dot_general x3, matrix products, grad_terms(): lax.dot_general(rows, part, SUM_ROWS, preferred_element_type=jnp.float32)  17.8 us
    dot_general x2, matrix products, on_device(): jnp.dot(rows[:, lo:hi], weights[f], preferred_element_type=jnp.float32)  10.4 us
    dot_general x2, matrix products, reduce_terms(): lax.dot_general(cot_rows, weights[f], KEEP_COLS, preferred_element_type=j...  8.77 us
  transfers between devices with their start and end apart: 29, of which 14 were waited for; matrix products, arithmetic and copies ran while one was open for 24% of the time, Pallas kernels for 0%

profile of v1, /device:TPU:8, one launch (start us, length us, event | category | flops | bytes accessed | tf_op | source)
XLA Modules:
  0.0 263.8 jit_solution(6667594565201052304)
XLA Ops:
  0.7 1.6 collective-permute-start.2
  2.2 1.5 slice.77
  3.7 1.6 collective-permute-start.6
  5.3 1.9 fusion.8
  7.2 2.3 collective-permute-start
  9.6 3.5 %collective-permute-start.1 = (bf16[128,5504]{1,0:T(8,128)(2,1)}, bf16[128,5504]{1,0:T(8,128)(2,1)}, u32[]{:S(2)}, u32[]{:S(2)}) collective-permute-start(bf16[128,5504]{1,0:T(8,128)(2,1)} %fusion.8), channel_id=1, source_target_pairs={{0,8},{2,10},{4,12},{6,14},{8,16},{10,18},{12,20},{14,22},{16,24},... | collective-permute-start | bytes 4227080 | tf_op jit(solution)/shard_map/ppermute | solution.py:40
  15.5 2.2 constant_dynamic-slice_fusion.15
  17.7 2.4 pad_maximum_fusion.14
  20.6 2.2 constant_dynamic-slice_fusion.8
  23.3 2.9 %collective-permute-start.4 = (bf16[128,1024]{1,0:T(8,128)(2,1)S(1)}, bf16[128,1024]{1,0:T(8,128)(2,1)S(1)}, u32[]{:S(2)}, u32[]{:S(2)}) collective-permute-start(bf16[128,1024]{1,0:T(8,128)(2,1)S(1)} %bitcast.19), channel_id=1, source_target_pairs={{0,16},{2,18},{4,20},{6,22},{8,24},{10,26},{12,28},{14,30},{16,0},... | collective-permute-start | bytes 786440 | tf_op jit(solution)/shard_map/ppermute | solution.py:36
  26.2 33.8 %collective-permute-done.3 = bf16[128,1024]{1,0:T(8,128)(2,1)S(1)} collective-permute-done((bf16[128,1024]{1,0:T(8,128)(2,1)S(1)}, bf16[128,1024]{1,0:T(8,128)(2,1)S(1)}, u32[]{:S(2)}, u32[]{:S(2)}) %collective-permute-start.3) | collective-permute-done | bytes 262176 | tf_op jit(solution)/shard_map/ppermute | solution.py:36
  60.0 3.1 %pad_maximum_fusion.3 = bf16[2816,512]{1,0:T(8,128)(2,1)} fusion(bf16[2816,256]{1,0:T(8,128)(2,1)} %collective-permute-done.6, bf16[2816,256]{1,0:T(8,128)(2,1)S(1)} %slice.77), kind=kLoop, calls=%fused_computation.12 | loop fusion | flops 5767168 | bytes 5767168 | tf_op jit(solution)/shard_map/concatenate | solution.py:104
  63.1 3.2 %collective-permute-done.5 = bf16[128,1024]{1,0:T(8,128)(2,1)S(1)} collective-permute-done((bf16[128,1024]{1,0:T(8,128)(2,1)S(1)}, bf16[128,1024]{1,0:T(8,128)(2,1)S(1)}, u32[]{:S(2)}, u32[]{:S(2)}) %collective-permute-start.5) | collective-permute-done | bytes 262176 | tf_op jit(solution)/shard_map/ppermute | solution.py:36
  66.5 1.5 slice.78
  68.7 3.1 %collective-permute-start.8 = (bf16[128,5504]{1,0:T(8,128)(2,1)}, bf16[128,5504]{1,0:T(8,128)(2,1)S(1)}, u32[]{:S(2)}, u32[]{:S(2)}) collective-permute-start(bf16[128,5504]{1,0:T(8,128)(2,1)} %collective-permute-done.1), channel_id=1, source_target_pairs={{8,16},{10,18},{12,20},{14,22},{16,24},{18,26},{20,28},{22,30},{9,... | collective-permute-start | bytes 4227080 | tf_op jit(solution)/shard_map/ppermute | solution.py:40
  71.8 2.1 collective-permute-start.7
  74.0 5.6 %convolution_convert_fusion.2 = bf16[512,2816]{1,0:T(8,128)(2,1)S(1)} fusion(bf16[2816,512]{1,0:T(8,128)(2,1)} %collective-permute-done.10, bf16[2816,256]{1,0:T(8,128)(2,1)} %collective-permute-done.6, bf16[2816,256]{1,0:T(8,128)(2,1)S(1)} %copy-done.3, bf16[128,1024]{1,0:T(8,128)(2,1)} %copy-done.26, bf16[128,1024]{1,0:T(8,128)(2,1)} %copy-done.23, ...), kind=kOutput, calls=%fused_computation.9 | convolution fusion | flops 2975727616 | bytes 9699328 | tf_op jit(solution)/shard_map/dot_general | solution.py:108
  80.9 19.8 %collective-permute-done.9 = bf16[2688,256]{1,0:T(8,128)(2,1)S(1)} collective-permute-done((bf16[2688,256]{1,0:T(8,128)(2,1)S(1)}, bf16[2688,256]{1,0:T(8,128)(2,1)S(1)}, u32[]{:S(2)}, u32[]{:S(2)}) %collective-permute-start.9) | collective-permute-done | bytes 1376288 | tf_op jit(solution)/shard_map/ppermute | solution.py:32
  101.0 1.6 collective-permute-done.8
  102.5 4.1 %collective-permute-done.7 = bf16[128,5504]{1,0:T(8,128)(2,1)S(1)} collective-permute-done((bf16[128,5504]{1,0:T(8,128)(2,1)}, bf16[128,5504]{1,0:T(8,128)(2,1)S(1)}, u32[]{:S(2)}, u32[]{:S(2)}) %collective-permute-start.7) | collective-permute-done | bytes 1409056 | tf_op jit(solution)/shard_map/ppermute | solution.py:40
  108.2 1.5 fusion.14
  111.0 4.6 %collective-permute-start.13 = (bf16[128,2816]{1,0:T(8,128)(2,1)}, bf16[128,2816]{1,0:T(8,128)(2,1)}, u32[]{:S(2)}, u32[]{:S(2)}) collective-permute-start(bf16[128,2816]{1,0:T(8,128)(2,1)} %get-tuple-element.41), channel_id=1, source_target_pairs={{0,8},{2,10},{4,12},{6,14},{8,16},{10,18},{12,20},{14,22},{1,9},{3... | collective-permute-start | bytes 2162696 | tf_op jit(solution)/shard_map/ppermute | solution.py:40
  115.5 3.3 %collective-permute-start.12 = (bf16[128,5504]{1,0:T(8,128)(2,1)}, bf16[128,5504]{1,0:T(8,128)(2,1)}, u32[]{:S(2)}, u32[]{:S(2)}) collective-permute-start(bf16[128,5504]{1,0:T(8,128)(2,1)} %broadcast_select_fusion.3), channel_id=1, source_target_pairs={{16,24},{18,26},{20,28},{22,30},{8,0},{10,2},{12,4},{14,6},{17,25}... | collective-permute-start | bytes 4227080 | tf_op jit(solution)/shard_map/ppermute | solution.py:40
  118.8 3.2 %convolution_convert_fusion.1 = bf16[512,2688]{1,0:T(8,128)(2,1)S(1)} fusion(bf16[2688,512]{1,0:T(8,128)(2,1)S(1)} %collective-permute-done.15, bf16[2688,256]{1,0:T(8,128)(2,1)S(1)} %collective-permute-done.9, bf16[2688,256]{1,0:T(8,128)(2,1)S(1)} %slice.78, bf16[128,1024]{1,0:T(8,128)(2,1)S(1)} %copy-done.27, bf16[128,1024]{1,0:T(8,128)(2,1)S(1)} %copy-done.24, ...), kind=kOutput, calls=%fused_computation.8 | convolution fusion | flops 2840657920 | bytes 9306112 | tf_op jit(solution)/shard_map/dot_general | solution.py:108
  122.1 1.5 copy-done
  127.0 3.1 %collective-permute-done.14 = bf16[128,2816]{1,0:T(8,128)(2,1)} collective-permute-done((bf16[128,2816]{1,0:T(8,128)(2,1)}, bf16[128,2816]{1,0:T(8,128)(2,1)}, u32[]{:S(2)}, u32[]{:S(2)}) %collective-permute-start.14) | collective-permute-done | bytes 720928 | tf_op jit(solution)/shard_map/ppermute | solution.py:40
  130.1 2.0 collective-permute-done.13
  132.1 16.1 %collective-permute-done.12 = bf16[128,5504]{1,0:T(8,128)(2,1)} collective-permute-done((bf16[128,5504]{1,0:T(8,128)(2,1)}, bf16[128,5504]{1,0:T(8,128)(2,1)}, u32[]{:S(2)}, u32[]{:S(2)}) %collective-permute-start.12) | collective-permute-done | bytes 1409056 | tf_op jit(solution)/shard_map/ppermute | solution.py:40
  148.2 1.6 broadcast_select_fusion.1
  149.8 3.0 %broadcast_select_fusion.2 = (bf16[128,5504]{1,0:T(8,128)(2,1)S(1)}, bf16[128,5504]{1,0:T(8,128)(2,1)S(1)}) fusion(bf16[128,5504]{1,0:T(8,128)(2,1)} %collective-permute-done, bf16[128,5504]{1,0:T(8,128)(2,1)} %collective-permute-done.12, pred[]{:T(512)S(6)} %lt.161, bf16[128,5504]{1,0:T(8,128)(2,1)} %collective-permute-done.1, pred[]{:T(512)S(6)} %lt.163), kind=kLoop, calls=%fused_computation.51 | loop fusion | flops 1409024 | bytes 7045122 | tf_op jit(solution)/shard_map/jit(_where)/select_n | solution.py:154
  152.8 6.8 %convolution_convert_fusion = bf16[5504,512]{1,0:T(8,128)(2,1)} fusion(bf16[512,1024]{1,0:T(8,128)(2,1)S(1)} %pad_maximum_fusion.15, bf16[128,5504]{1,0:T(8,128)(2,1)S(1)} %get-tuple-element.77, bf16[128,5504]{1,0:T(8,128)(2,1)S(1)} %broadcast_select_fusion.1, bf16[128,5504]{1,0:T(8,128)(2,1)S(1)} %get-tuple-element.76, bf16[128,5504]{1,0:T(8,128)(2,1)} %fusion.8), kind=kOutput, calls=%fused_computation | convolution fusion | flops 2911043584 | bytes 11796480 | tf_op jit(solution)/shard_map/dot_general | solution.py:159
  159.7 1.8 add_convert_fusion.1
  161.6 2.1 collective-permute-start.18
  163.6 4.0 %collective-permute-start.19 = (bf16[128,2816]{1,0:T(8,128)(2,1)S(1)}, bf16[128,2816]{1,0:T(8,128)(2,1)S(1)}, u32[]{:S(2)}, u32[]{:S(2)}) collective-permute-start(bf16[128,2816]{1,0:T(8,128)(2,1)S(1)} %get-tuple-element.72), channel_id=1, source_target_pairs={{24,16},{26,18},{28,20},{30,22},{16,8},{18,10},{20,12},{22,14},{8,... | collective-permute-start | bytes 2162696 | tf_op jit(solution)/shard_map/ppermute | solution.py:40
  170.4 4.9 %collective-permute-start.20 = (bf16[128,2688]{1,0:T(8,128)(2,1)S(1)}, bf16[128,2688]{1,0:T(8,128)(2,1)S(1)}, u32[]{:S(2)}, u32[]{:S(2)}) collective-permute-start(bf16[128,2688]{1,0:T(8,128)(2,1)S(1)} %get-tuple-element.52), channel_id=1, source_target_pairs={{0,8},{2,10},{4,12},{6,14},{8,16},{10,18},{12,20},{14,22},{1,9},{3... | collective-permute-start | bytes 2064392 | tf_op jit(solution)/shard_map/ppermute | solution.py:40
  175.3 2.9 %pad_maximum_fusion.1 = bf16[512,5504]{1,0:T(8,128)(2,1)S(1)} fusion(bf16[128,5504]{1,0:T(8,128)(2,1)S(1)} %copy-done.17, bf16[128,5504]{1,0:T(8,128)(2,1)S(1)} %copy-done.13, bf16[128,5504]{1,0:T(8,128)(2,1)S(1)} %copy-done.15, bf16[128,5504]{1,0:T(8,128)(2,1)} %fusion.8), kind=kLoop, calls=%fused_computation.6 | loop fusion | flops 22544384 | bytes 11272192 | tf_op jit(solution)/shard_map/concatenate | solution.py:155
  178.3 5.0 %fusion.1 = bf16[5504,256]{1,0:T(8,128)(2,1)} fusion(bf16[5504,512]{1,0:T(8,128)(2,1)} %collective-permute-done.17, bf16[128,1024]{1,0:T(8,128)(2,1)S(1)} %copy-done.28, bf16[128,1024]{1,0:T(8,128)(2,1)S(1)} %copy-done.25, bf16[128,1024]{1,0:T(8,128)(2,1)S(1)} %collective-permute-done.3, bf16[128,1024]{1,0:T(8,128)(2,1)S(1)} %bitcast.16, ...), kind=kOutput, calls=%fused_computation.4 | convolution fusion | flops 1470660608 | bytes 12320768 | tf_op jit(solution)/shard_map/dot_general | solution.py:159
  183.3 1.5 collective-permute-start.26
  184.8 13.8 %collective-permute-done.21 = bf16[128,2688]{1,0:T(8,128)(2,1)S(1)} collective-permute-done((bf16[128,2688]{1,0:T(8,128)(2,1)S(1)}, bf16[128,2688]{1,0:T(8,128)(2,1)S(1)}, u32[]{:S(2)}, u32[]{:S(2)}) %collective-permute-start.21) | collective-permute-done | bytes 688160 | tf_op jit(solution)/shard_map/ppermute | solution.py:40
  198.6 5.0 %fusion.9 = f32[512,1024]{1,0:T(8,128)S(1)} fusion(bf16[512,5504]{1,0:T(8,128)(2,1)S(1)} %pad_maximum_fusion.1, bf16[2688,512]{1,0:T(8,128)(2,1)} %copy-done.29, bf16[2688,256]{1,0:T(8,128)(2,1)S(1)} %copy-done.21, bf16[2688,256]{1,0:T(8,128)(2,1)S(1)} %copy-done.19), kind=kOutput, calls=%fused_computation.21 | convolution fusion | flops 2835087360 | bytes 10354688 | tf_op jit(solution)/shard_map/dot_general | solution.py:172
  203.6 5.4 %add_convert_fusion = bf16[512,1024]{1,0:T(8,128)(2,1)S(1)} fusion(f32[512,1024]{1,0:T(8,128)S(1)} %fusion.9, bf16[2816,512]{1,0:T(8,128)(2,1)} %collective-permute-done.10, bf16[2816,256]{1,0:T(8,128)(2,1)} %collective-permute-done.6, bf16[2816,256]{1,0:T(8,128)(2,1)S(1)} %copy-done.4, bf16[512,5504]{1,0:T(8,128)(2,1)S(1)} %pad_maximum_fusion.1), kind=kOutput, calls=%fused_computation.26 | convolution fusion | flops 2971140096 | bytes 11796480 | tf_op jit(solution)/shard_map/dot_general | solution.py:172
  209.9 2.1 collective-permute-start.27
  211.9 4.0 %collective-permute-start.28 = (bf16[128,2688]{1,0:T(8,128)(2,1)S(1)}, bf16[128,2688]{1,0:T(8,128)(2,1)S(1)}, u32[]{:S(2)}, u32[]{:S(2)}) collective-permute-start(bf16[128,2688]{1,0:T(8,128)(2,1)S(1)} %get-tuple-element.63), channel_id=1, source_target_pairs={{24,16},{26,18},{28,20},{30,22},{16,8},{18,10},{20,12},{22,14},{8,... | collective-permute-start | bytes 2064392 | tf_op jit(solution)/shard_map/ppermute | solution.py:40
  216.0 2.5 collective-permute-done.22
  219.5 26.9 %collective-permute-done.23 = bf16[128,1024]{1,0:T(8,128)(2,1)S(1)} collective-permute-done((bf16[128,1024]{1,0:T(8,128)(2,1)S(1)}, bf16[128,1024]{1,0:T(8,128)(2,1)S(1)}, u32[]{:S(2)}, u32[]{:S(2)}) %collective-permute-start.23) | collective-permute-done | bytes 262176 | tf_op jit(solution)/shard_map/ppermute | solution.py:36
  249.2 1.7 pad_maximum_fusion.11
  250.9 6.0 %fusion = f32[5504,256]{1,0:T(8,128)} fusion(bf16[512,5504]{1,0:T(8,128)(2,1)S(1)} %pad_maximum_fusion.1, bf16[5504,256]{1,0:T(8,128)(2,1)S(1)} %collective-permute-done.26, bf16[5504,512]{1,0:T(8,128)(2,1)} %collective-permute-done.17, bf16[128,1024]{1,0:T(8,128)(2,1)S(1)} %copy-done.28, bf16[128,1024]{1,0:T(8,128)(2,1)S(1)} %copy-done.25, ...), kind=kOutput, calls=%fused_computation.3 | convolution fusion | flops 1449525248 | bytes 17956864 | tf_op jit(solution)/shard_map/dot_general | solution.py:159
  257.0 2.8 %collective-permute-done.25 = bf16[128,2048]{1,0:T(8,128)(2,1)S(1)} collective-permute-done((bf16[128,2048]{1,0:T(8,128)(2,1)S(1)}, bf16[128,2048]{1,0:T(8,128)(2,1)S(1)}, u32[]{:S(2)}, u32[]{:S(2)}) %collective-permute-start.25) | collective-permute-done | bytes 524320 | tf_op jit(solution)/shard_map/ppermute | solution.py:49
  (115 shorter events, 23.1 us)
Async XLA Ops:
  0.7 13.9 %collective-permute-start.2 = (bf16[128,2048]{1,0:T(8,128)(2,1)}, bf16[128,2048]{1,0:T(8,128)(2,1)S(1)}, u32[]{:S(2)}, u32[]{:S(2)}) collective-permute-start(bf16[128,2048]{1,0:T(8,128)(2,1)} %param.6), channel_id=1, source_target_pairs={{0,1},{1,0},{2,3},{3,2},{4,5},{5,4},{6,7},{7,6},{8,9},{9,8},{10,11... | collective-permute-start | bytes 1572872 | tf_op jit(solution)/shard_map/ppermute | solution.py:49
  3.7 56.3 %copy-start.2 = (bf16[2816,256]{1,0:T(8,128)(2,1)}, bf16[2816,256]{1,0:T(8,128)(2,1)S(1)}, u32[]{:S(2)}) copy-start(bf16[2816,256]{1,0:T(8,128)(2,1)S(1)} %slice.77) | copy-start | bytes 4325380
  3.7 10.9 %copy-start.22 = (bf16[128,2048]{1,0:T(8,128)(2,1)S(1)}, bf16[128,2048]{1,0:T(8,128)(2,1)}, u32[]{:S(2)}) copy-start(bf16[128,2048]{1,0:T(8,128)(2,1)} %param.6) | copy-start | bytes 1572868
  3.7 56.3 %collective-permute-start.6 = (bf16[2816,256]{1,0:T(8,128)(2,1)S(1)}, bf16[2816,256]{1,0:T(8,128)(2,1)}, u32[]{:S(2)}, u32[]{:S(2)}) collective-permute-start(bf16[2816,256]{1,0:T(8,128)(2,1)S(1)} %slice.77), channel_id=1, source_target_pairs={{0,4},{2,6},{4,0},{6,2},{8,12},{10,14},{12,8},{14,10},{16,20},{18,... | collective-permute-start | bytes 4325384 | tf_op jit(solution)/shard_map/ppermute | solution.py:32
  7.2 59.1 %collective-permute-start = (bf16[128,5504]{1,0:T(8,128)(2,1)}, bf16[128,5504]{1,0:T(8,128)(2,1)}, u32[]{:S(2)}, u32[]{:S(2)}) collective-permute-start(bf16[128,5504]{1,0:T(8,128)(2,1)} %fusion.8), channel_id=1, source_target_pairs={{24,16},{26,18},{28,20},{30,22},{16,8},{18,10},{20,12},{22,14},{8,... | collective-permute-start | bytes 4227080 | tf_op jit(solution)/shard_map/ppermute | solution.py:40
  9.6 56.8 %collective-permute-start.1 = (bf16[128,5504]{1,0:T(8,128)(2,1)}, bf16[128,5504]{1,0:T(8,128)(2,1)}, u32[]{:S(2)}, u32[]{:S(2)}) collective-permute-start(bf16[128,5504]{1,0:T(8,128)(2,1)} %fusion.8), channel_id=1, source_target_pairs={{0,8},{2,10},{4,12},{6,14},{8,16},{10,18},{12,20},{14,22},{16,24},... | collective-permute-start | bytes 4227080 | tf_op jit(solution)/shard_map/ppermute | solution.py:40
  22.8 37.1 %collective-permute-start.3 = (bf16[128,1024]{1,0:T(8,128)(2,1)S(1)}, bf16[128,1024]{1,0:T(8,128)(2,1)S(1)}, u32[]{:S(2)}, u32[]{:S(2)}) collective-permute-start(bf16[128,1024]{1,0:T(8,128)(2,1)S(1)} %bitcast.20), channel_id=1, source_target_pairs={{0,24},{2,26},{4,28},{6,30},{8,0},{10,2},{12,4},{14,6},{16,8},{18,... | collective-permute-start | bytes 786440 | tf_op jit(solution)/shard_map/ppermute | solution.py:36
  23.3 39.9 %collective-permute-start.4 = (bf16[128,1024]{1,0:T(8,128)(2,1)S(1)}, bf16[128,1024]{1,0:T(8,128)(2,1)S(1)}, u32[]{:S(2)}, u32[]{:S(2)}) collective-permute-start(bf16[128,1024]{1,0:T(8,128)(2,1)S(1)} %bitcast.19), channel_id=1, source_target_pairs={{0,16},{2,18},{4,20},{6,22},{8,24},{10,26},{12,28},{14,30},{16,0},... | collective-permute-start | bytes 786440 | tf_op jit(solution)/shard_map/ppermute | solution.py:36
  60.0 6.4 %collective-permute-start.5 = (bf16[128,1024]{1,0:T(8,128)(2,1)S(1)}, bf16[128,1024]{1,0:T(8,128)(2,1)S(1)}, u32[]{:S(2)}, u32[]{:S(2)}) collective-permute-start(bf16[128,1024]{1,0:T(8,128)(2,1)S(1)} %bitcast.18), channel_id=1, source_target_pairs={{0,8},{2,10},{4,12},{6,14},{8,16},{10,18},{12,20},{14,22},{16,24},... | collective-permute-start | bytes 786440 | tf_op jit(solution)/shard_map/ppermute | solution.py:36
  63.1 10.8 %copy-start.23 = (bf16[128,1024]{1,0:T(8,128)(2,1)}, bf16[128,1024]{1,0:T(8,128)(2,1)S(1)}, u32[]{:S(2)}) copy-start(bf16[128,1024]{1,0:T(8,128)(2,1)S(1)} %collective-permute-done.4) | copy-start | bytes 786436
  66.4 7.6 %collective-permute-start.10 = (bf16[2816,512]{1,0:T(8,128)(2,1)}, bf16[2816,512]{1,0:T(8,128)(2,1)}, u32[]{:S(2)}, u32[]{:S(2)}) collective-permute-start(bf16[2816,512]{1,0:T(8,128)(2,1)} %pad_maximum_fusion.3), channel_id=1, source_target_pairs={{0,2},{2,0},{4,6},{6,4},{8,10},{10,8},{12,14},{14,12},{16,18},{18,... | collective-permute-start | bytes 8650760 | tf_op jit(solution)/shard_map/ppermute | solution.py:32
  68.0 50.8 %copy-start.18 = (bf16[2688,256]{1,0:T(8,128)(2,1)}, bf16[2688,256]{1,0:T(8,128)(2,1)S(1)}, u32[]{:S(2)}) copy-start(bf16[2688,256]{1,0:T(8,128)(2,1)S(1)} %slice.78) | copy-start | bytes 4128772
  68.1 32.6 %collective-permute-start.9 = (bf16[2688,256]{1,0:T(8,128)(2,1)S(1)}, bf16[2688,256]{1,0:T(8,128)(2,1)S(1)}, u32[]{:S(2)}, u32[]{:S(2)}) collective-permute-start(bf16[2688,256]{1,0:T(8,128)(2,1)S(1)} %slice.78), channel_id=1, source_target_pairs={{0,4},{2,6},{4,0},{6,2},{8,12},{10,14},{12,8},{14,10},{16,20},{18,... | collective-permute-start | bytes 4128776 | tf_op jit(solution)/shard_map/ppermute | solution.py:32
  68.7 33.9 %collective-permute-start.8 = (bf16[128,5504]{1,0:T(8,128)(2,1)}, bf16[128,5504]{1,0:T(8,128)(2,1)S(1)}, u32[]{:S(2)}, u32[]{:S(2)}) collective-permute-start(bf16[128,5504]{1,0:T(8,128)(2,1)} %collective-permute-done.1), channel_id=1, source_target_pairs={{8,16},{10,18},{12,20},{14,22},{16,24},{18,26},{20,28},{22,30},{9,... | collective-permute-start | bytes 4227080 | tf_op jit(solution)/shard_map/ppermute | solution.py:40
  71.8 34.8 %collective-permute-start.7 = (bf16[128,5504]{1,0:T(8,128)(2,1)}, bf16[128,5504]{1,0:T(8,128)(2,1)S(1)}, u32[]{:S(2)}, u32[]{:S(2)}) collective-permute-start(bf16[128,5504]{1,0:T(8,128)(2,1)} %collective-permute-done), channel_id=1, source_target_pairs={{16,8},{18,10},{20,12},{22,14},{8,0},{10,2},{12,4},{14,6},{17,9},{... | collective-permute-start | bytes 4227080 | tf_op jit(solution)/shard_map/ppermute | solution.py:40
  79.6 27.0 %collective-permute-start.11 = (bf16[128,2816]{1,0:T(8,128)(2,1)S(1)}, bf16[128,2816]{1,0:T(8,128)(2,1)S(1)}, u32[]{:S(2)}, u32[]{:S(2)}) collective-permute-start(bf16[128,2816]{1,0:T(8,128)(2,1)S(1)} %broadcast_select_fusion.4), channel_id=1, source_target_pairs={{0,8},{2,10},{4,12},{6,14},{24,16},{26,18},{28,20},{30,22},{1,9},{... | collective-permute-start | bytes 2162696 | tf_op jit(solution)/shard_map/ppermute | solution.py:40
  100.7 18.1 %copy-start.20 = (bf16[2688,256]{1,0:T(8,128)(2,1)}, bf16[2688,256]{1,0:T(8,128)(2,1)S(1)}, u32[]{:S(2)}) copy-start(bf16[2688,256]{1,0:T(8,128)(2,1)S(1)} %collective-permute-done.9) | copy-start | bytes 4128772
  106.6 12.2 %collective-permute-start.15 = (bf16[2688,512]{1,0:T(8,128)(2,1)S(1)}, bf16[2688,512]{1,0:T(8,128)(2,1)S(1)}, u32[]{:S(2)}, u32[]{:S(2)}) collective-permute-start(bf16[2688,512]{1,0:T(8,128)(2,1)S(1)} %pad_maximum_fusion.4), channel_id=1, source_target_pairs={{0,2},{2,0},{4,6},{6,4},{8,10},{10,8},{12,14},{14,12},{16,18},{18,... | collective-permute-start | bytes 8257544 | tf_op jit(solution)/shard_map/ppermute | solution.py:32
  108.2 10.6 %copy-start.24 = (bf16[128,1024]{1,0:T(8,128)(2,1)S(1)}, bf16[128,1024]{1,0:T(8,128)(2,1)}, u32[]{:S(2)}) copy-start(bf16[128,1024]{1,0:T(8,128)(2,1)} %copy-done.23) | copy-start | bytes 786436
  108.2 10.6 %copy-start.27 = (bf16[128,1024]{1,0:T(8,128)(2,1)S(1)}, bf16[128,1024]{1,0:T(8,128)(2,1)}, u32[]{:S(2)}) copy-start(bf16[128,1024]{1,0:T(8,128)(2,1)} %copy-done.26) | copy-start | bytes 786436
  109.7 20.5 %collective-permute-start.14 = (bf16[128,2816]{1,0:T(8,128)(2,1)}, bf16[128,2816]{1,0:T(8,128)(2,1)}, u32[]{:S(2)}, u32[]{:S(2)}) collective-permute-start(bf16[128,2816]{1,0:T(8,128)(2,1)} %get-tuple-element.42), channel_id=1, source_target_pairs={{24,16},{26,18},{28,20},{30,22},{16,8},{18,10},{20,12},{22,14},{25... | collective-permute-start | bytes 2162696 | tf_op jit(solution)/shard_map/ppermute | solution.py:40
  111.0 21.2 %collective-permute-start.13 = (bf16[128,2816]{1,0:T(8,128)(2,1)}, bf16[128,2816]{1,0:T(8,128)(2,1)}, u32[]{:S(2)}, u32[]{:S(2)}) collective-permute-start(bf16[128,2816]{1,0:T(8,128)(2,1)} %get-tuple-element.41), channel_id=1, source_target_pairs={{0,8},{2,10},{4,12},{6,14},{8,16},{10,18},{12,20},{14,22},{1,9},{3... | collective-permute-start | bytes 2162696 | tf_op jit(solution)/shard_map/ppermute | solution.py:40
  115.5 32.7 %collective-permute-start.12 = (bf16[128,5504]{1,0:T(8,128)(2,1)}, bf16[128,5504]{1,0:T(8,128)(2,1)}, u32[]{:S(2)}, u32[]{:S(2)}) collective-permute-start(bf16[128,5504]{1,0:T(8,128)(2,1)} %broadcast_select_fusion.3), channel_id=1, source_target_pairs={{16,24},{18,26},{20,28},{22,30},{8,0},{10,2},{12,4},{14,6},{17,25}... | collective-permute-start | bytes 4227080 | tf_op jit(solution)/shard_map/ppermute | solution.py:40
  124.5 23.7 %collective-permute-start.16 = (bf16[128,2688]{1,0:T(8,128)(2,1)}, bf16[128,2688]{1,0:T(8,128)(2,1)}, u32[]{:S(2)}, u32[]{:S(2)}) collective-permute-start(bf16[128,2688]{1,0:T(8,128)(2,1)} %broadcast_select_fusion.5), channel_id=1, source_target_pairs={{0,8},{2,10},{4,12},{6,14},{24,16},{26,18},{28,20},{30,22},{1,9},{... | collective-permute-start | bytes 2064392 | tf_op jit(solution)/shard_map/ppermute | solution.py:40
  125.8 22.4 %copy-start.10 = (bf16[128,5504]{1,0:T(8,128)(2,1)S(1)}, bf16[128,5504]{1,0:T(8,128)(2,1)}, u32[]{:S(2)}) copy-start(bf16[128,5504]{1,0:T(8,128)(2,1)} %copy-done.9) | copy-start | bytes 4227076
  159.6 18.7 %collective-permute-start.17 = (bf16[5504,512]{1,0:T(8,128)(2,1)}, bf16[5504,512]{1,0:T(8,128)(2,1)}, u32[]{:S(2)}, u32[]{:S(2)}) collective-permute-start(bf16[5504,512]{1,0:T(8,128)(2,1)} %convolution_convert_fusion), channel_id=1, source_target_pairs={{0,2},{2,0},{4,6},{6,4},{8,10},{10,8},{12,14},{14,12},{16,18},{18,... | collective-permute-start | bytes 16908296 | tf_op jit(solution)/shard_map/ppermute | solution.py:32
  159.7 7.9 %copy-start.1 = (bf16[512,2688]{1,0:T(8,128)(2,1)S(1)}, bf16[512,2688]{1,0:T(8,128)(2,1)}, u32[]{:S(2)}) copy-start(bf16[512,2688]{1,0:T(8,128)(2,1)} %copy-done) | copy-start | bytes 8257540
  159.7 15.6 %copy-start.15 = (bf16[128,5504]{1,0:T(8,128)(2,1)S(1)}, bf16[128,5504]{1,0:T(8,128)(2,1)}, u32[]{:S(2)}) copy-start(bf16[128,5504]{1,0:T(8,128)(2,1)} %copy-done.14) | copy-start | bytes 4227076
  159.7 15.6 %copy-start.17 = (bf16[128,5504]{1,0:T(8,128)(2,1)S(1)}, bf16[128,5504]{1,0:T(8,128)(2,1)}, u32[]{:S(2)}) copy-start(bf16[128,5504]{1,0:T(8,128)(2,1)} %copy-done.16) | copy-start | bytes 4227076
  161.6 13.7 %copy-start.13 = (bf16[128,5504]{1,0:T(8,128)(2,1)S(1)}, bf16[128,5504]{1,0:T(8,128)(2,1)}, u32[]{:S(2)}) copy-start(bf16[128,5504]{1,0:T(8,128)(2,1)} %copy-done.12) | copy-start | bytes 4227076
  161.6 47.5 %collective-permute-start.18 = (bf16[128,2816]{1,0:T(8,128)(2,1)S(1)}, bf16[128,2816]{1,0:T(8,128)(2,1)S(1)}, u32[]{:S(2)}, u32[]{:S(2)}) collective-permute-start(bf16[128,2816]{1,0:T(8,128)(2,1)S(1)} %get-tuple-element.73), channel_id=1, source_target_pairs={{0,8},{2,10},{4,12},{6,14},{8,16},{10,18},{12,20},{14,22},{16,24},... | collective-permute-start | bytes 2162696 | tf_op jit(solution)/shard_map/ppermute | solution.py:40
  163.6 45.5 %collective-permute-start.19 = (bf16[128,2816]{1,0:T(8,128)(2,1)S(1)}, bf16[128,2816]{1,0:T(8,128)(2,1)S(1)}, u32[]{:S(2)}, u32[]{:S(2)}) collective-permute-start(bf16[128,2816]{1,0:T(8,128)(2,1)S(1)} %get-tuple-element.72), channel_id=1, source_target_pairs={{24,16},{26,18},{28,20},{30,22},{16,8},{18,10},{20,12},{22,14},{8,... | collective-permute-start | bytes 2162696 | tf_op jit(solution)/shard_map/ppermute | solution.py:40
  169.0 29.6 %collective-permute-start.21 = (bf16[128,2688]{1,0:T(8,128)(2,1)S(1)}, bf16[128,2688]{1,0:T(8,128)(2,1)S(1)}, u32[]{:S(2)}, u32[]{:S(2)}) collective-permute-start(bf16[128,2688]{1,0:T(8,128)(2,1)S(1)} %get-tuple-element.53), channel_id=1, source_target_pairs={{24,16},{26,18},{28,20},{30,22},{16,8},{18,10},{20,12},{22,14},{25... | collective-permute-start | bytes 2064392 | tf_op jit(solution)/shard_map/ppermute | solution.py:40
  170.3 7.9 %copy-start.25 = (bf16[128,1024]{1,0:T(8,128)(2,1)S(1)}, bf16[128,1024]{1,0:T(8,128)(2,1)}, u32[]{:S(2)}) copy-start(bf16[128,1024]{1,0:T(8,128)(2,1)} %copy-done.23) | copy-start | bytes 786436
  170.3 7.9 %copy-start.28 = (bf16[128,1024]{1,0:T(8,128)(2,1)S(1)}, bf16[128,1024]{1,0:T(8,128)(2,1)}, u32[]{:S(2)}) copy-start(bf16[128,1024]{1,0:T(8,128)(2,1)} %copy-done.26) | copy-start | bytes 786436
  170.4 28.3 %collective-permute-start.20 = (bf16[128,2688]{1,0:T(8,128)(2,1)S(1)}, bf16[128,2688]{1,0:T(8,128)(2,1)S(1)}, u32[]{:S(2)}, u32[]{:S(2)}) collective-permute-start(bf16[128,2688]{1,0:T(8,128)(2,1)S(1)} %get-tuple-element.52), channel_id=1, source_target_pairs={{0,8},{2,10},{4,12},{6,14},{8,16},{10,18},{12,20},{14,22},{1,9},{3... | collective-permute-start | bytes 2064392 | tf_op jit(solution)/shard_map/ppermute | solution.py:40
  178.2 20.4 %copy-start.19 = (bf16[2688,256]{1,0:T(8,128)(2,1)S(1)}, bf16[2688,256]{1,0:T(8,128)(2,1)}, u32[]{:S(2)}) copy-start(bf16[2688,256]{1,0:T(8,128)(2,1)} %copy-done.18) | copy-start | bytes 4128772
  178.3 20.4 %copy-start.21 = (bf16[2688,256]{1,0:T(8,128)(2,1)S(1)}, bf16[2688,256]{1,0:T(8,128)(2,1)}, u32[]{:S(2)}) copy-start(bf16[2688,256]{1,0:T(8,128)(2,1)} %copy-done.20) | copy-start | bytes 4128772
  183.3 20.3 %copy-start.4 = (bf16[2816,256]{1,0:T(8,128)(2,1)S(1)}, bf16[2816,256]{1,0:T(8,128)(2,1)}, u32[]{:S(2)}) copy-start(bf16[2816,256]{1,0:T(8,128)(2,1)} %copy-done.2) | copy-start | bytes 4325380
  183.3 67.6 %collective-permute-start.26 = (bf16[5504,256]{1,0:T(8,128)(2,1)}, bf16[5504,256]{1,0:T(8,128)(2,1)S(1)}, u32[]{:S(2)}, u32[]{:S(2)}) collective-permute-start(bf16[5504,256]{1,0:T(8,128)(2,1)} %fusion.1), channel_id=1, source_target_pairs={{0,4},{2,6},{4,0},{6,2},{8,12},{10,14},{12,8},{14,10},{16,20},{18,... | collective-permute-start | bytes 8454152 | tf_op jit(solution)/shard_map/ppermute | solution.py:32
  209.2 9.3 %copy-start.6 = (bf16[128,5504]{1,0:T(8,128)(2,1)S(1)}, bf16[128,5504]{1,0:T(8,128)(2,1)}, u32[]{:S(2)}) copy-start(bf16[128,5504]{1,0:T(8,128)(2,1)} %param.5) | copy-start | bytes 4227076
  209.2 9.3 %copy-start.8 = (bf16[128,5504]{1,0:T(8,128)(2,1)S(1)}, bf16[128,5504]{1,0:T(8,128)(2,1)}, u32[]{:S(2)}) copy-start(bf16[128,5504]{1,0:T(8,128)(2,1)} %param.4) | copy-start | bytes 4227076
  209.2 9.3 %collective-permute-start.22 = (bf16[128,1024]{1,0:T(8,128)(2,1)S(1)}, bf16[128,1024]{1,0:T(8,128)(2,1)S(1)}, u32[]{:S(2)}, u32[]{:S(2)}) collective-permute-start(bf16[128,1024]{1,0:T(8,128)(2,1)S(1)} %get-tuple-element.85), channel_id=1, source_target_pairs={{0,8},{2,10},{4,12},{6,14},{8,16},{10,18},{12,20},{14,22},{16,24},... | collective-permute-start | bytes 786440 | tf_op jit(solution)/shard_map/ppermute | solution.py:36
  209.9 38.4 %collective-permute-start.27 = (bf16[128,2688]{1,0:T(8,128)(2,1)S(1)}, bf16[128,2688]{1,0:T(8,128)(2,1)S(1)}, u32[]{:S(2)}, u32[]{:S(2)}) collective-permute-start(bf16[128,2688]{1,0:T(8,128)(2,1)S(1)} %get-tuple-element.61), channel_id=1, source_target_pairs={{0,8},{2,10},{4,12},{6,14},{8,16},{10,18},{12,20},{14,22},{16,24},... | collective-permute-start | bytes 2064392 | tf_op jit(solution)/shard_map/ppermute | solution.py:40
  211.9 36.4 %collective-permute-start.28 = (bf16[128,2688]{1,0:T(8,128)(2,1)S(1)}, bf16[128,2688]{1,0:T(8,128)(2,1)S(1)}, u32[]{:S(2)}, u32[]{:S(2)}) collective-permute-start(bf16[128,2688]{1,0:T(8,128)(2,1)S(1)} %get-tuple-element.63), channel_id=1, source_target_pairs={{24,16},{26,18},{28,20},{30,22},{16,8},{18,10},{20,12},{22,14},{8,... | collective-permute-start | bytes 2064392 | tf_op jit(solution)/shard_map/ppermute | solution.py:40
  215.9 30.5 %collective-permute-start.23 = (bf16[128,1024]{1,0:T(8,128)(2,1)S(1)}, bf16[128,1024]{1,0:T(8,128)(2,1)S(1)}, u32[]{:S(2)}, u32[]{:S(2)}) collective-permute-start(bf16[128,1024]{1,0:T(8,128)(2,1)S(1)} %get-tuple-element.84), channel_id=1, source_target_pairs={{0,16},{2,18},{4,20},{6,22},{8,24},{10,26},{12,28},{14,30},{16,0},... | collective-permute-start | bytes 786440 | tf_op jit(solution)/shard_map/ppermute | solution.py:36
  218.5 28.8 %collective-permute-start.24 = (bf16[128,1024]{1,0:T(8,128)(2,1)S(1)}, bf16[128,1024]{1,0:T(8,128)(2,1)S(1)}, u32[]{:S(2)}, u32[]{:S(2)}) collective-permute-start(bf16[128,1024]{1,0:T(8,128)(2,1)S(1)} %get-tuple-element.55), channel_id=1, source_target_pairs={{0,24},{2,26},{4,28},{6,30},{8,0},{10,2},{12,4},{14,6},{16,8},{18,... | collective-permute-start | bytes 786440 | tf_op jit(solution)/shard_map/ppermute | solution.py:36
  247.5 12.2 %collective-permute-start.25 = (bf16[128,2048]{1,0:T(8,128)(2,1)S(1)}, bf16[128,2048]{1,0:T(8,128)(2,1)S(1)}, u32[]{:S(2)}, u32[]{:S(2)}) collective-permute-start(bf16[128,2048]{1,0:T(8,128)(2,1)S(1)} %pad_maximum_fusion.17), channel_id=1, source_target_pairs={{0,1},{1,0},{2,3},{3,2},{4,5},{5,4},{6,7},{7,6},{8,9},{9,8},{10,11... | collective-permute-start | bytes 1572872 | tf_op jit(solution)/shard_map/ppermute | solution.py:49
  (11 other events, 52.8 us)

commit v2 on v1

--- a/solution.py
+++ b/solution.py
@@ -102,7 +102,8 @@
         def weight_columns(f, other):
             lo, hi = bounds[f]
             pair = jnp.concatenate([down_weight[lo:hi], other], axis=1)
-            return jnp.concatenate([pair, move(swap, pair, 1)], axis=1)
+            far_pairs[f] = move(swap, pair, 1)
+            return jnp.concatenate([pair, far_pairs[f]], axis=1)
 
         def reduce_terms(f):
             dots = lax.dot_general(
@@ -110,10 +111,10 @@
             ).astype(jnp.bfloat16)
             return [dots[e * tokens : (e + 1) * tokens] for e in range(n_far)]
 
-        weights, terms = {}, {}
+        weights, far_pairs, terms = {}, {}, {}
 
         parts = [cotangent] + [local_shift(cotangent, n_local - s) for s in range(1, n_local)]
-        weight_side = swap(down_weight[:middle], 2)
+        weight_side = swap(after(down_weight[:middle], hidden), 2)
         waits = gather_hop(1)
         cot_slots = jnp.concatenate(parts, axis=1).reshape(tokens, n_far, QUAD, width)
         cot_slots = picked(cot_slots, [near ^ k for k in ORDER], 2).reshape(tokens, n_far, columns)
@@ -136,10 +137,11 @@
                 weight_side = move(swap, down_weight[middle:], 2)
                 terms[0] = reduce_terms(0)
                 waits.append(weight_side)
-            waits += reduce_hop(0, j - 1)
             if j == 3:
                 weights[1] = weight_columns(1, weight_side)
                 terms[1] = reduce_terms(1)
+                fence = fence + [far_pairs[1]]
+            waits += reduce_hop(0, j - 1)
             if j > 2:
                 waits += reduce_hop(1, j - 2)
             fence = waits
@@ -162,17 +164,18 @@
         give = grad_terms(1, 2) + theirs[:, width:].astype(jnp.float32)
         give = give.astype(jnp.bfloat16)
         other_grad = swap(give, 2)
-        for part in travel:
-            travel[part] = tuple(after(value, give) for value in travel[part])
         rows = after(rows, give)
         down_grad = grad_terms(0, 1) + after(theirs, give)[:, :width].astype(jnp.float32)
         down_grad = down_grad + other_grad.astype(jnp.float32)
         out_sum = 0.0
         for f, (lo, hi) in enumerate(bounds):
             out_sum += jnp.dot(rows[:, lo:hi], weights[f], preferred_element_type=jnp.float32)
+            if f == 0:
+                for part in travel:
+                    travel[part] = tuple(after(value, out_sum) for value in travel[part])
         out_terms = after(out_sum.astype(jnp.bfloat16), *waits)
 
-        fence = waits + [give]
+        fence = waits + [give, out_terms]
         waits = reduce_hop(1, last_hop)
         outs = [out_terms[:tokens]]
         for e in range(1, n_far):

time: 265 us -> 263 us (level)
  transfers between devices with their start and end apart: 29 -> 29, of which waited for: 14 -> 13; matrix products, arithmetic and copies ran while one was open for 24% -> 24% of each run, Pallas kernels for 0% -> 0%
where the time goes in v2:
time: 263 us; the launch traced here: 262 us
  waiting for transfers between devices  130 us (49%)
  starting transfers between devices  50.7 us (19%)
  matrix products  36 us (14%)
  other arithmetic  31 us (12%)
  local copies, waits for them, and re-layouts  12.2 us (5%)
    ppermute x6, waiting for transfers between devices, shift(): return lax.ppermute(value, 'hst', pairs)  67.8 us
    ppermute x15, starting transfers between devices, far_permute(): return lax.ppermute(value, 'hst', pairs)  41 us
    ppermute x15, waiting for transfers between devices, far_permute(): return lax.ppermute(value, 'hst', pairs)  38.7 us
    ppermute x6, waiting for transfers between devices, swap(): return lax.ppermute(value, 'hst', [(h, h ^ bit) for h in range(n_hst)])  19.8 us
    dot_general x3, matrix products, grad_terms(): lax.dot_general(rows, part, SUM_ROWS, preferred_element_type=jnp.float32)  16.7 us
    dot_general x2, matrix products, on_device(): jnp.dot(rows[:, lo:hi], weights[f], preferred_element_type=jnp.float32)  10.5 us
    dot_general x2, matrix products, reduce_terms(): lax.dot_general(cot_rows, weights[f], KEEP_COLS, preferred_element_type=j...  8.78 us
  transfers between devices with their start and end apart: 29, of which 13 were waited for; matrix products, arithmetic and copies ran while one was open for 24% of the time, Pallas kernels for 0%

profile of v2, /device:TPU:8, one launch (start us, length us, event | category | flops | bytes accessed | tf_op | source)
XLA Modules:
  0.0 261.9 jit_solution(14003849707066503789)
XLA Ops:
  0.6 1.6 collective-permute-start.2
  2.2 3.7 %fusion.8 = bf16[128,5504]{1,0:T(8,128)(2,1)} fusion(bf16[128,5504]{1,0:T(8,128)(2,1)} %param.5, bf16[128,5504]{1,0:T(8,128)(2,1)} %param.4), kind=kLoop, calls=%fused_computation.19 | loop fusion | flops 5636096 | bytes 4227072 | tf_op jit(solution)/shard_map/convert_element_type | solution.py:69
  6.0 1.6 collective-permute-start.6
  7.6 2.3 collective-permute-start
  10.0 3.5 %collective-permute-start.1 = (bf16[128,5504]{1,0:T(8,128)(2,1)}, bf16[128,5504]{1,0:T(8,128)(2,1)}, u32[]{:S(2)}, u32[]{:S(2)}) collective-permute-start(bf16[128,5504]{1,0:T(8,128)(2,1)} %fusion.8), channel_id=1, source_target_pairs={{0,8},{2,10},{4,12},{6,14},{8,16},{10,18},{12,20},{14,22},{16,24},... | collective-permute-start | bytes 4227080 | tf_op jit(solution)/shard_map/ppermute | solution.py:40
  15.5 2.2 constant_dynamic-slice_fusion.15
  17.7 2.4 pad_maximum_fusion.14
  20.6 2.2 constant_dynamic-slice_fusion.8
  23.5 3.0 %collective-permute-start.4 = (bf16[128,1024]{1,0:T(8,128)(2,1)S(1)}, bf16[128,1024]{1,0:T(8,128)(2,1)S(1)}, u32[]{:S(2)}, u32[]{:S(2)}) collective-permute-start(bf16[128,1024]{1,0:T(8,128)(2,1)S(1)} %bitcast.19), channel_id=1, source_target_pairs={{0,16},{2,18},{4,20},{6,22},{8,24},{10,26},{12,28},{14,30},{16,0},... | collective-permute-start | bytes 786440 | tf_op jit(solution)/shard_map/ppermute | solution.py:36
  26.5 33.9 %collective-permute-done.3 = bf16[128,1024]{1,0:T(8,128)(2,1)S(1)} collective-permute-done((bf16[128,1024]{1,0:T(8,128)(2,1)S(1)}, bf16[128,1024]{1,0:T(8,128)(2,1)S(1)}, u32[]{:S(2)}, u32[]{:S(2)}) %collective-permute-start.3) | collective-permute-done | bytes 262176 | tf_op jit(solution)/shard_map/ppermute | solution.py:36
  60.4 3.1 %pad_maximum_fusion.3 = bf16[2816,512]{1,0:T(8,128)(2,1)} fusion(bf16[2816,256]{1,0:T(8,128)(2,1)} %collective-permute-done.6, bf16[2816,256]{1,0:T(8,128)(2,1)S(1)} %slice.77), kind=kLoop, calls=%fused_computation.12 | loop fusion | flops 5767168 | bytes 5767168 | tf_op jit(solution)/shard_map/concatenate | solution.py:104
  63.5 3.2 %collective-permute-done.5 = bf16[128,1024]{1,0:T(8,128)(2,1)S(1)} collective-permute-done((bf16[128,1024]{1,0:T(8,128)(2,1)S(1)}, bf16[128,1024]{1,0:T(8,128)(2,1)S(1)}, u32[]{:S(2)}, u32[]{:S(2)}) %collective-permute-start.5) | collective-permute-done | bytes 262176 | tf_op jit(solution)/shard_map/ppermute | solution.py:36
  66.8 1.5 slice.78
  69.1 3.1 %collective-permute-start.8 = (bf16[128,5504]{1,0:T(8,128)(2,1)}, bf16[128,5504]{1,0:T(8,128)(2,1)S(1)}, u32[]{:S(2)}, u32[]{:S(2)}) collective-permute-start(bf16[128,5504]{1,0:T(8,128)(2,1)} %collective-permute-done.1), channel_id=1, source_target_pairs={{8,16},{10,18},{12,20},{14,22},{16,24},{18,26},{20,28},{22,30},{9,... | collective-permute-start | bytes 4227080 | tf_op jit(solution)/shard_map/ppermute | solution.py:40
  72.2 2.1 collective-permute-start.7
  74.4 5.6 %convolution_convert_fusion.2 = bf16[512,2816]{1,0:T(8,128)(2,1)S(1)} fusion(bf16[2816,512]{1,0:T(8,128)(2,1)} %collective-permute-done.10, bf16[2816,256]{1,0:T(8,128)(2,1)} %collective-permute-done.6, bf16[2816,256]{1,0:T(8,128)(2,1)S(1)} %copy-done.3, bf16[128,1024]{1,0:T(8,128)(2,1)} %copy-done.25, bf16[128,1024]{1,0:T(8,128)(2,1)} %copy-done.22, ...), kind=kOutput, calls=%fused_computation.9 | convolution fusion | flops 2975727616 | bytes 9699328 | tf_op jit(solution)/shard_map/dot_general | solution.py:109
  81.3 19.8 %collective-permute-done.9 = bf16[2688,256]{1,0:T(8,128)(2,1)S(1)} collective-permute-done((bf16[2688,256]{1,0:T(8,128)(2,1)S(1)}, bf16[2688,256]{1,0:T(8,128)(2,1)S(1)}, u32[]{:S(2)}, u32[]{:S(2)}) %collective-permute-start.9) | collective-permute-done | bytes 1376288 | tf_op jit(solution)/shard_map/ppermute | solution.py:32
  101.3 1.6 collective-permute-done.8
  102.9 4.1 %collective-permute-done.7 = bf16[128,5504]{1,0:T(8,128)(2,1)S(1)} collective-permute-done((bf16[128,5504]{1,0:T(8,128)(2,1)}, bf16[128,5504]{1,0:T(8,128)(2,1)S(1)}, u32[]{:S(2)}, u32[]{:S(2)}) %collective-permute-start.7) | collective-permute-done | bytes 1409056 | tf_op jit(solution)/shard_map/ppermute | solution.py:40
  107.0 1.4 broadcast_select_fusion.3
  108.6 3.4 %collective-permute-start.12 = (bf16[128,5504]{1,0:T(8,128)(2,1)}, bf16[128,5504]{1,0:T(8,128)(2,1)}, u32[]{:S(2)}, u32[]{:S(2)}) collective-permute-start(bf16[128,5504]{1,0:T(8,128)(2,1)} %broadcast_select_fusion.3), channel_id=1, source_target_pairs={{16,24},{18,26},{20,28},{22,30},{8,0},{10,2},{12,4},{14,6},{17,25}... | collective-permute-start | bytes 4227080 | tf_op jit(solution)/shard_map/ppermute | solution.py:40
  112.0 1.5 fusion.14
  114.8 4.6 %collective-permute-start.14 = (bf16[128,2816]{1,0:T(8,128)(2,1)}, bf16[128,2816]{1,0:T(8,128)(2,1)}, u32[]{:S(2)}, u32[]{:S(2)}) collective-permute-start(bf16[128,2816]{1,0:T(8,128)(2,1)} %get-tuple-element.44), channel_id=1, source_target_pairs={{0,8},{2,10},{4,12},{6,14},{8,16},{10,18},{12,20},{14,22},{1,9},{3... | collective-permute-start | bytes 2162696 | tf_op jit(solution)/shard_map/ppermute | solution.py:40
  119.4 3.2 %convolution_convert_fusion.1 = bf16[512,2688]{1,0:T(8,128)(2,1)S(1)} fusion(bf16[2688,512]{1,0:T(8,128)(2,1)S(1)} %collective-permute-done.13, bf16[2688,256]{1,0:T(8,128)(2,1)S(1)} %collective-permute-done.9, bf16[2688,256]{1,0:T(8,128)(2,1)S(1)} %slice.78, bf16[128,1024]{1,0:T(8,128)(2,1)S(1)} %copy-done.26, bf16[128,1024]{1,0:T(8,128)(2,1)S(1)} %copy-done.23, ...), kind=kOutput, calls=%fused_computation.8 | convolution fusion | flops 2840657920 | bytes 9306112 | tf_op jit(solution)/shard_map/dot_general | solution.py:109
  122.6 1.5 copy-done
  127.6 14.2 %collective-permute-done.12 = bf16[128,5504]{1,0:T(8,128)(2,1)} collective-permute-done((bf16[128,5504]{1,0:T(8,128)(2,1)}, bf16[128,5504]{1,0:T(8,128)(2,1)}, u32[]{:S(2)}, u32[]{:S(2)}) %collective-permute-start.12) | collective-permute-done | bytes 1409056 | tf_op jit(solution)/shard_map/ppermute | solution.py:40
  141.7 8.0 %collective-permute-done.16 = bf16[128,2688]{1,0:T(8,128)(2,1)} collective-permute-done((bf16[128,2688]{1,0:T(8,128)(2,1)}, bf16[128,2688]{1,0:T(8,128)(2,1)}, u32[]{:S(2)}, u32[]{:S(2)}) %collective-permute-start.16) | collective-permute-done | bytes 688160 | tf_op jit(solution)/shard_map/ppermute | solution.py:40
  149.7 1.6 broadcast_select_fusion.1
  151.3 3.0 %broadcast_select_fusion.2 = (bf16[128,5504]{1,0:T(8,128)(2,1)S(1)}, bf16[128,5504]{1,0:T(8,128)(2,1)S(1)}) fusion(bf16[128,5504]{1,0:T(8,128)(2,1)} %collective-permute-done, bf16[128,5504]{1,0:T(8,128)(2,1)} %collective-permute-done.12, pred[]{:T(512)S(6)} %lt.161, bf16[128,5504]{1,0:T(8,128)(2,1)} %collective-permute-done.1, pred[]{:T(512)S(6)} %lt.163), kind=kLoop, calls=%fused_computation.51 | loop fusion | flops 1409024 | bytes 7045122 | tf_op jit(solution)/shard_map/jit(_where)/select_n | solution.py:156
  154.3 6.8 %convolution_convert_fusion = bf16[5504,512]{1,0:T(8,128)(2,1)} fusion(bf16[512,1024]{1,0:T(8,128)(2,1)S(1)} %pad_maximum_fusion.15, bf16[128,5504]{1,0:T(8,128)(2,1)S(1)} %get-tuple-element.79, bf16[128,5504]{1,0:T(8,128)(2,1)S(1)} %broadcast_select_fusion.1, bf16[128,5504]{1,0:T(8,128)(2,1)S(1)} %get-tuple-element.78, bf16[128,5504]{1,0:T(8,128)(2,1)} %fusion.8), kind=kOutput, calls=%fused_computation | convolution fusion | flops 2911043584 | bytes 11796480 | tf_op jit(solution)/shard_map/dot_general | solution.py:161
  161.2 1.6 fusion.24
  162.9 1.8 add_convert_fusion.1
  164.7 1.9 collective-permute-start.18
  166.6 4.0 %collective-permute-start.19 = (bf16[128,2816]{1,0:T(8,128)(2,1)S(1)}, bf16[128,2816]{1,0:T(8,128)(2,1)S(1)}, u32[]{:S(2)}, u32[]{:S(2)}) collective-permute-start(bf16[128,2816]{1,0:T(8,128)(2,1)S(1)} %get-tuple-element.74), channel_id=1, source_target_pairs={{24,16},{26,18},{28,20},{30,22},{16,8},{18,10},{20,12},{22,14},{8,... | collective-permute-start | bytes 2162696 | tf_op jit(solution)/shard_map/ppermute | solution.py:40
  171.9 4.9 %collective-permute-start.20 = (bf16[128,2688]{1,0:T(8,128)(2,1)S(1)}, bf16[128,2688]{1,0:T(8,128)(2,1)S(1)}, u32[]{:S(2)}, u32[]{:S(2)}) collective-permute-start(bf16[128,2688]{1,0:T(8,128)(2,1)S(1)} %get-tuple-element.54), channel_id=1, source_target_pairs={{0,8},{2,10},{4,12},{6,14},{8,16},{10,18},{12,20},{14,22},{1,9},{3... | collective-permute-start | bytes 2064392 | tf_op jit(solution)/shard_map/ppermute | solution.py:40
  176.9 2.9 %pad_maximum_fusion.1 = bf16[512,5504]{1,0:T(8,128)(2,1)S(1)} fusion(bf16[128,5504]{1,0:T(8,128)(2,1)S(1)} %copy-done.15, bf16[128,5504]{1,0:T(8,128)(2,1)S(1)} %copy-done.11, bf16[128,5504]{1,0:T(8,128)(2,1)S(1)} %copy-done.13, bf16[128,5504]{1,0:T(8,128)(2,1)} %fusion.8), kind=kLoop, calls=%fused_computation.6 | loop fusion | flops 22544384 | bytes 11272192 | tf_op jit(solution)/shard_map/concatenate | solution.py:157
  179.9 3.9 %fusion.1 = bf16[5504,256]{1,0:T(8,128)(2,1)S(1)} fusion(bf16[5504,512]{1,0:T(8,128)(2,1)} %collective-permute-done.17, bf16[128,1024]{1,0:T(8,128)(2,1)S(1)} %copy-done.27, bf16[128,1024]{1,0:T(8,128)(2,1)S(1)} %copy-done.24, bf16[128,1024]{1,0:T(8,128)(2,1)S(1)} %collective-permute-done.3, bf16[128,1024]{1,0:T(8,128)(2,1)S(1)} %bitcast.16, ...), kind=kOutput, calls=%fused_computation.4 | convolution fusion | flops 1470660608 | bytes 12320768 | tf_op jit(solution)/shard_map/dot_general | solution.py:161
  183.8 1.6 collective-permute-start.26
  185.4 5.4 %fusion.2 = f32[512,1024]{1,0:T(8,128)S(1)} fusion(bf16[512,5504]{1,0:T(8,128)(2,1)S(1)} %pad_maximum_fusion.1, bf16[2816,512]{1,0:T(8,128)(2,1)} %collective-permute-done.10, bf16[2816,256]{1,0:T(8,128)(2,1)} %collective-permute-done.6, bf16[2816,256]{1,0:T(8,128)(2,1)S(1)} %copy-done.4), kind=kOutput, calls=%fused_computation.13 | convolution fusion | flops 2970091520 | bytes 10747904 | tf_op jit(solution)/shard_map/dot_general | solution.py:172
  190.8 10.9 %collective-permute-done.21 = bf16[128,2688]{1,0:T(8,128)(2,1)S(1)} collective-permute-done((bf16[128,2688]{1,0:T(8,128)(2,1)S(1)}, bf16[128,2688]{1,0:T(8,128)(2,1)S(1)}, u32[]{:S(2)}, u32[]{:S(2)}) %collective-permute-start.21) | collective-permute-done | bytes 688160 | tf_op jit(solution)/shard_map/ppermute | solution.py:40
  201.7 5.1 %add_convert_fusion = bf16[512,1024]{1,0:T(8,128)(2,1)S(1)} fusion(f32[512,1024]{1,0:T(8,128)S(1)} %fusion.2, bf16[2688,512]{1,0:T(8,128)(2,1)} %copy-done.28, bf16[2688,256]{1,0:T(8,128)(2,1)S(1)} %copy-done.20, bf16[2688,256]{1,0:T(8,128)(2,1)S(1)} %copy-done.17, bf16[512,5504]{1,0:T(8,128)(2,1)S(1)} %pad_maximum_fusion.1), kind=kOutput, calls=%fused_computation.26 | convolution fusion | flops 2836135936 | bytes 11403264 | tf_op jit(solution)/shard_map/dot_general | solution.py:172
  207.4 2.1 collective-permute-start.27
  209.4 4.0 %collective-permute-start.28 = (bf16[128,2688]{1,0:T(8,128)(2,1)S(1)}, bf16[128,2688]{1,0:T(8,128)(2,1)S(1)}, u32[]{:S(2)}, u32[]{:S(2)}) collective-permute-start(bf16[128,2688]{1,0:T(8,128)(2,1)S(1)} %get-tuple-element.65), channel_id=1, source_target_pairs={{24,16},{26,18},{28,20},{30,22},{16,8},{18,10},{20,12},{22,14},{8,... | collective-permute-start | bytes 2064392 | tf_op jit(solution)/shard_map/ppermute | solution.py:40
  213.5 2.8 %collective-permute-done.22 = bf16[128,1024]{1,0:T(8,128)(2,1)S(1)} collective-permute-done((bf16[128,1024]{1,0:T(8,128)(2,1)S(1)}, bf16[128,1024]{1,0:T(8,128)(2,1)S(1)}, u32[]{:S(2)}, u32[]{:S(2)}) %collective-permute-start.22) | collective-permute-done | bytes 262176 | tf_op jit(solution)/shard_map/ppermute | solution.py:36
  217.2 27.0 %collective-permute-done.23 = bf16[128,1024]{1,0:T(8,128)(2,1)S(1)} collective-permute-done((bf16[128,1024]{1,0:T(8,128)(2,1)S(1)}, bf16[128,1024]{1,0:T(8,128)(2,1)S(1)}, u32[]{:S(2)}, u32[]{:S(2)}) %collective-permute-start.23) | collective-permute-done | bytes 262176 | tf_op jit(solution)/shard_map/ppermute | solution.py:36
  247.0 1.7 pad_maximum_fusion.11
  248.8 6.0 %fusion = f32[5504,256]{1,0:T(8,128)} fusion(bf16[512,5504]{1,0:T(8,128)(2,1)S(1)} %pad_maximum_fusion.1, bf16[5504,256]{1,0:T(8,128)(2,1)S(1)} %collective-permute-done.26, bf16[5504,512]{1,0:T(8,128)(2,1)} %collective-permute-done.17, bf16[128,1024]{1,0:T(8,128)(2,1)S(1)} %copy-done.27, bf16[128,1024]{1,0:T(8,128)(2,1)S(1)} %copy-done.24, ...), kind=kOutput, calls=%fused_computation.3 | convolution fusion | flops 1449525248 | bytes 17956864 | tf_op jit(solution)/shard_map/dot_general | solution.py:161
  254.8 3.0 %collective-permute-done.25 = bf16[128,2048]{1,0:T(8,128)(2,1)S(1)} collective-permute-done((bf16[128,2048]{1,0:T(8,128)(2,1)S(1)}, bf16[128,2048]{1,0:T(8,128)(2,1)S(1)}, u32[]{:S(2)}, u32[]{:S(2)}) %collective-permute-start.25) | collective-permute-done | bytes 524320 | tf_op jit(solution)/shard_map/ppermute | solution.py:49
  (113 shorter events, 19.9 us)
Async XLA Ops:
  0.6 13.9 %collective-permute-start.2 = (bf16[128,2048]{1,0:T(8,128)(2,1)}, bf16[128,2048]{1,0:T(8,128)(2,1)S(1)}, u32[]{:S(2)}, u32[]{:S(2)}) collective-permute-start(bf16[128,2048]{1,0:T(8,128)(2,1)} %param.6), channel_id=1, source_target_pairs={{0,1},{1,0},{2,3},{3,2},{4,5},{5,4},{6,7},{7,6},{8,9},{9,8},{10,11... | collective-permute-start | bytes 1572872 | tf_op jit(solution)/shard_map/ppermute | solution.py:49
  5.9 8.7 %copy-start.21 = (bf16[128,2048]{1,0:T(8,128)(2,1)S(1)}, bf16[128,2048]{1,0:T(8,128)(2,1)}, u32[]{:S(2)}) copy-start(bf16[128,2048]{1,0:T(8,128)(2,1)} %param.6) | copy-start | bytes 1572868
  6.0 54.4 %copy-start.2 = (bf16[2816,256]{1,0:T(8,128)(2,1)}, bf16[2816,256]{1,0:T(8,128)(2,1)S(1)}, u32[]{:S(2)}) copy-start(bf16[2816,256]{1,0:T(8,128)(2,1)S(1)} %slice.77) | copy-start | bytes 4325380
  6.0 54.4 %collective-permute-start.6 = (bf16[2816,256]{1,0:T(8,128)(2,1)S(1)}, bf16[2816,256]{1,0:T(8,128)(2,1)}, u32[]{:S(2)}, u32[]{:S(2)}) collective-permute-start(bf16[2816,256]{1,0:T(8,128)(2,1)S(1)} %slice.77), channel_id=1, source_target_pairs={{0,4},{2,6},{4,0},{6,2},{8,12},{10,14},{12,8},{14,10},{16,20},{18,... | collective-permute-start | bytes 4325384 | tf_op jit(solution)/shard_map/ppermute | solution.py:32
  7.6 59.1 %collective-permute-start = (bf16[128,5504]{1,0:T(8,128)(2,1)}, bf16[128,5504]{1,0:T(8,128)(2,1)}, u32[]{:S(2)}, u32[]{:S(2)}) collective-permute-start(bf16[128,5504]{1,0:T(8,128)(2,1)} %fusion.8), channel_id=1, source_target_pairs={{24,16},{26,18},{28,20},{30,22},{16,8},{18,10},{20,12},{22,14},{8,... | collective-permute-start | bytes 4227080 | tf_op jit(solution)/shard_map/ppermute | solution.py:40
  10.0 56.8 %collective-permute-start.1 = (bf16[128,5504]{1,0:T(8,128)(2,1)}, bf16[128,5504]{1,0:T(8,128)(2,1)}, u32[]{:S(2)}, u32[]{:S(2)}) collective-permute-start(bf16[128,5504]{1,0:T(8,128)(2,1)} %fusion.8), channel_id=1, source_target_pairs={{0,8},{2,10},{4,12},{6,14},{8,16},{10,18},{12,20},{14,22},{16,24},... | collective-permute-start | bytes 4227080 | tf_op jit(solution)/shard_map/ppermute | solution.py:40
  22.8 37.5 %collective-permute-start.3 = (bf16[128,1024]{1,0:T(8,128)(2,1)S(1)}, bf16[128,1024]{1,0:T(8,128)(2,1)S(1)}, u32[]{:S(2)}, u32[]{:S(2)}) collective-permute-start(bf16[128,1024]{1,0:T(8,128)(2,1)S(1)} %bitcast.20), channel_id=1, source_target_pairs={{0,24},{2,26},{4,28},{6,30},{8,0},{10,2},{12,4},{14,6},{16,8},{18,... | collective-permute-start | bytes 786440 | tf_op jit(solution)/shard_map/ppermute | solution.py:36
  23.5 40.1 %collective-permute-start.4 = (bf16[128,1024]{1,0:T(8,128)(2,1)S(1)}, bf16[128,1024]{1,0:T(8,128)(2,1)S(1)}, u32[]{:S(2)}, u32[]{:S(2)}) collective-permute-start(bf16[128,1024]{1,0:T(8,128)(2,1)S(1)} %bitcast.19), channel_id=1, source_target_pairs={{0,16},{2,18},{4,20},{6,22},{8,24},{10,26},{12,28},{14,30},{16,0},... | collective-permute-start | bytes 786440 | tf_op jit(solution)/shard_map/ppermute | solution.py:36
  60.4 6.4 %collective-permute-start.5 = (bf16[128,1024]{1,0:T(8,128)(2,1)S(1)}, bf16[128,1024]{1,0:T(8,128)(2,1)S(1)}, u32[]{:S(2)}, u32[]{:S(2)}) collective-permute-start(bf16[128,1024]{1,0:T(8,128)(2,1)S(1)} %bitcast.18), channel_id=1, source_target_pairs={{0,8},{2,10},{4,12},{6,14},{8,16},{10,18},{12,20},{14,22},{16,24},... | collective-permute-start | bytes 786440 | tf_op jit(solution)/shard_map/ppermute | solution.py:36
  63.5 10.8 %copy-start.22 = (bf16[128,1024]{1,0:T(8,128)(2,1)}, bf16[128,1024]{1,0:T(8,128)(2,1)S(1)}, u32[]{:S(2)}) copy-start(bf16[128,1024]{1,0:T(8,128)(2,1)S(1)} %collective-permute-done.4) | copy-start | bytes 786436
  66.7 7.6 %copy-start.25 = (bf16[128,1024]{1,0:T(8,128)(2,1)}, bf16[128,1024]{1,0:T(8,128)(2,1)S(1)}, u32[]{:S(2)}) copy-start(bf16[128,1024]{1,0:T(8,128)(2,1)S(1)} %collective-permute-done.5) | copy-start | bytes 786436
  66.8 7.6 %collective-permute-start.10 = (bf16[2816,512]{1,0:T(8,128)(2,1)}, bf16[2816,512]{1,0:T(8,128)(2,1)}, u32[]{:S(2)}, u32[]{:S(2)}) collective-permute-start(bf16[2816,512]{1,0:T(8,128)(2,1)} %pad_maximum_fusion.3), channel_id=1, source_target_pairs={{0,2},{2,0},{4,6},{6,4},{8,10},{10,8},{12,14},{14,12},{16,18},{18,... | collective-permute-start | bytes 8650760 | tf_op jit(solution)/shard_map/ppermute | solution.py:32
  68.4 50.9 %copy-start.16 = (bf16[2688,256]{1,0:T(8,128)(2,1)}, bf16[2688,256]{1,0:T(8,128)(2,1)S(1)}, u32[]{:S(2)}) copy-start(bf16[2688,256]{1,0:T(8,128)(2,1)S(1)} %slice.78) | copy-start | bytes 4128772
  68.5 32.6 %collective-permute-start.9 = (bf16[2688,256]{1,0:T(8,128)(2,1)S(1)}, bf16[2688,256]{1,0:T(8,128)(2,1)S(1)}, u32[]{:S(2)}, u32[]{:S(2)}) collective-permute-start(bf16[2688,256]{1,0:T(8,128)(2,1)S(1)} %slice.78), channel_id=1, source_target_pairs={{0,4},{2,6},{4,0},{6,2},{8,12},{10,14},{12,8},{14,10},{16,20},{18,... | collective-permute-start | bytes 4128776 | tf_op jit(solution)/shard_map/ppermute | solution.py:32
  69.1 33.9 %collective-permute-start.8 = (bf16[128,5504]{1,0:T(8,128)(2,1)}, bf16[128,5504]{1,0:T(8,128)(2,1)S(1)}, u32[]{:S(2)}, u32[]{:S(2)}) collective-permute-start(bf16[128,5504]{1,0:T(8,128)(2,1)} %collective-permute-done.1), channel_id=1, source_target_pairs={{8,16},{10,18},{12,20},{14,22},{16,24},{18,26},{20,28},{22,30},{9,... | collective-permute-start | bytes 4227080 | tf_op jit(solution)/shard_map/ppermute | solution.py:40
  72.2 34.8 %collective-permute-start.7 = (bf16[128,5504]{1,0:T(8,128)(2,1)}, bf16[128,5504]{1,0:T(8,128)(2,1)S(1)}, u32[]{:S(2)}, u32[]{:S(2)}) collective-permute-start(bf16[128,5504]{1,0:T(8,128)(2,1)} %collective-permute-done), channel_id=1, source_target_pairs={{16,8},{18,10},{20,12},{22,14},{8,0},{10,2},{12,4},{14,6},{17,9},{... | collective-permute-start | bytes 4227080 | tf_op jit(solution)/shard_map/ppermute | solution.py:40
  80.0 27.0 %collective-permute-start.11 = (bf16[128,2816]{1,0:T(8,128)(2,1)S(1)}, bf16[128,2816]{1,0:T(8,128)(2,1)S(1)}, u32[]{:S(2)}, u32[]{:S(2)}) collective-permute-start(bf16[128,2816]{1,0:T(8,128)(2,1)S(1)} %broadcast_select_fusion.4), channel_id=1, source_target_pairs={{0,8},{2,10},{4,12},{6,14},{24,16},{26,18},{28,20},{30,22},{1,9},{... | collective-permute-start | bytes 2162696 | tf_op jit(solution)/shard_map/ppermute | solution.py:40
  101.1 18.2 %copy-start.19 = (bf16[2688,256]{1,0:T(8,128)(2,1)}, bf16[2688,256]{1,0:T(8,128)(2,1)S(1)}, u32[]{:S(2)}) copy-start(bf16[2688,256]{1,0:T(8,128)(2,1)S(1)} %collective-permute-done.9) | copy-start | bytes 4128772
  107.0 6.5 %collective-permute-start.13 = (bf16[2688,512]{1,0:T(8,128)(2,1)S(1)}, bf16[2688,512]{1,0:T(8,128)(2,1)S(1)}, u32[]{:S(2)}, u32[]{:S(2)}) collective-permute-start(bf16[2688,512]{1,0:T(8,128)(2,1)S(1)} %pad_maximum_fusion.4), channel_id=1, source_target_pairs={{0,2},{2,0},{4,6},{6,4},{8,10},{10,8},{12,14},{14,12},{16,18},{18,... | collective-permute-start | bytes 8257544 | tf_op jit(solution)/shard_map/ppermute | solution.py:32
  108.6 10.8 %copy-start.23 = (bf16[128,1024]{1,0:T(8,128)(2,1)S(1)}, bf16[128,1024]{1,0:T(8,128)(2,1)}, u32[]{:S(2)}) copy-start(bf16[128,1024]{1,0:T(8,128)(2,1)} %copy-done.22) | copy-start | bytes 786436
  108.6 10.8 %copy-start.26 = (bf16[128,1024]{1,0:T(8,128)(2,1)S(1)}, bf16[128,1024]{1,0:T(8,128)(2,1)}, u32[]{:S(2)}) copy-start(bf16[128,1024]{1,0:T(8,128)(2,1)} %copy-done.25) | copy-start | bytes 786436
  108.6 33.2 %collective-permute-start.12 = (bf16[128,5504]{1,0:T(8,128)(2,1)}, bf16[128,5504]{1,0:T(8,128)(2,1)}, u32[]{:S(2)}, u32[]{:S(2)}) collective-permute-start(bf16[128,5504]{1,0:T(8,128)(2,1)} %broadcast_select_fusion.3), channel_id=1, source_target_pairs={{16,24},{18,26},{20,28},{22,30},{8,0},{10,2},{12,4},{14,6},{17,25}... | collective-permute-start | bytes 4227080 | tf_op jit(solution)/shard_map/ppermute | solution.py:40
  113.5 9.1 %copy-start.28 = (bf16[2688,512]{1,0:T(8,128)(2,1)}, bf16[2688,512]{1,0:T(8,128)(2,1)S(1)}, u32[]{:S(2)}) copy-start(bf16[2688,512]{1,0:T(8,128)(2,1)S(1)} %collective-permute-done.13) | copy-start | bytes 8257540
  113.5 36.2 %collective-permute-start.15 = (bf16[128,2816]{1,0:T(8,128)(2,1)}, bf16[128,2816]{1,0:T(8,128)(2,1)}, u32[]{:S(2)}, u32[]{:S(2)}) collective-permute-start(bf16[128,2816]{1,0:T(8,128)(2,1)} %get-tuple-element.45), channel_id=1, source_target_pairs={{24,16},{26,18},{28,20},{30,22},{16,8},{18,10},{20,12},{22,14},{25... | collective-permute-start | bytes 2162696 | tf_op jit(solution)/shard_map/ppermute | solution.py:40
  114.8 34.9 %collective-permute-start.14 = (bf16[128,2816]{1,0:T(8,128)(2,1)}, bf16[128,2816]{1,0:T(8,128)(2,1)}, u32[]{:S(2)}, u32[]{:S(2)}) collective-permute-start(bf16[128,2816]{1,0:T(8,128)(2,1)} %get-tuple-element.44), channel_id=1, source_target_pairs={{0,8},{2,10},{4,12},{6,14},{8,16},{10,18},{12,20},{14,22},{1,9},{3... | collective-permute-start | bytes 2162696 | tf_op jit(solution)/shard_map/ppermute | solution.py:40
  125.0 24.7 %collective-permute-start.16 = (bf16[128,2688]{1,0:T(8,128)(2,1)}, bf16[128,2688]{1,0:T(8,128)(2,1)}, u32[]{:S(2)}, u32[]{:S(2)}) collective-permute-start(bf16[128,2688]{1,0:T(8,128)(2,1)} %broadcast_select_fusion.5), channel_id=1, source_target_pairs={{0,8},{2,10},{4,12},{6,14},{24,16},{26,18},{28,20},{30,22},{1,9},{... | collective-permute-start | bytes 2064392 | tf_op jit(solution)/shard_map/ppermute | solution.py:40
  126.3 23.4 %copy-start.8 = (bf16[128,5504]{1,0:T(8,128)(2,1)S(1)}, bf16[128,5504]{1,0:T(8,128)(2,1)}, u32[]{:S(2)}) copy-start(bf16[128,5504]{1,0:T(8,128)(2,1)} %copy-done.7) | copy-start | bytes 4227076
  161.1 18.7 %collective-permute-start.17 = (bf16[5504,512]{1,0:T(8,128)(2,1)}, bf16[5504,512]{1,0:T(8,128)(2,1)}, u32[]{:S(2)}, u32[]{:S(2)}) collective-permute-start(bf16[5504,512]{1,0:T(8,128)(2,1)} %convolution_convert_fusion), channel_id=1, source_target_pairs={{0,2},{2,0},{4,6},{6,4},{8,10},{10,8},{12,14},{14,12},{16,18},{18,... | collective-permute-start | bytes 16908296 | tf_op jit(solution)/shard_map/ppermute | solution.py:32
  162.9 14.0 %copy-start.11 = (bf16[128,5504]{1,0:T(8,128)(2,1)S(1)}, bf16[128,5504]{1,0:T(8,128)(2,1)}, u32[]{:S(2)}) copy-start(bf16[128,5504]{1,0:T(8,128)(2,1)} %copy-done.10) | copy-start | bytes 4227076
  162.9 14.0 %copy-start.13 = (bf16[128,5504]{1,0:T(8,128)(2,1)S(1)}, bf16[128,5504]{1,0:T(8,128)(2,1)}, u32[]{:S(2)}) copy-start(bf16[128,5504]{1,0:T(8,128)(2,1)} %copy-done.12) | copy-start | bytes 4227076
  162.9 14.0 %copy-start.15 = (bf16[128,5504]{1,0:T(8,128)(2,1)S(1)}, bf16[128,5504]{1,0:T(8,128)(2,1)}, u32[]{:S(2)}) copy-start(bf16[128,5504]{1,0:T(8,128)(2,1)} %copy-done.14) | copy-start | bytes 4227076
  164.7 42.1 %collective-permute-start.18 = (bf16[128,2816]{1,0:T(8,128)(2,1)S(1)}, bf16[128,2816]{1,0:T(8,128)(2,1)S(1)}, u32[]{:S(2)}, u32[]{:S(2)}) collective-permute-start(bf16[128,2816]{1,0:T(8,128)(2,1)S(1)} %get-tuple-element.75), channel_id=1, source_target_pairs={{0,8},{2,10},{4,12},{6,14},{8,16},{10,18},{12,20},{14,22},{16,24},... | collective-permute-start | bytes 2162696 | tf_op jit(solution)/shard_map/ppermute | solution.py:40
  166.6 40.2 %collective-permute-start.19 = (bf16[128,2816]{1,0:T(8,128)(2,1)S(1)}, bf16[128,2816]{1,0:T(8,128)(2,1)S(1)}, u32[]{:S(2)}, u32[]{:S(2)}) collective-permute-start(bf16[128,2816]{1,0:T(8,128)(2,1)S(1)} %get-tuple-element.74), channel_id=1, source_target_pairs={{24,16},{26,18},{28,20},{30,22},{16,8},{18,10},{20,12},{22,14},{8,... | collective-permute-start | bytes 2162696 | tf_op jit(solution)/shard_map/ppermute | solution.py:40
  170.6 31.1 %collective-permute-start.21 = (bf16[128,2688]{1,0:T(8,128)(2,1)S(1)}, bf16[128,2688]{1,0:T(8,128)(2,1)S(1)}, u32[]{:S(2)}, u32[]{:S(2)}) collective-permute-start(bf16[128,2688]{1,0:T(8,128)(2,1)S(1)} %get-tuple-element.55), channel_id=1, source_target_pairs={{24,16},{26,18},{28,20},{30,22},{16,8},{18,10},{20,12},{22,14},{25... | collective-permute-start | bytes 2064392 | tf_op jit(solution)/shard_map/ppermute | solution.py:40
  171.9 7.9 %copy-start.24 = (bf16[128,1024]{1,0:T(8,128)(2,1)S(1)}, bf16[128,1024]{1,0:T(8,128)(2,1)}, u32[]{:S(2)}) copy-start(bf16[128,1024]{1,0:T(8,128)(2,1)} %copy-done.22) | copy-start | bytes 786436
  171.9 7.9 %copy-start.27 = (bf16[128,1024]{1,0:T(8,128)(2,1)S(1)}, bf16[128,1024]{1,0:T(8,128)(2,1)}, u32[]{:S(2)}) copy-start(bf16[128,1024]{1,0:T(8,128)(2,1)} %copy-done.25) | copy-start | bytes 786436
  171.9 29.7 %collective-permute-start.20 = (bf16[128,2688]{1,0:T(8,128)(2,1)S(1)}, bf16[128,2688]{1,0:T(8,128)(2,1)S(1)}, u32[]{:S(2)}, u32[]{:S(2)}) collective-permute-start(bf16[128,2688]{1,0:T(8,128)(2,1)S(1)} %get-tuple-element.54), channel_id=1, source_target_pairs={{0,8},{2,10},{4,12},{6,14},{8,16},{10,18},{12,20},{14,22},{1,9},{3... | collective-permute-start | bytes 2064392 | tf_op jit(solution)/shard_map/ppermute | solution.py:40
  183.8 17.9 %copy-start.17 = (bf16[2688,256]{1,0:T(8,128)(2,1)S(1)}, bf16[2688,256]{1,0:T(8,128)(2,1)}, u32[]{:S(2)}) copy-start(bf16[2688,256]{1,0:T(8,128)(2,1)} %copy-done.16) | copy-start | bytes 4128772
  183.8 17.9 %copy-start.20 = (bf16[2688,256]{1,0:T(8,128)(2,1)S(1)}, bf16[2688,256]{1,0:T(8,128)(2,1)}, u32[]{:S(2)}) copy-start(bf16[2688,256]{1,0:T(8,128)(2,1)} %copy-done.19) | copy-start | bytes 4128772
  183.8 65.0 %collective-permute-start.26 = (bf16[5504,256]{1,0:T(8,128)(2,1)S(1)}, bf16[5504,256]{1,0:T(8,128)(2,1)S(1)}, u32[]{:S(2)}, u32[]{:S(2)}) collective-permute-start(bf16[5504,256]{1,0:T(8,128)(2,1)S(1)} %fusion.1), channel_id=1, source_target_pairs={{0,4},{2,6},{4,0},{6,2},{8,12},{10,14},{12,8},{14,10},{16,20},{18,... | collective-permute-start | bytes 8454152 | tf_op jit(solution)/shard_map/ppermute | solution.py:32
  206.9 9.3 %copy-start.5 = (bf16[128,5504]{1,0:T(8,128)(2,1)S(1)}, bf16[128,5504]{1,0:T(8,128)(2,1)}, u32[]{:S(2)}) copy-start(bf16[128,5504]{1,0:T(8,128)(2,1)} %param.5) | copy-start | bytes 4227076
  206.9 9.3 %copy-start.6 = (bf16[128,5504]{1,0:T(8,128)(2,1)S(1)}, bf16[128,5504]{1,0:T(8,128)(2,1)}, u32[]{:S(2)}) copy-start(bf16[128,5504]{1,0:T(8,128)(2,1)} %param.4) | copy-start | bytes 4227076
  207.0 9.3 %collective-permute-start.22 = (bf16[128,1024]{1,0:T(8,128)(2,1)S(1)}, bf16[128,1024]{1,0:T(8,128)(2,1)S(1)}, u32[]{:S(2)}, u32[]{:S(2)}) collective-permute-start(bf16[128,1024]{1,0:T(8,128)(2,1)S(1)} %get-tuple-element.87), channel_id=1, source_target_pairs={{0,8},{2,10},{4,12},{6,14},{8,16},{10,18},{12,20},{14,22},{16,24},... | collective-permute-start | bytes 786440 | tf_op jit(solution)/shard_map/ppermute | solution.py:36
  207.4 38.7 %collective-permute-start.27 = (bf16[128,2688]{1,0:T(8,128)(2,1)S(1)}, bf16[128,2688]{1,0:T(8,128)(2,1)S(1)}, u32[]{:S(2)}, u32[]{:S(2)}) collective-permute-start(bf16[128,2688]{1,0:T(8,128)(2,1)S(1)} %get-tuple-element.63), channel_id=1, source_target_pairs={{0,8},{2,10},{4,12},{6,14},{8,16},{10,18},{12,20},{14,22},{16,24},... | collective-permute-start | bytes 2064392 | tf_op jit(solution)/shard_map/ppermute | solution.py:40
  209.4 36.7 %collective-permute-start.28 = (bf16[128,2688]{1,0:T(8,128)(2,1)S(1)}, bf16[128,2688]{1,0:T(8,128)(2,1)S(1)}, u32[]{:S(2)}, u32[]{:S(2)}) collective-permute-start(bf16[128,2688]{1,0:T(8,128)(2,1)S(1)} %get-tuple-element.65), channel_id=1, source_target_pairs={{24,16},{26,18},{28,20},{30,22},{16,8},{18,10},{20,12},{22,14},{8,... | collective-permute-start | bytes 2064392 | tf_op jit(solution)/shard_map/ppermute | solution.py:40
  213.4 30.8 %collective-permute-start.23 = (bf16[128,1024]{1,0:T(8,128)(2,1)S(1)}, bf16[128,1024]{1,0:T(8,128)(2,1)S(1)}, u32[]{:S(2)}, u32[]{:S(2)}) collective-permute-start(bf16[128,1024]{1,0:T(8,128)(2,1)S(1)} %get-tuple-element.86), channel_id=1, source_target_pairs={{0,16},{2,18},{4,20},{6,22},{8,24},{10,26},{12,28},{14,30},{16,0},... | collective-permute-start | bytes 786440 | tf_op jit(solution)/shard_map/ppermute | solution.py:36
  216.2 28.9 %collective-permute-start.24 = (bf16[128,1024]{1,0:T(8,128)(2,1)S(1)}, bf16[128,1024]{1,0:T(8,128)(2,1)S(1)}, u32[]{:S(2)}, u32[]{:S(2)}) collective-permute-start(bf16[128,1024]{1,0:T(8,128)(2,1)S(1)} %get-tuple-element.57), channel_id=1, source_target_pairs={{0,24},{2,26},{4,28},{6,30},{8,0},{10,2},{12,4},{14,6},{16,8},{18,... | collective-permute-start | bytes 786440 | tf_op jit(solution)/shard_map/ppermute | solution.py:36
  245.3 12.5 %collective-permute-start.25 = (bf16[128,2048]{1,0:T(8,128)(2,1)S(1)}, bf16[128,2048]{1,0:T(8,128)(2,1)S(1)}, u32[]{:S(2)}, u32[]{:S(2)}) collective-permute-start(bf16[128,2048]{1,0:T(8,128)(2,1)S(1)} %pad_maximum_fusion.17), channel_id=1, source_target_pairs={{0,1},{1,0},{2,3},{3,2},{4,5},{5,4},{6,7},{7,6},{8,9},{9,8},{10,11... | collective-permute-start | bytes 1572872 | tf_op jit(solution)/shard_map/ppermute | solution.py:49
  (10 other events, 48.8 us)

commit v3 on v2

--- a/solution.py
+++ b/solution.py
@@ -160,7 +160,7 @@
             part = cot_rows[:, lo * width : hi * width]
             return lax.dot_general(rows, part, SUM_ROWS, preferred_element_type=jnp.float32)
 
-        theirs = swap(grad_terms(2, 4).astype(jnp.bfloat16), 1)
+        theirs = swap(after(grad_terms(2, 4).astype(jnp.bfloat16), *travel[0]), 1)
         give = grad_terms(1, 2) + theirs[:, width:].astype(jnp.float32)
         give = give.astype(jnp.bfloat16)
         other_grad = swap(give, 2)

time: 263 us -> 258 us (0.981)
  waiting for transfers between devices: 130 us -> 120 us
  starting transfers between devices: 50.7 us -> 54.3 us
    ppermute x15, waiting for transfers between devices: 38.7 us -> 27.6 us  [far_permute(): return lax.ppermute(value, 'hst', pairs)]
    ppermute x6, waiting for transfers between devices: 19.8 us -> 25 us  [swap(): return lax.ppermute(value, 'hst', [(h, h ^ bit) for h in range(n_hst)])]
    ppermute x6, starting transfers between devices: 3.59 us -> 6.96 us  [shift(): return lax.ppermute(value, 'hst', pairs)]
    ppermute x2, waiting for transfers between devices: 3.88 us -> 0.84 us  [local_shift(): lax.ppermute(value, 'local', [(i, (i + step) % n_local) for i in range(n_...]
  transfers between devices with their start and end apart: 29 -> 29, of which waited for: 13 -> 15; matrix products, arithmetic and copies ran while one was open for 24% -> 29% of each run, Pallas kernels for 0% -> 0%
where the time goes in v3:
time: 258 us; the launch traced here: 256 us
  waiting for transfers between devices  120 us (47%)
  starting transfers between devices  54.3 us (21%)
  matrix products  37.8 us (15%)
  other arithmetic  29.6 us (11%)
  local copies, waits for them, and re-layouts  13.2 us (5%)
    ppermute x6, waiting for transfers between devices, shift(): return lax.ppermute(value, 'hst', pairs)  66.5 us
    ppermute x15, starting transfers between devices, far_permute(): return lax.ppermute(value, 'hst', pairs)  41.2 us
    ppermute x15, waiting for transfers between devices, far_permute(): return lax.ppermute(value, 'hst', pairs)  27.6 us
    ppermute x6, waiting for transfers between devices, swap(): return lax.ppermute(value, 'hst', [(h, h ^ bit) for h in range(n_hst)])  25 us
    dot_general x3, matrix products, grad_terms(): lax.dot_general(rows, part, SUM_ROWS, preferred_element_type=jnp.float32)  16.7 us
    dot_general x2, matrix products, reduce_terms(): lax.dot_general(cot_rows, weights[f], KEEP_COLS, preferred_element_type=j...  10.6 us
    dot_general x2, matrix products, on_device(): jnp.dot(rows[:, lo:hi], weights[f], preferred_element_type=jnp.float32)  10.5 us
    ppermute x6, starting transfers between devices, shift(): return lax.ppermute(value, 'hst', pairs)  6.96 us
  transfers between devices with their start and end apart: 29, of which 15 were waited for; matrix products, arithmetic and copies ran while one was open for 29% of the time, Pallas kernels for 0%

profile of v3, /device:TPU:8, one launch (start us, length us, event | category | flops | bytes accessed | tf_op | source)
XLA Modules:
  0.0 256.5 jit_solution(14523253142056506240)
XLA Ops:
  0.6 1.6 collective-permute-start.2
  2.2 3.7 %fusion.8 = bf16[128,5504]{1,0:T(8,128)(2,1)} fusion(bf16[128,5504]{1,0:T(8,128)(2,1)} %param.5, bf16[128,5504]{1,0:T(8,128)(2,1)} %param.4), kind=kLoop, calls=%fused_computation.19 | loop fusion | flops 5636096 | bytes 4227072 | tf_op jit(solution)/shard_map/convert_element_type | solution.py:69
  6.0 1.6 collective-permute-start.6
  7.6 2.3 collective-permute-start
  10.0 3.5 %collective-permute-start.1 = (bf16[128,5504]{1,0:T(8,128)(2,1)}, bf16[128,5504]{1,0:T(8,128)(2,1)}, u32[]{:S(2)}, u32[]{:S(2)}) collective-permute-start(bf16[128,5504]{1,0:T(8,128)(2,1)} %fusion.8), channel_id=1, source_target_pairs={{0,8},{2,10},{4,12},{6,14},{8,16},{10,18},{12,20},{14,22},{16,24},... | collective-permute-start | bytes 4227080 | tf_op jit(solution)/shard_map/ppermute | solution.py:40
  15.5 2.2 constant_dynamic-slice_fusion.15
  17.7 2.4 pad_maximum_fusion.14
  20.6 2.2 constant_dynamic-slice_fusion.8
  23.5 3.0 %collective-permute-start.4 = (bf16[128,1024]{1,0:T(8,128)(2,1)S(1)}, bf16[128,1024]{1,0:T(8,128)(2,1)S(1)}, u32[]{:S(2)}, u32[]{:S(2)}) collective-permute-start(bf16[128,1024]{1,0:T(8,128)(2,1)S(1)} %bitcast.19), channel_id=1, source_target_pairs={{0,16},{2,18},{4,20},{6,22},{8,24},{10,26},{12,28},{14,30},{16,0},... | collective-permute-start | bytes 786440 | tf_op jit(solution)/shard_map/ppermute | solution.py:36
  26.4 33.9 %collective-permute-done.3 = bf16[128,1024]{1,0:T(8,128)(2,1)S(1)} collective-permute-done((bf16[128,1024]{1,0:T(8,128)(2,1)S(1)}, bf16[128,1024]{1,0:T(8,128)(2,1)S(1)}, u32[]{:S(2)}, u32[]{:S(2)}) %collective-permute-start.3) | collective-permute-done | bytes 262176 | tf_op jit(solution)/shard_map/ppermute | solution.py:36
  60.4 3.1 %pad_maximum_fusion.3 = bf16[2816,512]{1,0:T(8,128)(2,1)} fusion(bf16[2816,256]{1,0:T(8,128)(2,1)} %collective-permute-done.6, bf16[2816,256]{1,0:T(8,128)(2,1)S(1)} %slice.77), kind=kLoop, calls=%fused_computation.12 | loop fusion | flops 5767168 | bytes 5767168 | tf_op jit(solution)/shard_map/concatenate | solution.py:104
  63.5 3.2 %collective-permute-done.5 = bf16[128,1024]{1,0:T(8,128)(2,1)S(1)} collective-permute-done((bf16[128,1024]{1,0:T(8,128)(2,1)S(1)}, bf16[128,1024]{1,0:T(8,128)(2,1)S(1)}, u32[]{:S(2)}, u32[]{:S(2)}) %collective-permute-start.5) | collective-permute-done | bytes 262176 | tf_op jit(solution)/shard_map/ppermute | solution.py:36
  66.8 1.5 slice.78
  69.1 4.2 %collective-permute-start.8 = (bf16[128,5504]{1,0:T(8,128)(2,1)}, bf16[128,5504]{1,0:T(8,128)(2,1)}, u32[]{:S(2)}, u32[]{:S(2)}) collective-permute-start(bf16[128,5504]{1,0:T(8,128)(2,1)} %collective-permute-done.1), channel_id=1, source_target_pairs={{8,16},{10,18},{12,20},{14,22},{16,24},{18,26},{20,28},{22,30},{9,... | collective-permute-start | bytes 4227080 | tf_op jit(solution)/shard_map/ppermute | solution.py:40
  73.3 2.1 collective-permute-start.7
  75.4 5.6 %convolution_convert_fusion.2 = bf16[512,2816]{1,0:T(8,128)(2,1)S(1)} fusion(bf16[2816,512]{1,0:T(8,128)(2,1)} %collective-permute-done.10, bf16[2816,256]{1,0:T(8,128)(2,1)} %collective-permute-done.6, bf16[2816,256]{1,0:T(8,128)(2,1)S(1)} %copy-done.3, bf16[128,1024]{1,0:T(8,128)(2,1)} %copy-done.31, bf16[128,1024]{1,0:T(8,128)(2,1)} %copy-done.28, ...), kind=kOutput, calls=%fused_computation.9 | convolution fusion | flops 2975727616 | bytes 9699328 | tf_op jit(solution)/shard_map/dot_general | solution.py:109
  82.4 18.7 %collective-permute-done.9 = bf16[2688,256]{1,0:T(8,128)(2,1)S(1)} collective-permute-done((bf16[2688,256]{1,0:T(8,128)(2,1)S(1)}, bf16[2688,256]{1,0:T(8,128)(2,1)S(1)}, u32[]{:S(2)}, u32[]{:S(2)}) %collective-permute-start.9) | collective-permute-done | bytes 1376288 | tf_op jit(solution)/shard_map/ppermute | solution.py:32
  101.1 1.9 pad_maximum_fusion.4
  103.2 5.0 %collective-permute-done.7 = bf16[128,5504]{1,0:T(8,128)(2,1)} collective-permute-done((bf16[128,5504]{1,0:T(8,128)(2,1)}, bf16[128,5504]{1,0:T(8,128)(2,1)}, u32[]{:S(2)}, u32[]{:S(2)}) %collective-permute-start.7) | collective-permute-done | bytes 1409056 | tf_op jit(solution)/shard_map/ppermute | solution.py:40
  110.2 1.6 broadcast_select_fusion.3
  111.8 2.5 collective-permute-start.12
  114.7 1.3 collective-permute-start.15
  116.0 4.6 %collective-permute-start.14 = (bf16[128,2816]{1,0:T(8,128)(2,1)S(1)}, bf16[128,2816]{1,0:T(8,128)(2,1)S(1)}, u32[]{:S(2)}, u32[]{:S(2)}) collective-permute-start(bf16[128,2816]{1,0:T(8,128)(2,1)S(1)} %get-tuple-element.45), channel_id=1, source_target_pairs={{0,8},{2,10},{4,12},{6,14},{8,16},{10,18},{12,20},{14,22},{1,9},{3... | collective-permute-start | bytes 2162696 | tf_op jit(solution)/shard_map/ppermute | solution.py:40
  120.6 5.0 %convolution_convert_fusion.1 = bf16[512,2688]{1,0:T(8,128)(2,1)S(1)} fusion(bf16[2688,512]{1,0:T(8,128)(2,1)} %collective-permute-done.13, bf16[2688,256]{1,0:T(8,128)(2,1)S(1)} %copy-done.18, bf16[2688,256]{1,0:T(8,128)(2,1)S(1)} %copy-done.14, bf16[128,1024]{1,0:T(8,128)(2,1)S(1)} %copy-done.32, bf16[128,1024]{1,0:T(8,128)(2,1)S(1)} %copy-done.29, ...), kind=kOutput, calls=%fused_computation.8 | convolution fusion | flops 2840657920 | bytes 9306112 | tf_op jit(solution)/shard_map/dot_general | solution.py:109
  127.0 7.9 %collective-permute-done.15 = bf16[128,2816]{1,0:T(8,128)(2,1)S(1)} collective-permute-done((bf16[128,2816]{1,0:T(8,128)(2,1)S(1)}, bf16[128,2816]{1,0:T(8,128)(2,1)S(1)}, u32[]{:S(2)}, u32[]{:S(2)}) %collective-permute-start.15) | collective-permute-done | bytes 720928 | tf_op jit(solution)/shard_map/ppermute | solution.py:40
  134.9 2.0 collective-permute-done.14
  137.3 3.6 %collective-permute-start.17 = (bf16[128,2816]{1,0:T(8,128)(2,1)S(1)}, bf16[128,2816]{1,0:T(8,128)(2,1)S(1)}, u32[]{:S(2)}, u32[]{:S(2)}) collective-permute-start(bf16[128,2816]{1,0:T(8,128)(2,1)S(1)} %get-tuple-element.77), channel_id=1, source_target_pairs={{0,8},{2,10},{4,12},{6,14},{8,16},{10,18},{12,20},{14,22},{16,24},... | collective-permute-start | bytes 2162696 | tf_op jit(solution)/shard_map/ppermute | solution.py:40
  140.9 2.3 collective-permute-start.18
  143.2 2.3 collective-permute-done.12
  145.4 6.2 %collective-permute-done.16 = bf16[128,2688]{1,0:T(8,128)(2,1)S(1)} collective-permute-done((bf16[128,2688]{1,0:T(8,128)(2,1)S(1)}, bf16[128,2688]{1,0:T(8,128)(2,1)S(1)}, u32[]{:S(2)}, u32[]{:S(2)}) %collective-permute-start.16) | collective-permute-done | bytes 688160 | tf_op jit(solution)/shard_map/ppermute | solution.py:40
  151.6 1.8 broadcast_select_fusion.1
  153.4 2.6 %broadcast_select_fusion.2 = (bf16[128,5504]{1,0:T(8,128)(2,1)S(1)}, bf16[128,5504]{1,0:T(8,128)(2,1)S(1)}) fusion(bf16[128,5504]{1,0:T(8,128)(2,1)} %collective-permute-done, bf16[128,5504]{1,0:T(8,128)(2,1)S(1)} %collective-permute-done.12, pred[]{:T(512)S(6)} %lt.161, bf16[128,5504]{1,0:T(8,128)(2,1)} %collective-permute-done.1, pred[]{:T(512)S(6)} %lt.163), kind=kLoop, calls=%fused_computation.51 | loop fusion | flops 1409024 | bytes 7045122 | tf_op jit(solution)/shard_map/jit(_where)/select_n | solution.py:156
  156.1 6.8 %convolution_convert_fusion = bf16[5504,512]{1,0:T(8,128)(2,1)} fusion(bf16[512,1024]{1,0:T(8,128)(2,1)S(1)} %pad_maximum_fusion.15, bf16[128,5504]{1,0:T(8,128)(2,1)S(1)} %get-tuple-element.81, bf16[128,5504]{1,0:T(8,128)(2,1)S(1)} %broadcast_select_fusion.1, bf16[128,5504]{1,0:T(8,128)(2,1)S(1)} %get-tuple-element.80, bf16[128,5504]{1,0:T(8,128)(2,1)} %fusion.8), kind=kOutput, calls=%fused_computation | convolution fusion | flops 2911043584 | bytes 11796480 | tf_op jit(solution)/shard_map/dot_general | solution.py:161
  162.9 3.5 %collective-permute-done.17 = bf16[128,2816]{1,0:T(8,128)(2,1)S(1)} collective-permute-done((bf16[128,2816]{1,0:T(8,128)(2,1)S(1)}, bf16[128,2816]{1,0:T(8,128)(2,1)S(1)}, u32[]{:S(2)}, u32[]{:S(2)}) %collective-permute-start.17) | collective-permute-done | bytes 720928 | tf_op jit(solution)/shard_map/ppermute | solution.py:40
  168.1 1.7 fusion.24
  171.2 5.0 %collective-permute-start.20 = (bf16[128,2688]{1,0:T(8,128)(2,1)S(1)}, bf16[128,2688]{1,0:T(8,128)(2,1)S(1)}, u32[]{:S(2)}, u32[]{:S(2)}) collective-permute-start(bf16[128,2688]{1,0:T(8,128)(2,1)S(1)} %get-tuple-element.56), channel_id=1, source_target_pairs={{0,8},{2,10},{4,12},{6,14},{8,16},{10,18},{12,20},{14,22},{1,9},{3... | collective-permute-start | bytes 2064392 | tf_op jit(solution)/shard_map/ppermute | solution.py:40
  176.2 3.2 %pad_maximum_fusion.1 = bf16[512,5504]{1,0:T(8,128)(2,1)S(1)} fusion(bf16[128,5504]{1,0:T(8,128)(2,1)} %copy-done.11, bf16[128,5504]{1,0:T(8,128)(2,1)S(1)} %copy-done.8, bf16[128,5504]{1,0:T(8,128)(2,1)} %copy-done.9, bf16[128,5504]{1,0:T(8,128)(2,1)} %fusion.8), kind=kLoop, calls=%fused_computation.6 | loop fusion | flops 22544384 | bytes 11272192 | tf_op jit(solution)/shard_map/concatenate | solution.py:157
  179.5 3.9 %fusion.1 = bf16[5504,256]{1,0:T(8,128)(2,1)S(1)} fusion(bf16[5504,512]{1,0:T(8,128)(2,1)} %collective-permute-done.19, bf16[128,1024]{1,0:T(8,128)(2,1)S(1)} %copy-done.33, bf16[128,1024]{1,0:T(8,128)(2,1)S(1)} %copy-done.30, bf16[128,1024]{1,0:T(8,128)(2,1)S(1)} %collective-permute-done.3, bf16[128,1024]{1,0:T(8,128)(2,1)S(1)} %bitcast.16, ...), kind=kOutput, calls=%fused_computation.4 | convolution fusion | flops 1470660608 | bytes 12320768 | tf_op jit(solution)/shard_map/dot_general | solution.py:161
  183.4 1.6 collective-permute-start.26
  185.0 5.4 %fusion.2 = f32[512,1024]{1,0:T(8,128)S(1)} fusion(bf16[512,5504]{1,0:T(8,128)(2,1)S(1)} %pad_maximum_fusion.1, bf16[2816,512]{1,0:T(8,128)(2,1)} %collective-permute-done.10, bf16[2816,256]{1,0:T(8,128)(2,1)} %collective-permute-done.6, bf16[2816,256]{1,0:T(8,128)(2,1)S(1)} %copy-done.4), kind=kOutput, calls=%fused_computation.13 | convolution fusion | flops 2970091520 | bytes 10747904 | tf_op jit(solution)/shard_map/dot_general | solution.py:172
  191.2 5.1 %add_convert_fusion = bf16[512,1024]{1,0:T(8,128)(2,1)S(1)} fusion(f32[512,1024]{1,0:T(8,128)S(1)} %fusion.2, bf16[2688,512]{1,0:T(8,128)(2,1)} %collective-permute-done.13, bf16[2688,256]{1,0:T(8,128)(2,1)S(1)} %copy-done.19, bf16[2688,256]{1,0:T(8,128)(2,1)S(1)} %copy-done.15, bf16[512,5504]{1,0:T(8,128)(2,1)S(1)} %pad_maximum_fusion.1), kind=kOutput, calls=%fused_computation.26 | convolution fusion | flops 2836135936 | bytes 11403264 | tf_op jit(solution)/shard_map/dot_general | solution.py:172
  196.5 2.4 collective-permute-start.22
  199.2 2.1 collective-permute-start.27
  201.3 3.8 %collective-permute-start.28 = (bf16[128,2688]{1,0:T(8,128)(2,1)S(1)}, bf16[128,2688]{1,0:T(8,128)(2,1)S(1)}, u32[]{:S(2)}, u32[]{:S(2)}) collective-permute-start(bf16[128,2688]{1,0:T(8,128)(2,1)S(1)} %get-tuple-element.67), channel_id=1, source_target_pairs={{24,16},{26,18},{28,20},{30,22},{16,8},{18,10},{20,12},{22,14},{8,... | collective-permute-start | bytes 2064392 | tf_op jit(solution)/shard_map/ppermute | solution.py:40
  207.7 27.9 %collective-permute-done.23 = bf16[128,1024]{1,0:T(8,128)(2,1)S(1)} collective-permute-done((bf16[128,1024]{1,0:T(8,128)(2,1)S(1)}, bf16[128,1024]{1,0:T(8,128)(2,1)S(1)}, u32[]{:S(2)}, u32[]{:S(2)}) %collective-permute-start.23) | collective-permute-done | bytes 262176 | tf_op jit(solution)/shard_map/ppermute | solution.py:36
  238.4 1.7 pad_maximum_fusion.11
  240.2 6.2 %collective-permute-done.26 = bf16[5504,256]{1,0:T(8,128)(2,1)S(1)} collective-permute-done((bf16[5504,256]{1,0:T(8,128)(2,1)S(1)}, bf16[5504,256]{1,0:T(8,128)(2,1)S(1)}, u32[]{:S(2)}, u32[]{:S(2)}) %collective-permute-start.26) | collective-permute-done | bytes 2818080 | tf_op jit(solution)/shard_map/ppermute | solution.py:32
  246.4 6.0 %fusion = f32[5504,256]{1,0:T(8,128)} fusion(bf16[512,5504]{1,0:T(8,128)(2,1)S(1)} %pad_maximum_fusion.1, bf16[5504,256]{1,0:T(8,128)(2,1)S(1)} %collective-permute-done.26, bf16[5504,512]{1,0:T(8,128)(2,1)} %collective-permute-done.19, bf16[128,1024]{1,0:T(8,128)(2,1)S(1)} %copy-done.33, bf16[128,1024]{1,0:T(8,128)(2,1)S(1)} %copy-done.30, ...), kind=kOutput, calls=%fused_computation.3 | convolution fusion | flops 1449525248 | bytes 17956864 | tf_op jit(solution)/shard_map/dot_general | solution.py:161
  (123 shorter events, 23.0 us)
Async XLA Ops:
  0.6 13.9 %collective-permute-start.2 = (bf16[128,2048]{1,0:T(8,128)(2,1)}, bf16[128,2048]{1,0:T(8,128)(2,1)S(1)}, u32[]{:S(2)}, u32[]{:S(2)}) collective-permute-start(bf16[128,2048]{1,0:T(8,128)(2,1)} %param.6), channel_id=1, source_target_pairs={{0,1},{1,0},{2,3},{3,2},{4,5},{5,4},{6,7},{7,6},{8,9},{9,8},{10,11... | collective-permute-start | bytes 1572872 | tf_op jit(solution)/shard_map/ppermute | solution.py:49
  5.9 8.7 %copy-start.27 = (bf16[128,2048]{1,0:T(8,128)(2,1)S(1)}, bf16[128,2048]{1,0:T(8,128)(2,1)}, u32[]{:S(2)}) copy-start(bf16[128,2048]{1,0:T(8,128)(2,1)} %param.6) | copy-start | bytes 1572868
  6.0 54.4 %copy-start.2 = (bf16[2816,256]{1,0:T(8,128)(2,1)}, bf16[2816,256]{1,0:T(8,128)(2,1)S(1)}, u32[]{:S(2)}) copy-start(bf16[2816,256]{1,0:T(8,128)(2,1)S(1)} %slice.77) | copy-start | bytes 4325380
  6.0 54.4 %collective-permute-start.6 = (bf16[2816,256]{1,0:T(8,128)(2,1)S(1)}, bf16[2816,256]{1,0:T(8,128)(2,1)}, u32[]{:S(2)}, u32[]{:S(2)}) collective-permute-start(bf16[2816,256]{1,0:T(8,128)(2,1)S(1)} %slice.77), channel_id=1, source_target_pairs={{0,4},{2,6},{4,0},{6,2},{8,12},{10,14},{12,8},{14,10},{16,20},{18,... | collective-permute-start | bytes 4325384 | tf_op jit(solution)/shard_map/ppermute | solution.py:32
  7.6 59.1 %collective-permute-start = (bf16[128,5504]{1,0:T(8,128)(2,1)}, bf16[128,5504]{1,0:T(8,128)(2,1)}, u32[]{:S(2)}, u32[]{:S(2)}) collective-permute-start(bf16[128,5504]{1,0:T(8,128)(2,1)} %fusion.8), channel_id=1, source_target_pairs={{24,16},{26,18},{28,20},{30,22},{16,8},{18,10},{20,12},{22,14},{8,... | collective-permute-start | bytes 4227080 | tf_op jit(solution)/shard_map/ppermute | solution.py:40
  10.0 56.8 %collective-permute-start.1 = (bf16[128,5504]{1,0:T(8,128)(2,1)}, bf16[128,5504]{1,0:T(8,128)(2,1)}, u32[]{:S(2)}, u32[]{:S(2)}) collective-permute-start(bf16[128,5504]{1,0:T(8,128)(2,1)} %fusion.8), channel_id=1, source_target_pairs={{0,8},{2,10},{4,12},{6,14},{8,16},{10,18},{12,20},{14,22},{16,24},... | collective-permute-start | bytes 4227080 | tf_op jit(solution)/shard_map/ppermute | solution.py:40
  22.8 37.5 %collective-permute-start.3 = (bf16[128,1024]{1,0:T(8,128)(2,1)S(1)}, bf16[128,1024]{1,0:T(8,128)(2,1)S(1)}, u32[]{:S(2)}, u32[]{:S(2)}) collective-permute-start(bf16[128,1024]{1,0:T(8,128)(2,1)S(1)} %bitcast.20), channel_id=1, source_target_pairs={{0,24},{2,26},{4,28},{6,30},{8,0},{10,2},{12,4},{14,6},{16,8},{18,... | collective-permute-start | bytes 786440 | tf_op jit(solution)/shard_map/ppermute | solution.py:36
  23.5 40.1 %collective-permute-start.4 = (bf16[128,1024]{1,0:T(8,128)(2,1)S(1)}, bf16[128,1024]{1,0:T(8,128)(2,1)S(1)}, u32[]{:S(2)}, u32[]{:S(2)}) collective-permute-start(bf16[128,1024]{1,0:T(8,128)(2,1)S(1)} %bitcast.19), channel_id=1, source_target_pairs={{0,16},{2,18},{4,20},{6,22},{8,24},{10,26},{12,28},{14,30},{16,0},... | collective-permute-start | bytes 786440 | tf_op jit(solution)/shard_map/ppermute | solution.py:36
  60.4 6.4 %collective-permute-start.5 = (bf16[128,1024]{1,0:T(8,128)(2,1)S(1)}, bf16[128,1024]{1,0:T(8,128)(2,1)S(1)}, u32[]{:S(2)}, u32[]{:S(2)}) collective-permute-start(bf16[128,1024]{1,0:T(8,128)(2,1)S(1)} %bitcast.18), channel_id=1, source_target_pairs={{0,8},{2,10},{4,12},{6,14},{8,16},{10,18},{12,20},{14,22},{16,24},... | collective-permute-start | bytes 786440 | tf_op jit(solution)/shard_map/ppermute | solution.py:36
  63.5 11.8 %copy-start.28 = (bf16[128,1024]{1,0:T(8,128)(2,1)}, bf16[128,1024]{1,0:T(8,128)(2,1)S(1)}, u32[]{:S(2)}) copy-start(bf16[128,1024]{1,0:T(8,128)(2,1)S(1)} %collective-permute-done.4) | copy-start | bytes 786436
  66.7 8.6 %copy-start.31 = (bf16[128,1024]{1,0:T(8,128)(2,1)}, bf16[128,1024]{1,0:T(8,128)(2,1)S(1)}, u32[]{:S(2)}) copy-start(bf16[128,1024]{1,0:T(8,128)(2,1)S(1)} %collective-permute-done.5) | copy-start | bytes 786436
  66.8 8.6 %collective-permute-start.10 = (bf16[2816,512]{1,0:T(8,128)(2,1)}, bf16[2816,512]{1,0:T(8,128)(2,1)}, u32[]{:S(2)}, u32[]{:S(2)}) collective-permute-start(bf16[2816,512]{1,0:T(8,128)(2,1)} %pad_maximum_fusion.3), channel_id=1, source_target_pairs={{0,2},{2,0},{4,6},{6,4},{8,10},{10,8},{12,14},{14,12},{16,18},{18,... | collective-permute-start | bytes 8650760 | tf_op jit(solution)/shard_map/ppermute | solution.py:32
  66.8 8.6 %copy-start.3 = (bf16[2816,256]{1,0:T(8,128)(2,1)S(1)}, bf16[2816,256]{1,0:T(8,128)(2,1)}, u32[]{:S(2)}) copy-start(bf16[2816,256]{1,0:T(8,128)(2,1)} %copy-done.2) | copy-start | bytes 4325380
  68.4 32.7 %copy-start.13 = (bf16[2688,256]{1,0:T(8,128)(2,1)}, bf16[2688,256]{1,0:T(8,128)(2,1)S(1)}, u32[]{:S(2)}) copy-start(bf16[2688,256]{1,0:T(8,128)(2,1)S(1)} %slice.78) | copy-start | bytes 4128772
  68.5 32.6 %collective-permute-start.9 = (bf16[2688,256]{1,0:T(8,128)(2,1)S(1)}, bf16[2688,256]{1,0:T(8,128)(2,1)S(1)}, u32[]{:S(2)}, u32[]{:S(2)}) collective-permute-start(bf16[2688,256]{1,0:T(8,128)(2,1)S(1)} %slice.78), channel_id=1, source_target_pairs={{0,4},{2,6},{4,0},{6,2},{8,12},{10,14},{12,8},{14,10},{16,20},{18,... | collective-permute-start | bytes 4128776 | tf_op jit(solution)/shard_map/ppermute | solution.py:32
  69.1 34.1 %collective-permute-start.8 = (bf16[128,5504]{1,0:T(8,128)(2,1)}, bf16[128,5504]{1,0:T(8,128)(2,1)}, u32[]{:S(2)}, u32[]{:S(2)}) collective-permute-start(bf16[128,5504]{1,0:T(8,128)(2,1)} %collective-permute-done.1), channel_id=1, source_target_pairs={{8,16},{10,18},{12,20},{14,22},{16,24},{18,26},{20,28},{22,30},{9,... | collective-permute-start | bytes 4227080 | tf_op jit(solution)/shard_map/ppermute | solution.py:40
  73.3 34.9 %collective-permute-start.7 = (bf16[128,5504]{1,0:T(8,128)(2,1)}, bf16[128,5504]{1,0:T(8,128)(2,1)}, u32[]{:S(2)}, u32[]{:S(2)}) collective-permute-start(bf16[128,5504]{1,0:T(8,128)(2,1)} %collective-permute-done), channel_id=1, source_target_pairs={{16,8},{18,10},{20,12},{22,14},{8,0},{10,2},{12,4},{14,6},{17,9},{... | collective-permute-start | bytes 4227080 | tf_op jit(solution)/shard_map/ppermute | solution.py:40
  81.1 27.1 %collective-permute-start.11 = (bf16[128,2816]{1,0:T(8,128)(2,1)S(1)}, bf16[128,2816]{1,0:T(8,128)(2,1)S(1)}, u32[]{:S(2)}, u32[]{:S(2)}) collective-permute-start(bf16[128,2816]{1,0:T(8,128)(2,1)S(1)} %broadcast_select_fusion.4), channel_id=1, source_target_pairs={{0,8},{2,10},{4,12},{6,14},{24,16},{26,18},{28,20},{30,22},{1,9},{... | collective-permute-start | bytes 2162696 | tf_op jit(solution)/shard_map/ppermute | solution.py:40
  109.0 5.7 %collective-permute-start.13 = (bf16[2688,512]{1,0:T(8,128)(2,1)}, bf16[2688,512]{1,0:T(8,128)(2,1)}, u32[]{:S(2)}, u32[]{:S(2)}) collective-permute-start(bf16[2688,512]{1,0:T(8,128)(2,1)} %pad_maximum_fusion.4), channel_id=1, source_target_pairs={{0,2},{2,0},{4,6},{6,4},{8,10},{10,8},{12,14},{14,12},{16,18},{18,... | collective-permute-start | bytes 8257544 | tf_op jit(solution)/shard_map/ppermute | solution.py:32
  110.1 10.4 %copy-start.29 = (bf16[128,1024]{1,0:T(8,128)(2,1)S(1)}, bf16[128,1024]{1,0:T(8,128)(2,1)}, u32[]{:S(2)}) copy-start(bf16[128,1024]{1,0:T(8,128)(2,1)} %copy-done.28) | copy-start | bytes 786436
  110.2 10.4 %copy-start.32 = (bf16[128,1024]{1,0:T(8,128)(2,1)S(1)}, bf16[128,1024]{1,0:T(8,128)(2,1)}, u32[]{:S(2)}) copy-start(bf16[128,1024]{1,0:T(8,128)(2,1)} %copy-done.31) | copy-start | bytes 786436
  111.8 8.8 %copy-start.14 = (bf16[2688,256]{1,0:T(8,128)(2,1)S(1)}, bf16[2688,256]{1,0:T(8,128)(2,1)}, u32[]{:S(2)}) copy-start(bf16[2688,256]{1,0:T(8,128)(2,1)} %copy-done.13) | copy-start | bytes 4128772
  111.8 8.8 %copy-start.18 = (bf16[2688,256]{1,0:T(8,128)(2,1)S(1)}, bf16[2688,256]{1,0:T(8,128)(2,1)}, u32[]{:S(2)}) copy-start(bf16[2688,256]{1,0:T(8,128)(2,1)} %copy-done.17) | copy-start | bytes 4128772
  111.8 33.6 %collective-permute-start.12 = (bf16[128,5504]{1,0:T(8,128)(2,1)S(1)}, bf16[128,5504]{1,0:T(8,128)(2,1)S(1)}, u32[]{:S(2)}, u32[]{:S(2)}) collective-permute-start(bf16[128,5504]{1,0:T(8,128)(2,1)S(1)} %broadcast_select_fusion.3), channel_id=1, source_target_pairs={{16,24},{18,26},{20,28},{22,30},{8,0},{10,2},{12,4},{14,6},{17,25}... | collective-permute-start | bytes 4227080 | tf_op jit(solution)/shard_map/ppermute | solution.py:40
  114.7 20.2 %collective-permute-start.15 = (bf16[128,2816]{1,0:T(8,128)(2,1)S(1)}, bf16[128,2816]{1,0:T(8,128)(2,1)S(1)}, u32[]{:S(2)}, u32[]{:S(2)}) collective-permute-start(bf16[128,2816]{1,0:T(8,128)(2,1)S(1)} %get-tuple-element.46), channel_id=1, source_target_pairs={{24,16},{26,18},{28,20},{30,22},{16,8},{18,10},{20,12},{22,14},{25... | collective-permute-start | bytes 2162696 | tf_op jit(solution)/shard_map/ppermute | solution.py:40
  116.0 20.9 %collective-permute-start.14 = (bf16[128,2816]{1,0:T(8,128)(2,1)S(1)}, bf16[128,2816]{1,0:T(8,128)(2,1)S(1)}, u32[]{:S(2)}, u32[]{:S(2)}) collective-permute-start(bf16[128,2816]{1,0:T(8,128)(2,1)S(1)} %get-tuple-element.45), channel_id=1, source_target_pairs={{0,8},{2,10},{4,12},{6,14},{8,16},{10,18},{12,20},{14,22},{1,9},{3... | collective-permute-start | bytes 2162696 | tf_op jit(solution)/shard_map/ppermute | solution.py:40
  125.6 11.7 %copy-start = (bf16[512,2688]{1,0:T(8,128)(2,1)}, bf16[512,2688]{1,0:T(8,128)(2,1)S(1)}, u32[]{:S(2)}) copy-start(bf16[512,2688]{1,0:T(8,128)(2,1)S(1)} %convolution_convert_fusion.1) | copy-start | bytes 8257540
  125.7 25.9 %collective-permute-start.16 = (bf16[128,2688]{1,0:T(8,128)(2,1)S(1)}, bf16[128,2688]{1,0:T(8,128)(2,1)S(1)}, u32[]{:S(2)}, u32[]{:S(2)}) collective-permute-start(bf16[128,2688]{1,0:T(8,128)(2,1)S(1)} %broadcast_select_fusion.5), channel_id=1, source_target_pairs={{0,8},{2,10},{4,12},{6,14},{24,16},{26,18},{28,20},{30,22},{1,9},{... | collective-permute-start | bytes 2064392 | tf_op jit(solution)/shard_map/ppermute | solution.py:40
  137.3 29.1 %collective-permute-start.17 = (bf16[128,2816]{1,0:T(8,128)(2,1)S(1)}, bf16[128,2816]{1,0:T(8,128)(2,1)S(1)}, u32[]{:S(2)}, u32[]{:S(2)}) collective-permute-start(bf16[128,2816]{1,0:T(8,128)(2,1)S(1)} %get-tuple-element.77), channel_id=1, source_target_pairs={{0,8},{2,10},{4,12},{6,14},{8,16},{10,18},{12,20},{14,22},{16,24},... | collective-permute-start | bytes 2162696 | tf_op jit(solution)/shard_map/ppermute | solution.py:40
  140.9 26.4 %collective-permute-start.18 = (bf16[128,2816]{1,0:T(8,128)(2,1)S(1)}, bf16[128,2816]{1,0:T(8,128)(2,1)S(1)}, u32[]{:S(2)}, u32[]{:S(2)}) collective-permute-start(bf16[128,2816]{1,0:T(8,128)(2,1)S(1)} %get-tuple-element.76), channel_id=1, source_target_pairs={{24,16},{26,18},{28,20},{30,22},{16,8},{18,10},{20,12},{22,14},{8,... | collective-permute-start | bytes 2162696 | tf_op jit(solution)/shard_map/ppermute | solution.py:40
  168.1 11.3 %collective-permute-start.19 = (bf16[5504,512]{1,0:T(8,128)(2,1)}, bf16[5504,512]{1,0:T(8,128)(2,1)}, u32[]{:S(2)}, u32[]{:S(2)}) collective-permute-start(bf16[5504,512]{1,0:T(8,128)(2,1)} %convolution_convert_fusion), channel_id=1, source_target_pairs={{0,2},{2,0},{4,6},{6,4},{8,10},{10,8},{12,14},{14,12},{16,18},{18,... | collective-permute-start | bytes 16908296 | tf_op jit(solution)/shard_map/ppermute | solution.py:32
  169.8 20.6 %collective-permute-start.21 = (bf16[128,2688]{1,0:T(8,128)(2,1)S(1)}, bf16[128,2688]{1,0:T(8,128)(2,1)S(1)}, u32[]{:S(2)}, u32[]{:S(2)}) collective-permute-start(bf16[128,2688]{1,0:T(8,128)(2,1)S(1)} %get-tuple-element.57), channel_id=1, source_target_pairs={{24,16},{26,18},{28,20},{30,22},{16,8},{18,10},{20,12},{22,14},{25... | collective-permute-start | bytes 2064392 | tf_op jit(solution)/shard_map/ppermute | solution.py:40
  171.1 8.3 %copy-start.10 = (bf16[128,5504]{1,0:T(8,128)(2,1)S(1)}, bf16[128,5504]{1,0:T(8,128)(2,1)}, u32[]{:S(2)}) copy-start(bf16[128,5504]{1,0:T(8,128)(2,1)} %copy-done.9) | copy-start | bytes 4227076
  171.2 8.3 %copy-start.12 = (bf16[128,5504]{1,0:T(8,128)(2,1)S(1)}, bf16[128,5504]{1,0:T(8,128)(2,1)}, u32[]{:S(2)}) copy-start(bf16[128,5504]{1,0:T(8,128)(2,1)} %copy-done.11) | copy-start | bytes 4227076
  171.2 8.3 %copy-start.30 = (bf16[128,1024]{1,0:T(8,128)(2,1)S(1)}, bf16[128,1024]{1,0:T(8,128)(2,1)}, u32[]{:S(2)}) copy-start(bf16[128,1024]{1,0:T(8,128)(2,1)} %copy-done.28) | copy-start | bytes 786436
  171.2 8.3 %copy-start.33 = (bf16[128,1024]{1,0:T(8,128)(2,1)S(1)}, bf16[128,1024]{1,0:T(8,128)(2,1)}, u32[]{:S(2)}) copy-start(bf16[128,1024]{1,0:T(8,128)(2,1)} %copy-done.31) | copy-start | bytes 786436
  171.2 20.0 %collective-permute-start.20 = (bf16[128,2688]{1,0:T(8,128)(2,1)S(1)}, bf16[128,2688]{1,0:T(8,128)(2,1)S(1)}, u32[]{:S(2)}, u32[]{:S(2)}) collective-permute-start(bf16[128,2688]{1,0:T(8,128)(2,1)S(1)} %get-tuple-element.56), channel_id=1, source_target_pairs={{0,8},{2,10},{4,12},{6,14},{8,16},{10,18},{12,20},{14,22},{1,9},{3... | collective-permute-start | bytes 2064392 | tf_op jit(solution)/shard_map/ppermute | solution.py:40
  183.4 63.0 %collective-permute-start.26 = (bf16[5504,256]{1,0:T(8,128)(2,1)S(1)}, bf16[5504,256]{1,0:T(8,128)(2,1)S(1)}, u32[]{:S(2)}, u32[]{:S(2)}) collective-permute-start(bf16[5504,256]{1,0:T(8,128)(2,1)S(1)} %fusion.1), channel_id=1, source_target_pairs={{0,4},{2,6},{4,0},{6,2},{8,12},{10,14},{12,8},{14,10},{16,20},{18,... | collective-permute-start | bytes 8454152 | tf_op jit(solution)/shard_map/ppermute | solution.py:32
  196.3 10.4 %copy-start.23 = (bf16[128,2816]{1,0:T(8,128)(2,1)S(1)}, bf16[128,2816]{1,0:T(8,128)(2,1)}, u32[]{:S(2)}) copy-start(bf16[128,2816]{1,0:T(8,128)(2,1)} %copy-done.22) | copy-start | bytes 2162692
  196.4 10.3 %copy-start.5 = (bf16[128,5504]{1,0:T(8,128)(2,1)S(1)}, bf16[128,5504]{1,0:T(8,128)(2,1)}, u32[]{:S(2)}) copy-start(bf16[128,5504]{1,0:T(8,128)(2,1)} %param.5) | copy-start | bytes 4227076
  196.4 10.3 %copy-start.6 = (bf16[128,5504]{1,0:T(8,128)(2,1)S(1)}, bf16[128,5504]{1,0:T(8,128)(2,1)}, u32[]{:S(2)}) copy-start(bf16[128,5504]{1,0:T(8,128)(2,1)} %param.4) | copy-start | bytes 4227076
  196.5 10.3 %copy-start.21 = (bf16[128,2816]{1,0:T(8,128)(2,1)S(1)}, bf16[128,2816]{1,0:T(8,128)(2,1)}, u32[]{:S(2)}) copy-start(bf16[128,2816]{1,0:T(8,128)(2,1)} %copy-done.20) | copy-start | bytes 2162692
  196.5 9.3 %collective-permute-start.22 = (bf16[128,1024]{1,0:T(8,128)(2,1)S(1)}, bf16[128,1024]{1,0:T(8,128)(2,1)S(1)}, u32[]{:S(2)}, u32[]{:S(2)}) collective-permute-start(bf16[128,1024]{1,0:T(8,128)(2,1)S(1)} %get-tuple-element.89), channel_id=1, source_target_pairs={{0,8},{2,10},{4,12},{6,14},{8,16},{10,18},{12,20},{14,22},{16,24},... | collective-permute-start | bytes 786440 | tf_op jit(solution)/shard_map/ppermute | solution.py:36
  199.2 38.3 %collective-permute-start.27 = (bf16[128,2688]{1,0:T(8,128)(2,1)S(1)}, bf16[128,2688]{1,0:T(8,128)(2,1)S(1)}, u32[]{:S(2)}, u32[]{:S(2)}) collective-permute-start(bf16[128,2688]{1,0:T(8,128)(2,1)S(1)} %get-tuple-element.65), channel_id=1, source_target_pairs={{0,8},{2,10},{4,12},{6,14},{8,16},{10,18},{12,20},{14,22},{16,24},... | collective-permute-start | bytes 2064392 | tf_op jit(solution)/shard_map/ppermute | solution.py:40
  201.3 36.3 %collective-permute-start.28 = (bf16[128,2688]{1,0:T(8,128)(2,1)S(1)}, bf16[128,2688]{1,0:T(8,128)(2,1)S(1)}, u32[]{:S(2)}, u32[]{:S(2)}) collective-permute-start(bf16[128,2688]{1,0:T(8,128)(2,1)S(1)} %get-tuple-element.67), channel_id=1, source_target_pairs={{24,16},{26,18},{28,20},{30,22},{16,8},{18,10},{20,12},{22,14},{8,... | collective-permute-start | bytes 2064392 | tf_op jit(solution)/shard_map/ppermute | solution.py:40
  205.1 30.5 %collective-permute-start.23 = (bf16[128,1024]{1,0:T(8,128)(2,1)S(1)}, bf16[128,1024]{1,0:T(8,128)(2,1)S(1)}, u32[]{:S(2)}, u32[]{:S(2)}) collective-permute-start(bf16[128,1024]{1,0:T(8,128)(2,1)S(1)} %get-tuple-element.88), channel_id=1, source_target_pairs={{0,16},{2,18},{4,20},{6,22},{8,24},{10,26},{12,28},{14,30},{16,0},... | collective-permute-start | bytes 786440 | tf_op jit(solution)/shard_map/ppermute | solution.py:36
  205.7 30.8 %collective-permute-start.24 = (bf16[128,1024]{1,0:T(8,128)(2,1)S(1)}, bf16[128,1024]{1,0:T(8,128)(2,1)S(1)}, u32[]{:S(2)}, u32[]{:S(2)}) collective-permute-start(bf16[128,1024]{1,0:T(8,128)(2,1)S(1)} %get-tuple-element.59), channel_id=1, source_target_pairs={{0,24},{2,26},{4,28},{6,30},{8,0},{10,2},{12,4},{14,6},{16,8},{18,... | collective-permute-start | bytes 786440 | tf_op jit(solution)/shard_map/ppermute | solution.py:36
  236.8 15.7 %collective-permute-start.25 = (bf16[128,2048]{1,0:T(8,128)(2,1)S(1)}, bf16[128,2048]{1,0:T(8,128)(2,1)S(1)}, u32[]{:S(2)}, u32[]{:S(2)}) collective-permute-start(bf16[128,2048]{1,0:T(8,128)(2,1)S(1)} %pad_maximum_fusion.17), channel_id=1, source_target_pairs={{0,1},{1,0},{2,3},{3,2},{4,5},{5,4},{6,7},{7,6},{8,9},{9,8},{10,11... | collective-permute-start | bytes 1572872 | tf_op jit(solution)/shard_map/ppermute | solution.py:49
  (15 other events, 69.1 us)

commit v4 on v3

--- a/solution.py
+++ b/solution.py
@@ -119,20 +119,37 @@
         cot_slots = jnp.concatenate(parts, axis=1).reshape(tokens, n_far, QUAD, width)
         cot_slots = picked(cot_slots, [near ^ k for k in ORDER], 2).reshape(tokens, n_far, columns)
 
-        def cot_for(step):
+        block = tokens // n_local
+
+        def cot_for(step, first_row, count):
             place = (far + step) % n_far
             start = (place // per_half - x) % n_local * per_half + place % per_half
-            return lax.dynamic_index_in_dim(cot_slots, start, axis=1, keepdims=False)
+            found = lax.dynamic_slice(cot_slots, (first_row, start, 0), (count, 1, columns))
+            return found.reshape(count, columns)
 
         came = []
         for e in range(1, n_far):
-            came.append(shift(after(cot_for(n_far - e), *came[: max(0, e - 2)]), n_far - e))
-        cot_rows = jnp.concatenate([cot_for(0)] + came, axis=0)
+            sent = cot_for(n_far - e, x * block, block)
+            came.append(shift(after(sent, *came[: max(0, e - 2)]), n_far - e))
         fence = waits + came + [weight_side]
+
+        def whole_rows():
+            mine = jnp.concatenate(came, axis=0)
+            sides = [mine] + [move(local_shift, mine, n_local - i) for i in range(1, n_local)]
+            blocks = []
+            for i in range(n_local):
+                picked_block = sides[0]
+                for turn in range(1, n_local):
+                    here = (i - x) % n_local == turn
+                    picked_block = jnp.where(here, sides[turn], picked_block)
+                blocks.append(picked_block.reshape(n_far - 1, block, columns))
+            others = jnp.concatenate(blocks, axis=1).reshape((n_far - 1) * tokens, columns)
+            return jnp.concatenate([cot_for(0, 0, tokens), others], axis=0)
 
         for j in range(2, n_far):
             waits = gather_hop(j)
             if j == 2:
+                cot_rows = whole_rows()
                 weights[0] = weight_columns(0, weight_side)
                 weight_side = move(swap, down_weight[middle:], 2)
                 terms[0] = reduce_terms(0)

time: 258 us -> 249 us (0.965)
  waiting for transfers between devices: 120 us -> 108 us
  other arithmetic: 29.6 us -> 35.1 us
    ppermute x6, waiting for transfers between devices: 66.5 us -> 57.2 us  [shift(): return lax.ppermute(value, 'hst', pairs)]
    add x0 -> x1, other arithmetic: none -> 5.01 us  [on_device(): down_grad = down_grad + other_grad.astype(jnp.float32)]
    dot_general x3, matrix products: 16.7 us -> 13.4 us  [grad_terms(): lax.dot_general(rows, part, SUM_ROWS, preferred_element_type=jnp.float32)]
  transfers between devices with their start and end apart: 29 -> 30, of which waited for: 15 -> 16; matrix products, arithmetic and copies ran while one was open for 29% -> 31% of each run, Pallas kernels for 0% -> 0%
where the time goes in v4:
time: 249 us; the launch traced here: 247 us
  waiting for transfers between devices  108 us (43%)
  starting transfers between devices  54.3 us (22%)
  matrix products  35.4 us (14%)
  other arithmetic  35.1 us (14%)
  local copies, waits for them, and re-layouts  13.2 us (5%)
    ppermute x6, waiting for transfers between devices, shift(): return lax.ppermute(value, 'hst', pairs)  57.2 us
    ppermute x15, starting transfers between devices, far_permute(): return lax.ppermute(value, 'hst', pairs)  41.5 us
    ppermute x15, waiting for transfers between devices, far_permute(): return lax.ppermute(value, 'hst', pairs)  25.3 us
    ppermute x6, waiting for transfers between devices, swap(): return lax.ppermute(value, 'hst', [(h, h ^ bit) for h in range(n_hst)])  23.8 us
    dot_general x3, matrix products, grad_terms(): lax.dot_general(rows, part, SUM_ROWS, preferred_element_type=jnp.float32)  13.4 us
    dot_general x2, matrix products, reduce_terms(): lax.dot_general(cot_rows, weights[f], KEEP_COLS, preferred_element_type=j...  11 us
    dot_general x2, matrix products, on_device(): jnp.dot(rows[:, lo:hi], weights[f], preferred_element_type=jnp.float32)  11 us
    concatenate x2, other arithmetic, weight_columns(): pair = jnp.concatenate([down_weight[lo:hi], other], axis=1)  6.74 us
  transfers between devices with their start and end apart: 30, of which 16 were waited for; matrix products, arithmetic and copies ran while one was open for 31% of the time, Pallas kernels for 0%

profile of v4, /device:TPU:8, one launch (start us, length us, event | category | flops | bytes accessed | tf_op | source)
XLA Modules:
  0.0 247.2 jit_solution(6368750696014659895)
XLA Ops:
  0.6 1.6 collective-permute-start.2
  2.2 3.7 %fusion.6 = bf16[128,5504]{1,0:T(8,128)(2,1)} fusion(bf16[128,5504]{1,0:T(8,128)(2,1)} %param.5, bf16[128,5504]{1,0:T(8,128)(2,1)} %param.4), kind=kLoop, calls=%fused_computation.17 | loop fusion | flops 5636096 | bytes 4227072 | tf_op jit(solution)/shard_map/convert_element_type | solution.py:69
  6.0 1.6 collective-permute-start.6
  7.6 2.3 collective-permute-start
  10.0 3.5 %collective-permute-start.1 = (bf16[128,5504]{1,0:T(8,128)(2,1)}, bf16[128,5504]{1,0:T(8,128)(2,1)}, u32[]{:S(2)}, u32[]{:S(2)}) collective-permute-start(bf16[128,5504]{1,0:T(8,128)(2,1)} %fusion.6), channel_id=1, source_target_pairs={{0,8},{2,10},{4,12},{6,14},{8,16},{10,18},{12,20},{14,22},{16,24},... | collective-permute-start | bytes 4227080 | tf_op jit(solution)/shard_map/ppermute | solution.py:40
  15.5 2.2 constant_dynamic-slice_fusion.15
  17.7 2.4 pad_maximum_fusion.15
  21.9 2.9 %collective-permute-start.4 = (bf16[64,1024]{1,0:T(8,128)(2,1)S(1)}, bf16[64,1024]{1,0:T(8,128)(2,1)S(1)}, u32[]{:S(2)}, u32[]{:S(2)}) collective-permute-start(bf16[64,1024]{1,0:T(8,128)(2,1)S(1)} %bitcast.28), channel_id=1, source_target_pairs={{0,16},{2,18},{4,20},{6,22},{8,24},{10,26},{12,28},{14,30},{16,0},... | collective-permute-start | bytes 393224 | tf_op jit(solution)/shard_map/ppermute | solution.py:36
  24.9 25.3 %collective-permute-done.3 = bf16[64,1024]{1,0:T(8,128)(2,1)S(1)} collective-permute-done((bf16[64,1024]{1,0:T(8,128)(2,1)S(1)}, bf16[64,1024]{1,0:T(8,128)(2,1)S(1)}, u32[]{:S(2)}, u32[]{:S(2)}) %collective-permute-start.3) | collective-permute-done | bytes 131104 | tf_op jit(solution)/shard_map/ppermute | solution.py:36
  50.2 3.1 %pad_maximum_fusion.3 = bf16[2816,512]{1,0:T(8,128)(2,1)} fusion(bf16[2816,256]{1,0:T(8,128)(2,1)} %collective-permute-done.6, bf16[2816,256]{1,0:T(8,128)(2,1)S(1)} %slice.77), kind=kLoop, calls=%fused_computation.10 | loop fusion | flops 5767168 | bytes 5767168 | tf_op jit(solution)/shard_map/concatenate | solution.py:104
  53.3 1.8 collective-permute-done.5
  56.0 2.5 %slice.78 = bf16[2688,256]{1,0:T(8,128)(2,1)} slice(bf16[5504,256]{1,0:T(8,128)(2,1)} %param.7), slice={[2816:5504], [0:256]} | slice | bytes 2752512 | tf_op jit(solution)/shard_map/slice | solution.py:154
  59.7 4.6 %collective-permute-start.8 = (bf16[128,5504]{1,0:T(8,128)(2,1)}, bf16[128,5504]{1,0:T(8,128)(2,1)}, u32[]{:S(2)}, u32[]{:S(2)}) collective-permute-start(bf16[128,5504]{1,0:T(8,128)(2,1)} %collective-permute-done.1), channel_id=1, source_target_pairs={{8,16},{10,18},{12,20},{14,22},{16,24},{18,26},{20,28},{22,30},{9,... | collective-permute-start | bytes 4227080 | tf_op jit(solution)/shard_map/ppermute | solution.py:40
  64.3 2.1 collective-permute-start.7
  67.0 5.7 %convolution_convert_fusion.2 = bf16[512,2816]{1,0:T(8,128)(2,1)S(1)} fusion(bf16[2816,512]{1,0:T(8,128)(2,1)} %collective-permute-done.11, bf16[2816,256]{1,0:T(8,128)(2,1)} %collective-permute-done.6, bf16[2816,256]{1,0:T(8,128)(2,1)S(1)} %copy-done.3, bf16[128,1024]{1,0:T(8,128)(2,1)S(1)} %bitcast.23, bf16[384,1024]{1,0:T(8,128)(2,1)S(1)} %bitcast.16), kind=kOutput, calls=%fused_computation.7 | convolution fusion | flops 2973630464 | bytes 9699328 | tf_op jit(solution)/shard_map/dot_general | solution.py:109
  72.7 1.3 collective-permute-start.12
  74.0 17.7 %collective-permute-done.9 = bf16[2688,256]{1,0:T(8,128)(2,1)S(1)} collective-permute-done((bf16[2688,256]{1,0:T(8,128)(2,1)}, bf16[2688,256]{1,0:T(8,128)(2,1)S(1)}, u32[]{:S(2)}, u32[]{:S(2)}) %collective-permute-start.9) | collective-permute-done | bytes 1376288 | tf_op jit(solution)/shard_map/ppermute | solution.py:32
  91.7 3.6 %pad_maximum_fusion.4 = bf16[2688,512]{1,0:T(8,128)(2,1)} fusion(bf16[2688,256]{1,0:T(8,128)(2,1)S(1)} %collective-permute-done.9, bf16[2688,256]{1,0:T(8,128)(2,1)} %slice.78), kind=kLoop, calls=%fused_computation.18 | loop fusion | flops 5505024 | bytes 5505024 | tf_op jit(solution)/shard_map/concatenate | solution.py:104
  95.3 3.7 %collective-permute-done.7 = bf16[128,5504]{1,0:T(8,128)(2,1)} collective-permute-done((bf16[128,5504]{1,0:T(8,128)(2,1)}, bf16[128,5504]{1,0:T(8,128)(2,1)}, u32[]{:S(2)}, u32[]{:S(2)}) %collective-permute-start.7) | collective-permute-done | bytes 1409056 | tf_op jit(solution)/shard_map/ppermute | solution.py:40
  99.9 1.6 broadcast_select_fusion.3
  101.5 2.4 collective-permute-start.13
  106.6 4.6 %collective-permute-start.15 = (bf16[128,2816]{1,0:T(8,128)(2,1)S(1)}, bf16[128,2816]{1,0:T(8,128)(2,1)S(1)}, u32[]{:S(2)}, u32[]{:S(2)}) collective-permute-start(bf16[128,2816]{1,0:T(8,128)(2,1)S(1)} %get-tuple-element.47), channel_id=1, source_target_pairs={{0,8},{2,10},{4,12},{6,14},{8,16},{10,18},{12,20},{14,22},{1,9},{3... | collective-permute-start | bytes 2162696 | tf_op jit(solution)/shard_map/ppermute | solution.py:40
  111.2 5.4 %convolution_convert_fusion.1 = bf16[512,2688]{1,0:T(8,128)(2,1)S(1)} fusion(bf16[2688,512]{1,0:T(8,128)(2,1)} %collective-permute-done.14, bf16[2688,256]{1,0:T(8,128)(2,1)S(1)} %copy-done.18, bf16[2688,256]{1,0:T(8,128)(2,1)} %slice.78, bf16[128,1024]{1,0:T(8,128)(2,1)S(1)} %bitcast.24, bf16[384,1024]{1,0:T(8,128)(2,1)S(1)} %bitcast.17), kind=kOutput, calls=%fused_computation.6 | convolution fusion | flops 2838560768 | bytes 9306112 | tf_op jit(solution)/shard_map/dot_general | solution.py:109
  118.0 7.4 %collective-permute-done.16 = bf16[128,2816]{1,0:T(8,128)(2,1)S(1)} collective-permute-done((bf16[128,2816]{1,0:T(8,128)(2,1)S(1)}, bf16[128,2816]{1,0:T(8,128)(2,1)S(1)}, u32[]{:S(2)}, u32[]{:S(2)}) %collective-permute-start.16) | collective-permute-done | bytes 720928 | tf_op jit(solution)/shard_map/ppermute | solution.py:40
  125.4 2.1 collective-permute-done.15
  127.8 3.5 %collective-permute-start.18 = (bf16[128,2816]{1,0:T(8,128)(2,1)S(1)}, bf16[128,2816]{1,0:T(8,128)(2,1)S(1)}, u32[]{:S(2)}, u32[]{:S(2)}) collective-permute-start(bf16[128,2816]{1,0:T(8,128)(2,1)S(1)} %get-tuple-element.79), channel_id=1, source_target_pairs={{0,8},{2,10},{4,12},{6,14},{8,16},{10,18},{12,20},{14,22},{16,24},... | collective-permute-start | bytes 2162696 | tf_op jit(solution)/shard_map/ppermute | solution.py:40
  131.3 2.4 collective-permute-start.19
  135.0 7.2 %collective-permute-done.17 = bf16[128,2688]{1,0:T(8,128)(2,1)S(1)} collective-permute-done((bf16[128,2688]{1,0:T(8,128)(2,1)S(1)}, bf16[128,2688]{1,0:T(8,128)(2,1)S(1)}, u32[]{:S(2)}, u32[]{:S(2)}) %collective-permute-start.17) | collective-permute-done | bytes 688160 | tf_op jit(solution)/shard_map/ppermute | solution.py:40
  142.3 1.8 broadcast_select_fusion.1
  144.0 2.6 %broadcast_select_fusion.2 = (bf16[128,5504]{1,0:T(8,128)(2,1)S(1)}, bf16[128,5504]{1,0:T(8,128)(2,1)S(1)}) fusion(bf16[128,5504]{1,0:T(8,128)(2,1)} %collective-permute-done, bf16[128,5504]{1,0:T(8,128)(2,1)S(1)} %collective-permute-done.13, pred[]{:T(512)S(6)} %lt.176, bf16[128,5504]{1,0:T(8,128)(2,1)} %collective-permute-done.1, pred[]{:T(512)S(6)} %lt.178), kind=kLoop, calls=%fused_computation.52 | loop fusion | flops 1409024 | bytes 7045122 | tf_op jit(solution)/shard_map/jit(_where)/select_n | solution.py:173
  146.6 6.8 %convolution_convert_fusion = bf16[5504,512]{1,0:T(8,128)(2,1)} fusion(bf16[384,1024]{1,0:T(8,128)(2,1)S(1)} %bitcast.18, bf16[128,1024]{1,0:T(8,128)(2,1)S(1)} %bitcast.25, bf16[128,5504]{1,0:T(8,128)(2,1)S(1)} %get-tuple-element.83, bf16[128,5504]{1,0:T(8,128)(2,1)S(1)} %broadcast_select_fusion.1, bf16[128,5504]{1,0:T(8,128)(2,1)S(1)} %get-tuple-element.82, ...), kind=kOutput, calls=%fused_computation | convolution fusion | flops 2912092160 | bytes 12320768 | tf_op jit(solution)/shard_map/dot_general | solution.py:178
  153.4 3.5 %collective-permute-done.18 = bf16[128,2816]{1,0:T(8,128)(2,1)S(1)} collective-permute-done((bf16[128,2816]{1,0:T(8,128)(2,1)S(1)}, bf16[128,2816]{1,0:T(8,128)(2,1)S(1)}, u32[]{:S(2)}, u32[]{:S(2)}) %collective-permute-start.18) | collective-permute-done | bytes 720928 | tf_op jit(solution)/shard_map/ppermute | solution.py:40
  158.7 1.7 fusion.22
  161.8 5.0 %collective-permute-start.21 = (bf16[128,2688]{1,0:T(8,128)(2,1)S(1)}, bf16[128,2688]{1,0:T(8,128)(2,1)S(1)}, u32[]{:S(2)}, u32[]{:S(2)}) collective-permute-start(bf16[128,2688]{1,0:T(8,128)(2,1)S(1)} %get-tuple-element.58), channel_id=1, source_target_pairs={{0,8},{2,10},{4,12},{6,14},{8,16},{10,18},{12,20},{14,22},{1,9},{3... | collective-permute-start | bytes 2064392 | tf_op jit(solution)/shard_map/ppermute | solution.py:40
  166.8 3.2 %pad_maximum_fusion.1 = bf16[512,5504]{1,0:T(8,128)(2,1)S(1)} fusion(bf16[128,5504]{1,0:T(8,128)(2,1)} %copy-done.11, bf16[128,5504]{1,0:T(8,128)(2,1)S(1)} %copy-done.8, bf16[128,5504]{1,0:T(8,128)(2,1)} %copy-done.9, bf16[128,5504]{1,0:T(8,128)(2,1)} %fusion.6), kind=kLoop, calls=%fused_computation.2 | loop fusion | flops 22544384 | bytes 11272192 | tf_op jit(solution)/shard_map/concatenate | solution.py:174
  170.1 5.0 %add_convert_fusion = bf16[5504,256]{1,0:T(8,128)(2,1)} fusion(bf16[5504,512]{1,0:T(8,128)(2,1)} %collective-permute-done.20, bf16[384,1024]{1,0:T(8,128)(2,1)S(1)} %bitcast.19, bf16[128,1024]{1,0:T(8,128)(2,1)S(1)} %bitcast.26, bf16[128,5504]{1,0:T(8,128)(2,1)S(1)} %copy-done.12, bf16[128,5504]{1,0:T(8,128)(2,1)S(1)} %copy-done.8, ...), kind=kOutput, calls=%fused_computation.4 | convolution fusion | flops 1470136320 | bytes 12320768 | tf_op jit(solution)/shard_map/dot_general | solution.py:178
  175.0 1.4 collective-permute-start.27
  176.4 5.4 %fusion = f32[512,1024]{1,0:T(8,128)S(1)} fusion(bf16[512,5504]{1,0:T(8,128)(2,1)S(1)} %pad_maximum_fusion.1, bf16[2816,512]{1,0:T(8,128)(2,1)} %collective-permute-done.11, bf16[2816,256]{1,0:T(8,128)(2,1)} %collective-permute-done.6, bf16[2816,256]{1,0:T(8,128)(2,1)S(1)} %copy-done.4), kind=kOutput, calls=%fused_computation.11 | convolution fusion | flops 2970091520 | bytes 10747904 | tf_op jit(solution)/shard_map/dot_general | solution.py:189
  181.9 1.7 fusion.34
  183.6 5.5 %add_convert_fusion.1 = bf16[512,1024]{1,0:T(8,128)(2,1)S(1)} fusion(f32[512,1024]{1,0:T(8,128)S(1)} %fusion, bf16[2688,512]{1,0:T(8,128)(2,1)} %collective-permute-done.14, bf16[2688,256]{1,0:T(8,128)(2,1)S(1)} %copy-done.19, bf16[2688,256]{1,0:T(8,128)(2,1)} %slice.78, bf16[512,5504]{1,0:T(8,128)(2,1)S(1)} %pad_maximum_fusion.1), kind=kOutput, calls=%fused_computation.24 | convolution fusion | flops 2836135936 | bytes 11403264 | tf_op jit(solution)/shard_map/dot_general | solution.py:189
  190.2 2.1 collective-permute-start.28
  192.3 4.0 %collective-permute-start.29 = (bf16[128,2688]{1,0:T(8,128)(2,1)S(1)}, bf16[128,2688]{1,0:T(8,128)(2,1)S(1)}, u32[]{:S(2)}, u32[]{:S(2)}) collective-permute-start(bf16[128,2688]{1,0:T(8,128)(2,1)S(1)} %get-tuple-element.69), channel_id=1, source_target_pairs={{24,16},{26,18},{28,20},{30,22},{16,8},{18,10},{20,12},{22,14},{8,... | collective-permute-start | bytes 2064392 | tf_op jit(solution)/shard_map/ppermute | solution.py:40
  199.8 26.8 %collective-permute-done.24 = bf16[128,1024]{1,0:T(8,128)(2,1)S(1)} collective-permute-done((bf16[128,1024]{1,0:T(8,128)(2,1)S(1)}, bf16[128,1024]{1,0:T(8,128)(2,1)S(1)}, u32[]{:S(2)}, u32[]{:S(2)}) %collective-permute-start.24) | collective-permute-done | bytes 262176 | tf_op jit(solution)/shard_map/ppermute | solution.py:36
  226.6 2.2 collective-permute-done.25
  229.0 1.4 collective-permute-start.26
  231.3 1.7 pad_maximum_fusion.12
  233.1 5.1 %collective-permute-done.27 = bf16[5504,256]{1,0:T(8,128)(2,1)S(1)} collective-permute-done((bf16[5504,256]{1,0:T(8,128)(2,1)}, bf16[5504,256]{1,0:T(8,128)(2,1)S(1)}, u32[]{:S(2)}, u32[]{:S(2)}) %collective-permute-start.27) | collective-permute-done | bytes 2818080 | tf_op jit(solution)/shard_map/ppermute | solution.py:32
  238.2 5.0 %convert_add_fusion = f32[5504,256]{1,0:T(8,128)} fusion(bf16[5504,256]{1,0:T(8,128)(2,1)S(1)} %collective-permute-done.27, f32[5504,256]{1,0:T(8,128)S(1)} %fusion.34, bf16[5504,512]{1,0:T(8,128)(2,1)} %collective-permute-done.20), kind=kLoop, calls=%fused_computation.3 | loop fusion | flops 5636096 | bytes 16908288 | tf_op jit(solution)/shard_map/add | solution.py:186
  (119 shorter events, 25.8 us)
Async XLA Ops:
  0.6 13.9 %collective-permute-start.2 = (bf16[128,2048]{1,0:T(8,128)(2,1)}, bf16[128,2048]{1,0:T(8,128)(2,1)S(1)}, u32[]{:S(2)}, u32[]{:S(2)}) collective-permute-start(bf16[128,2048]{1,0:T(8,128)(2,1)} %param.6), channel_id=1, source_target_pairs={{0,1},{1,0},{2,3},{3,2},{4,5},{5,4},{6,7},{7,6},{8,9},{9,8},{10,11... | collective-permute-start | bytes 1572872 | tf_op jit(solution)/shard_map/ppermute | solution.py:49
  5.9 8.7 %copy-start.27 = (bf16[128,2048]{1,0:T(8,128)(2,1)S(1)}, bf16[128,2048]{1,0:T(8,128)(2,1)}, u32[]{:S(2)}) copy-start(bf16[128,2048]{1,0:T(8,128)(2,1)} %param.6) | copy-start | bytes 1572868
  6.0 44.2 %copy-start.2 = (bf16[2816,256]{1,0:T(8,128)(2,1)}, bf16[2816,256]{1,0:T(8,128)(2,1)S(1)}, u32[]{:S(2)}) copy-start(bf16[2816,256]{1,0:T(8,128)(2,1)S(1)} %slice.77) | copy-start | bytes 4325380
  6.0 44.2 %collective-permute-start.6 = (bf16[2816,256]{1,0:T(8,128)(2,1)S(1)}, bf16[2816,256]{1,0:T(8,128)(2,1)}, u32[]{:S(2)}, u32[]{:S(2)}) collective-permute-start(bf16[2816,256]{1,0:T(8,128)(2,1)S(1)} %slice.77), channel_id=1, source_target_pairs={{0,4},{2,6},{4,0},{6,2},{8,12},{10,14},{12,8},{14,10},{16,20},{18,... | collective-permute-start | bytes 4325384 | tf_op jit(solution)/shard_map/ppermute | solution.py:32
  7.6 47.6 %collective-permute-start = (bf16[128,5504]{1,0:T(8,128)(2,1)}, bf16[128,5504]{1,0:T(8,128)(2,1)}, u32[]{:S(2)}, u32[]{:S(2)}) collective-permute-start(bf16[128,5504]{1,0:T(8,128)(2,1)} %fusion.6), channel_id=1, source_target_pairs={{24,16},{26,18},{28,20},{30,22},{16,8},{18,10},{20,12},{22,14},{8,... | collective-permute-start | bytes 4227080 | tf_op jit(solution)/shard_map/ppermute | solution.py:40
  10.0 45.2 %collective-permute-start.1 = (bf16[128,5504]{1,0:T(8,128)(2,1)}, bf16[128,5504]{1,0:T(8,128)(2,1)}, u32[]{:S(2)}, u32[]{:S(2)}) collective-permute-start(bf16[128,5504]{1,0:T(8,128)(2,1)} %fusion.6), channel_id=1, source_target_pairs={{0,8},{2,10},{4,12},{6,14},{8,16},{10,18},{12,20},{14,22},{16,24},... | collective-permute-start | bytes 4227080 | tf_op jit(solution)/shard_map/ppermute | solution.py:40
  21.4 28.7 %collective-permute-start.3 = (bf16[64,1024]{1,0:T(8,128)(2,1)S(1)}, bf16[64,1024]{1,0:T(8,128)(2,1)S(1)}, u32[]{:S(2)}, u32[]{:S(2)}) collective-permute-start(bf16[64,1024]{1,0:T(8,128)(2,1)S(1)} %bitcast.30), channel_id=1, source_target_pairs={{0,24},{2,26},{4,28},{6,30},{8,0},{10,2},{12,4},{14,6},{16,8},{18,... | collective-permute-start | bytes 393224 | tf_op jit(solution)/shard_map/ppermute | solution.py:36
  21.9 31.4 %collective-permute-start.4 = (bf16[64,1024]{1,0:T(8,128)(2,1)S(1)}, bf16[64,1024]{1,0:T(8,128)(2,1)S(1)}, u32[]{:S(2)}, u32[]{:S(2)}) collective-permute-start(bf16[64,1024]{1,0:T(8,128)(2,1)S(1)} %bitcast.28), channel_id=1, source_target_pairs={{0,16},{2,18},{4,20},{6,22},{8,24},{10,26},{12,28},{14,30},{16,0},... | collective-permute-start | bytes 393224 | tf_op jit(solution)/shard_map/ppermute | solution.py:36
  50.2 5.0 %collective-permute-start.5 = (bf16[64,1024]{1,0:T(8,128)(2,1)S(1)}, bf16[64,1024]{1,0:T(8,128)(2,1)S(1)}, u32[]{:S(2)}, u32[]{:S(2)}) collective-permute-start(bf16[64,1024]{1,0:T(8,128)(2,1)S(1)} %bitcast.29), channel_id=1, source_target_pairs={{0,8},{2,10},{4,12},{6,14},{8,16},{10,18},{12,20},{14,22},{16,24},... | collective-permute-start | bytes 393224 | tf_op jit(solution)/shard_map/ppermute | solution.py:36
  55.2 11.8 %collective-permute-start.11 = (bf16[2816,512]{1,0:T(8,128)(2,1)}, bf16[2816,512]{1,0:T(8,128)(2,1)}, u32[]{:S(2)}, u32[]{:S(2)}) collective-permute-start(bf16[2816,512]{1,0:T(8,128)(2,1)} %pad_maximum_fusion.3), channel_id=1, source_target_pairs={{0,2},{2,0},{4,6},{6,4},{8,10},{10,8},{12,14},{14,12},{16,18},{18,... | collective-permute-start | bytes 8650760 | tf_op jit(solution)/shard_map/ppermute | solution.py:32
  55.2 11.6 %collective-permute-start.10 = (bf16[192,1024]{1,0:T(8,128)(2,1)S(1)}, bf16[192,1024]{1,0:T(8,128)(2,1)S(1)}, u32[]{:S(2)}, u32[]{:S(2)}) collective-permute-start(bf16[192,1024]{1,0:T(8,128)(2,1)S(1)} %constant_dynamic-update-slice_fusion), channel_id=1, source_target_pairs={{0,1},{1,0},{2,3},{3,2},{4,5},{5,4},{6,7},{7,6},{8,9},{9,8},{10,11... | collective-permute-start | bytes 1179656 | tf_op jit(solution)/shard_map/ppermute | solution.py:49
  59.0 7.9 %copy-start.3 = (bf16[2816,256]{1,0:T(8,128)(2,1)S(1)}, bf16[2816,256]{1,0:T(8,128)(2,1)}, u32[]{:S(2)}) copy-start(bf16[2816,256]{1,0:T(8,128)(2,1)} %copy-done.2) | copy-start | bytes 4325380
  59.1 32.6 %collective-permute-start.9 = (bf16[2688,256]{1,0:T(8,128)(2,1)}, bf16[2688,256]{1,0:T(8,128)(2,1)S(1)}, u32[]{:S(2)}, u32[]{:S(2)}) collective-permute-start(bf16[2688,256]{1,0:T(8,128)(2,1)} %slice.78), channel_id=1, source_target_pairs={{0,4},{2,6},{4,0},{6,2},{8,12},{10,14},{12,8},{14,10},{16,20},{18,... | collective-permute-start | bytes 4128776 | tf_op jit(solution)/shard_map/ppermute | solution.py:32
  59.7 35.6 %collective-permute-start.8 = (bf16[128,5504]{1,0:T(8,128)(2,1)}, bf16[128,5504]{1,0:T(8,128)(2,1)}, u32[]{:S(2)}, u32[]{:S(2)}) collective-permute-start(bf16[128,5504]{1,0:T(8,128)(2,1)} %collective-permute-done.1), channel_id=1, source_target_pairs={{8,16},{10,18},{12,20},{14,22},{16,24},{18,26},{20,28},{22,30},{9,... | collective-permute-start | bytes 4227080 | tf_op jit(solution)/shard_map/ppermute | solution.py:40
  64.3 34.8 %collective-permute-start.7 = (bf16[128,5504]{1,0:T(8,128)(2,1)}, bf16[128,5504]{1,0:T(8,128)(2,1)}, u32[]{:S(2)}, u32[]{:S(2)}) collective-permute-start(bf16[128,5504]{1,0:T(8,128)(2,1)} %collective-permute-done), channel_id=1, source_target_pairs={{16,8},{18,10},{20,12},{22,14},{8,0},{10,2},{12,4},{14,6},{17,9},{... | collective-permute-start | bytes 4227080 | tf_op jit(solution)/shard_map/ppermute | solution.py:40
  72.7 26.3 %collective-permute-start.12 = (bf16[128,2816]{1,0:T(8,128)(2,1)S(1)}, bf16[128,2816]{1,0:T(8,128)(2,1)S(1)}, u32[]{:S(2)}, u32[]{:S(2)}) collective-permute-start(bf16[128,2816]{1,0:T(8,128)(2,1)S(1)} %broadcast_select_fusion.4), channel_id=1, source_target_pairs={{0,8},{2,10},{4,12},{6,14},{24,16},{26,18},{28,20},{30,22},{1,9},{... | collective-permute-start | bytes 2162696 | tf_op jit(solution)/shard_map/ppermute | solution.py:40
  99.9 5.4 %collective-permute-start.14 = (bf16[2688,512]{1,0:T(8,128)(2,1)}, bf16[2688,512]{1,0:T(8,128)(2,1)}, u32[]{:S(2)}, u32[]{:S(2)}) collective-permute-start(bf16[2688,512]{1,0:T(8,128)(2,1)} %pad_maximum_fusion.4), channel_id=1, source_target_pairs={{0,2},{2,0},{4,6},{6,4},{8,10},{10,8},{12,14},{14,12},{16,18},{18,... | collective-permute-start | bytes 8257544 | tf_op jit(solution)/shard_map/ppermute | solution.py:32
  101.5 9.7 %copy-start.14 = (bf16[3,128,1024]{2,1,0:T(8,128)(2,1)S(1)}, bf16[3,128,1024]{2,1,0:T(8,128)(2,1)}, u32[]{:S(2)}) copy-start(bf16[3,128,1024]{2,1,0:T(8,128)(2,1)} %copy-done.13) | copy-start | bytes 2359300
  101.5 9.7 %copy-start.18 = (bf16[2688,256]{1,0:T(8,128)(2,1)S(1)}, bf16[2688,256]{1,0:T(8,128)(2,1)}, u32[]{:S(2)}) copy-start(bf16[2688,256]{1,0:T(8,128)(2,1)} %copy-done.17) | copy-start | bytes 4128772
  101.5 33.5 %collective-permute-start.13 = (bf16[128,5504]{1,0:T(8,128)(2,1)S(1)}, bf16[128,5504]{1,0:T(8,128)(2,1)S(1)}, u32[]{:S(2)}, u32[]{:S(2)}) collective-permute-start(bf16[128,5504]{1,0:T(8,128)(2,1)S(1)} %broadcast_select_fusion.3), channel_id=1, source_target_pairs={{16,24},{18,26},{20,28},{22,30},{8,0},{10,2},{12,4},{14,6},{17,25}... | collective-permute-start | bytes 4227080 | tf_op jit(solution)/shard_map/ppermute | solution.py:40
  105.3 20.1 %collective-permute-start.16 = (bf16[128,2816]{1,0:T(8,128)(2,1)S(1)}, bf16[128,2816]{1,0:T(8,128)(2,1)S(1)}, u32[]{:S(2)}, u32[]{:S(2)}) collective-permute-start(bf16[128,2816]{1,0:T(8,128)(2,1)S(1)} %get-tuple-element.48), channel_id=1, source_target_pairs={{24,16},{26,18},{28,20},{30,22},{16,8},{18,10},{20,12},{22,14},{25... | collective-permute-start | bytes 2162696 | tf_op jit(solution)/shard_map/ppermute | solution.py:40
  106.6 20.9 %collective-permute-start.15 = (bf16[128,2816]{1,0:T(8,128)(2,1)S(1)}, bf16[128,2816]{1,0:T(8,128)(2,1)S(1)}, u32[]{:S(2)}, u32[]{:S(2)}) collective-permute-start(bf16[128,2816]{1,0:T(8,128)(2,1)S(1)} %get-tuple-element.47), channel_id=1, source_target_pairs={{0,8},{2,10},{4,12},{6,14},{8,16},{10,18},{12,20},{14,22},{1,9},{3... | collective-permute-start | bytes 2162696 | tf_op jit(solution)/shard_map/ppermute | solution.py:40
  116.6 11.3 %copy-start = (bf16[512,2688]{1,0:T(8,128)(2,1)}, bf16[512,2688]{1,0:T(8,128)(2,1)S(1)}, u32[]{:S(2)}) copy-start(bf16[512,2688]{1,0:T(8,128)(2,1)S(1)} %convolution_convert_fusion.1) | copy-start | bytes 8257540
  116.7 25.6 %collective-permute-start.17 = (bf16[128,2688]{1,0:T(8,128)(2,1)S(1)}, bf16[128,2688]{1,0:T(8,128)(2,1)S(1)}, u32[]{:S(2)}, u32[]{:S(2)}) collective-permute-start(bf16[128,2688]{1,0:T(8,128)(2,1)S(1)} %broadcast_select_fusion.5), channel_id=1, source_target_pairs={{0,8},{2,10},{4,12},{6,14},{24,16},{26,18},{28,20},{30,22},{1,9},{... | collective-permute-start | bytes 2064392 | tf_op jit(solution)/shard_map/ppermute | solution.py:40
  127.8 29.1 %collective-permute-start.18 = (bf16[128,2816]{1,0:T(8,128)(2,1)S(1)}, bf16[128,2816]{1,0:T(8,128)(2,1)S(1)}, u32[]{:S(2)}, u32[]{:S(2)}) collective-permute-start(bf16[128,2816]{1,0:T(8,128)(2,1)S(1)} %get-tuple-element.79), channel_id=1, source_target_pairs={{0,8},{2,10},{4,12},{6,14},{8,16},{10,18},{12,20},{14,22},{16,24},... | collective-permute-start | bytes 2162696 | tf_op jit(solution)/shard_map/ppermute | solution.py:40
  131.3 26.4 %collective-permute-start.19 = (bf16[128,2816]{1,0:T(8,128)(2,1)S(1)}, bf16[128,2816]{1,0:T(8,128)(2,1)S(1)}, u32[]{:S(2)}, u32[]{:S(2)}) collective-permute-start(bf16[128,2816]{1,0:T(8,128)(2,1)S(1)} %get-tuple-element.78), channel_id=1, source_target_pairs={{24,16},{26,18},{28,20},{30,22},{16,8},{18,10},{20,12},{22,14},{8,... | collective-permute-start | bytes 2162696 | tf_op jit(solution)/shard_map/ppermute | solution.py:40
  146.6 6.8 %copy-start.9 = (bf16[128,5504]{1,0:T(8,128)(2,1)}, bf16[128,5504]{1,0:T(8,128)(2,1)S(1)}, u32[]{:S(2)}) copy-start(bf16[128,5504]{1,0:T(8,128)(2,1)S(1)} %get-tuple-element.82) | copy-start | bytes 4227076
  146.6 6.8 %copy-start.11 = (bf16[128,5504]{1,0:T(8,128)(2,1)}, bf16[128,5504]{1,0:T(8,128)(2,1)S(1)}, u32[]{:S(2)}) copy-start(bf16[128,5504]{1,0:T(8,128)(2,1)S(1)} %get-tuple-element.83) | copy-start | bytes 4227076
  158.7 11.3 %collective-permute-start.20 = (bf16[5504,512]{1,0:T(8,128)(2,1)}, bf16[5504,512]{1,0:T(8,128)(2,1)}, u32[]{:S(2)}, u32[]{:S(2)}) collective-permute-start(bf16[5504,512]{1,0:T(8,128)(2,1)} %convolution_convert_fusion), channel_id=1, source_target_pairs={{0,2},{2,0},{4,6},{6,4},{8,10},{10,8},{12,14},{14,12},{16,18},{18,... | collective-permute-start | bytes 16908296 | tf_op jit(solution)/shard_map/ppermute | solution.py:32
  158.7 8.1 %copy-start.8 = (bf16[128,5504]{1,0:T(8,128)(2,1)S(1)}, bf16[128,5504]{1,0:T(8,128)(2,1)}, u32[]{:S(2)}) copy-start(bf16[128,5504]{1,0:T(8,128)(2,1)} %copy-done.7) | copy-start | bytes 4227076
  160.4 21.4 %collective-permute-start.22 = (bf16[128,2688]{1,0:T(8,128)(2,1)S(1)}, bf16[128,2688]{1,0:T(8,128)(2,1)S(1)}, u32[]{:S(2)}, u32[]{:S(2)}) collective-permute-start(bf16[128,2688]{1,0:T(8,128)(2,1)S(1)} %get-tuple-element.59), channel_id=1, source_target_pairs={{24,16},{26,18},{28,20},{30,22},{16,8},{18,10},{20,12},{22,14},{25... | collective-permute-start | bytes 2064392 | tf_op jit(solution)/shard_map/ppermute | solution.py:40
  161.7 8.3 %copy-start.10 = (bf16[128,5504]{1,0:T(8,128)(2,1)S(1)}, bf16[128,5504]{1,0:T(8,128)(2,1)}, u32[]{:S(2)}) copy-start(bf16[128,5504]{1,0:T(8,128)(2,1)} %copy-done.9) | copy-start | bytes 4227076
  161.7 8.3 %copy-start.12 = (bf16[128,5504]{1,0:T(8,128)(2,1)S(1)}, bf16[128,5504]{1,0:T(8,128)(2,1)}, u32[]{:S(2)}) copy-start(bf16[128,5504]{1,0:T(8,128)(2,1)} %copy-done.11) | copy-start | bytes 4227076
  161.8 8.3 %copy-start.15 = (bf16[3,128,1024]{2,1,0:T(8,128)(2,1)S(1)}, bf16[3,128,1024]{2,1,0:T(8,128)(2,1)}, u32[]{:S(2)}) copy-start(bf16[3,128,1024]{2,1,0:T(8,128)(2,1)} %copy-done.13) | copy-start | bytes 2359300
  161.8 21.8 %collective-permute-start.21 = (bf16[128,2688]{1,0:T(8,128)(2,1)S(1)}, bf16[128,2688]{1,0:T(8,128)(2,1)S(1)}, u32[]{:S(2)}, u32[]{:S(2)}) collective-permute-start(bf16[128,2688]{1,0:T(8,128)(2,1)S(1)} %get-tuple-element.58), channel_id=1, source_target_pairs={{0,8},{2,10},{4,12},{6,14},{8,16},{10,18},{12,20},{14,22},{1,9},{3... | collective-permute-start | bytes 2064392 | tf_op jit(solution)/shard_map/ppermute | solution.py:40
  170.0 6.4 %copy-start.4 = (bf16[2816,256]{1,0:T(8,128)(2,1)S(1)}, bf16[2816,256]{1,0:T(8,128)(2,1)}, u32[]{:S(2)}) copy-start(bf16[2816,256]{1,0:T(8,128)(2,1)} %copy-done.2) | copy-start | bytes 4325380
  175.0 63.1 %collective-permute-start.27 = (bf16[5504,256]{1,0:T(8,128)(2,1)}, bf16[5504,256]{1,0:T(8,128)(2,1)S(1)}, u32[]{:S(2)}, u32[]{:S(2)}) collective-permute-start(bf16[5504,256]{1,0:T(8,128)(2,1)} %add_convert_fusion), channel_id=1, source_target_pairs={{0,4},{2,6},{4,0},{6,2},{8,12},{10,14},{12,8},{14,10},{16,20},{18,... | collective-permute-start | bytes 8454152 | tf_op jit(solution)/shard_map/ppermute | solution.py:32
  183.6 6.3 %copy-start.1 = (bf16[512,2688]{1,0:T(8,128)(2,1)S(1)}, bf16[512,2688]{1,0:T(8,128)(2,1)}, u32[]{:S(2)}) copy-start(bf16[512,2688]{1,0:T(8,128)(2,1)} %copy-done) | copy-start | bytes 8257540
  189.1 9.7 %copy-start.23 = (bf16[128,2816]{1,0:T(8,128)(2,1)S(1)}, bf16[128,2816]{1,0:T(8,128)(2,1)}, u32[]{:S(2)}) copy-start(bf16[128,2816]{1,0:T(8,128)(2,1)} %copy-done.22) | copy-start | bytes 2162692
  189.2 9.6 %copy-start.5 = (bf16[128,5504]{1,0:T(8,128)(2,1)S(1)}, bf16[128,5504]{1,0:T(8,128)(2,1)}, u32[]{:S(2)}) copy-start(bf16[128,5504]{1,0:T(8,128)(2,1)} %param.5) | copy-start | bytes 4227076
  189.2 9.6 %copy-start.6 = (bf16[128,5504]{1,0:T(8,128)(2,1)S(1)}, bf16[128,5504]{1,0:T(8,128)(2,1)}, u32[]{:S(2)}) copy-start(bf16[128,5504]{1,0:T(8,128)(2,1)} %param.4) | copy-start | bytes 4227076
  189.2 9.6 %copy-start.21 = (bf16[128,2816]{1,0:T(8,128)(2,1)S(1)}, bf16[128,2816]{1,0:T(8,128)(2,1)}, u32[]{:S(2)}) copy-start(bf16[128,2816]{1,0:T(8,128)(2,1)} %copy-done.20) | copy-start | bytes 2162692
  189.2 9.3 %collective-permute-start.23 = (bf16[128,1024]{1,0:T(8,128)(2,1)S(1)}, bf16[128,1024]{1,0:T(8,128)(2,1)S(1)}, u32[]{:S(2)}, u32[]{:S(2)}) collective-permute-start(bf16[128,1024]{1,0:T(8,128)(2,1)S(1)} %get-tuple-element.91), channel_id=1, source_target_pairs={{0,8},{2,10},{4,12},{6,14},{8,16},{10,18},{12,20},{14,22},{16,24},... | collective-permute-start | bytes 786440 | tf_op jit(solution)/shard_map/ppermute | solution.py:36
  190.2 40.2 %collective-permute-start.28 = (bf16[128,2688]{1,0:T(8,128)(2,1)S(1)}, bf16[128,2688]{1,0:T(8,128)(2,1)S(1)}, u32[]{:S(2)}, u32[]{:S(2)}) collective-permute-start(bf16[128,2688]{1,0:T(8,128)(2,1)S(1)} %get-tuple-element.67), channel_id=1, source_target_pairs={{0,8},{2,10},{4,12},{6,14},{8,16},{10,18},{12,20},{14,22},{16,24},... | collective-permute-start | bytes 2064392 | tf_op jit(solution)/shard_map/ppermute | solution.py:40
  192.3 38.2 %collective-permute-start.29 = (bf16[128,2688]{1,0:T(8,128)(2,1)S(1)}, bf16[128,2688]{1,0:T(8,128)(2,1)S(1)}, u32[]{:S(2)}, u32[]{:S(2)}) collective-permute-start(bf16[128,2688]{1,0:T(8,128)(2,1)S(1)} %get-tuple-element.69), channel_id=1, source_target_pairs={{24,16},{26,18},{28,20},{30,22},{16,8},{18,10},{20,12},{22,14},{8,... | collective-permute-start | bytes 2064392 | tf_op jit(solution)/shard_map/ppermute | solution.py:40
  196.2 30.4 %collective-permute-start.24 = (bf16[128,1024]{1,0:T(8,128)(2,1)S(1)}, bf16[128,1024]{1,0:T(8,128)(2,1)S(1)}, u32[]{:S(2)}, u32[]{:S(2)}) collective-permute-start(bf16[128,1024]{1,0:T(8,128)(2,1)S(1)} %get-tuple-element.90), channel_id=1, source_target_pairs={{0,16},{2,18},{4,20},{6,22},{8,24},{10,26},{12,28},{14,30},{16,0},... | collective-permute-start | bytes 786440 | tf_op jit(solution)/shard_map/ppermute | solution.py:36
  198.5 30.3 %collective-permute-start.25 = (bf16[128,1024]{1,0:T(8,128)(2,1)S(1)}, bf16[128,1024]{1,0:T(8,128)(2,1)S(1)}, u32[]{:S(2)}, u32[]{:S(2)}) collective-permute-start(bf16[128,1024]{1,0:T(8,128)(2,1)S(1)} %get-tuple-element.61), channel_id=1, source_target_pairs={{0,24},{2,26},{4,28},{6,30},{8,0},{10,2},{12,4},{14,6},{16,8},{18,... | collective-permute-start | bytes 786440 | tf_op jit(solution)/shard_map/ppermute | solution.py:36
  229.0 14.2 %collective-permute-start.26 = (bf16[128,2048]{1,0:T(8,128)(2,1)S(1)}, bf16[128,2048]{1,0:T(8,128)(2,1)S(1)}, u32[]{:S(2)}, u32[]{:S(2)}) collective-permute-start(bf16[128,2048]{1,0:T(8,128)(2,1)S(1)} %pad_maximum_fusion.20), channel_id=1, source_target_pairs={{0,1},{1,0},{2,3},{3,2},{4,5},{5,4},{6,7},{7,6},{8,9},{9,8},{10,11... | collective-permute-start | bytes 1572872 | tf_op jit(solution)/shard_map/ppermute | solution.py:49
  (10 other events, 27.3 us)

commit v5 on v4

--- a/solution.py
+++ b/solution.py
@@ -131,7 +131,8 @@
         for e in range(1, n_far):
             sent = cot_for(n_far - e, x * block, block)
             came.append(shift(after(sent, *came[: max(0, e - 2)]), n_far - e))
-        fence = waits + came + [weight_side]
+        second_weight = lax.optimization_barrier(down_weight[middle:])
+        fence = waits + came + [weight_side, second_weight]
 
         def whole_rows():
             mine = jnp.concatenate(came, axis=0)
@@ -151,7 +152,7 @@
             if j == 2:
                 cot_rows = whole_rows()
                 weights[0] = weight_columns(0, weight_side)
-                weight_side = move(swap, down_weight[middle:], 2)
+                weight_side = move(swap, second_weight, 2)
                 terms[0] = reduce_terms(0)
                 waits.append(weight_side)
             if j == 3:
@@ -226,7 +227,7 @@
         sides = [local_shift(half_of(step), step) for step in range(1, n_local)]
         output = half_of(0).astype(jnp.float32)
         for side in sides:
-            output = output + after(side, down_grad).astype(jnp.float32)
+            output = output + side.astype(jnp.float32)
         output = output.astype(jnp.bfloat16).reshape(tokens, per_half, QUAD, width)
         return (
             picked(output, slot_of(near), 2).reshape(tokens, half),

time: 249 us -> 257 us (1.032)
  starting transfers between devices: 54.3 us -> 57.7 us
    ppermute x3, waiting for transfers between devices: 1.33 us -> 11.2 us  [local_shift(): lax.ppermute(value, 'local', [(i, (i + step) % n_local) for i in range(n_...]
    ppermute x6, waiting for transfers between devices: 23.8 us -> 17.1 us  [swap(): return lax.ppermute(value, 'hst', [(h, h ^ bit) for h in range(n_hst)])]
    ppermute x15, waiting for transfers between devices: 25.3 us -> 21.3 us  [far_permute(): return lax.ppermute(value, 'hst', pairs)]
    ppermute x15, starting transfers between devices: 41.5 us -> 44.8 us  [far_permute(): return lax.ppermute(value, 'hst', pairs)]
  transfers between devices with their start and end apart: 30 -> 30, of which waited for: 16 -> 13; matrix products, arithmetic and copies ran while one was open for 31% -> 31% of each run, Pallas kernels for 0% -> 0%
where the time goes in v5:
time: 257 us; the launch traced here: 256 us
  waiting for transfers between devices  108 us (42%)
  starting transfers between devices  57.7 us (22%)
  matrix products  37.7 us (15%)
  other arithmetic  37.6 us (15%)
  local copies, waits for them, and re-layouts  13.2 us (5%)
    ppermute x6, waiting for transfers between devices, shift(): return lax.ppermute(value, 'hst', pairs)  58.5 us
    ppermute x15, starting transfers between devices, far_permute(): return lax.ppermute(value, 'hst', pairs)  44.8 us
    ppermute x15, waiting for transfers between devices, far_permute(): return lax.ppermute(value, 'hst', pairs)  21.3 us
    ppermute x6, waiting for transfers between devices, swap(): return lax.ppermute(value, 'hst', [(h, h ^ bit) for h in range(n_hst)])  17.1 us
    dot_general x3, matrix products, grad_terms(): lax.dot_general(rows, part, SUM_ROWS, preferred_element_type=jnp.float32)  15.9 us
    ppermute x3, waiting for transfers between devices, local_shift(): lax.ppermute(value, 'local', [(i, (i + step) % n_local) for i in range(n_...  11.2 us
    dot_general x2, matrix products, reduce_terms(): lax.dot_general(cot_rows, weights[f], KEEP_COLS, preferred_element_type=j...  11 us
    dot_general x2, matrix products, on_device(): jnp.dot(rows[:, lo:hi], weights[f], preferred_element_type=jnp.float32)  10.8 us
  transfers between devices with their start and end apart: 30, of which 13 were waited for; matrix products, arithmetic and copies ran while one was open for 31% of the time, Pallas kernels for 0%

profile of v5, /device:TPU:8, one launch (start us, length us, event | category | flops | bytes accessed | tf_op | source)
XLA Modules:
  0.0 256.0 jit_solution(5944189678312525542)
XLA Ops:
  0.6 1.6 collective-permute-start.2
  2.2 3.7 %fusion.6 = bf16[128,5504]{1,0:T(8,128)(2,1)} fusion(bf16[128,5504]{1,0:T(8,128)(2,1)} %param.5, bf16[128,5504]{1,0:T(8,128)(2,1)} %param.4), kind=kLoop, calls=%fused_computation.17 | loop fusion | flops 5636096 | bytes 4227072 | tf_op jit(solution)/shard_map/convert_element_type | solution.py:69
  6.0 1.6 collective-permute-start.6
  7.6 3.5 %collective-permute-start.1 = (bf16[128,5504]{1,0:T(8,128)(2,1)}, bf16[128,5504]{1,0:T(8,128)(2,1)}, u32[]{:S(2)}, u32[]{:S(2)}) collective-permute-start(bf16[128,5504]{1,0:T(8,128)(2,1)} %fusion.6), channel_id=1, source_target_pairs={{0,8},{2,10},{4,12},{6,14},{8,16},{10,18},{12,20},{14,22},{16,24},... | collective-permute-start | bytes 4227080 | tf_op jit(solution)/shard_map/ppermute | solution.py:40
  11.1 3.4 %collective-permute-start = (bf16[128,5504]{1,0:T(8,128)(2,1)}, bf16[128,5504]{1,0:T(8,128)(2,1)}, u32[]{:S(2)}, u32[]{:S(2)}) collective-permute-start(bf16[128,5504]{1,0:T(8,128)(2,1)} %fusion.6), channel_id=1, source_target_pairs={{24,16},{26,18},{28,20},{30,22},{16,8},{18,10},{20,12},{22,14},{8,... | collective-permute-start | bytes 4227080 | tf_op jit(solution)/shard_map/ppermute | solution.py:40
  15.7 2.2 constant_dynamic-slice_fusion.15
  17.9 2.4 pad_maximum_fusion.15
  21.7 2.5 slice.78
  24.3 2.9 %collective-permute-start.4 = (bf16[64,1024]{1,0:T(8,128)(2,1)S(1)}, bf16[64,1024]{1,0:T(8,128)(2,1)S(1)}, u32[]{:S(2)}, u32[]{:S(2)}) collective-permute-start(bf16[64,1024]{1,0:T(8,128)(2,1)S(1)} %bitcast.29), channel_id=1, source_target_pairs={{0,16},{2,18},{4,20},{6,22},{8,24},{10,26},{12,28},{14,30},{16,0},... | collective-permute-start | bytes 393224 | tf_op jit(solution)/shard_map/ppermute | solution.py:36
  27.2 26.2 %collective-permute-done.3 = bf16[64,1024]{1,0:T(8,128)(2,1)S(1)} collective-permute-done((bf16[64,1024]{1,0:T(8,128)(2,1)S(1)}, bf16[64,1024]{1,0:T(8,128)(2,1)S(1)}, u32[]{:S(2)}, u32[]{:S(2)}) %collective-permute-start.3) | collective-permute-done | bytes 131104 | tf_op jit(solution)/shard_map/ppermute | solution.py:36
  53.4 3.2 %pad_maximum_fusion.3 = bf16[2816,512]{1,0:T(8,128)(2,1)} fusion(bf16[2816,256]{1,0:T(8,128)(2,1)} %collective-permute-done.6, bf16[2816,256]{1,0:T(8,128)(2,1)S(1)} %slice.77), kind=kLoop, calls=%fused_computation.10 | loop fusion | flops 5767168 | bytes 5767168 | tf_op jit(solution)/shard_map/concatenate | solution.py:104
  56.6 1.8 collective-permute-done.5
  60.4 2.2 collective-permute-start.7
  62.6 5.9 %collective-permute-start.8 = (bf16[128,5504]{1,0:T(8,128)(2,1)}, bf16[128,5504]{1,0:T(8,128)(2,1)}, u32[]{:S(2)}, u32[]{:S(2)}) collective-permute-start(bf16[128,5504]{1,0:T(8,128)(2,1)} %collective-permute-done.1), channel_id=1, source_target_pairs={{8,16},{10,18},{12,20},{14,22},{16,24},{18,26},{20,28},{22,30},{9,... | collective-permute-start | bytes 4227080 | tf_op jit(solution)/shard_map/ppermute | solution.py:40
  68.5 1.5 collective-permute-done.10
  70.2 5.7 %convolution_convert_fusion.2 = bf16[512,2816]{1,0:T(8,128)(2,1)S(1)} fusion(bf16[2816,512]{1,0:T(8,128)(2,1)} %collective-permute-done.11, bf16[2816,256]{1,0:T(8,128)(2,1)} %collective-permute-done.6, bf16[2816,256]{1,0:T(8,128)(2,1)S(1)} %copy-done.3, bf16[128,1024]{1,0:T(8,128)(2,1)S(1)} %bitcast.23, bf16[384,1024]{1,0:T(8,128)(2,1)S(1)} %bitcast.16), kind=kOutput, calls=%fused_computation.7 | convolution fusion | flops 2973630464 | bytes 9699328 | tf_op jit(solution)/shard_map/dot_general | solution.py:109
  77.3 15.2 %collective-permute-done.9 = bf16[2688,256]{1,0:T(8,128)(2,1)S(1)} collective-permute-done((bf16[2688,256]{1,0:T(8,128)(2,1)}, bf16[2688,256]{1,0:T(8,128)(2,1)S(1)}, u32[]{:S(2)}, u32[]{:S(2)}) %collective-permute-start.9) | collective-permute-done | bytes 1376288 | tf_op jit(solution)/shard_map/ppermute | solution.py:32
  92.4 3.6 %pad_maximum_fusion.4 = bf16[2688,512]{1,0:T(8,128)(2,1)} fusion(bf16[2688,256]{1,0:T(8,128)(2,1)S(1)} %collective-permute-done.9, bf16[2688,256]{1,0:T(8,128)(2,1)} %slice.78), kind=kLoop, calls=%fused_computation.18 | loop fusion | flops 5505024 | bytes 5505024 | tf_op jit(solution)/shard_map/concatenate | solution.py:104
  96.0 1.7 collective-permute-done.8
  98.6 1.6 broadcast_select_fusion.3
  102.1 2.0 collective-permute-done.14
  104.0 4.4 %collective-permute-start.15 = (bf16[128,2816]{1,0:T(8,128)(2,1)S(1)}, bf16[128,2816]{1,0:T(8,128)(2,1)S(1)}, u32[]{:S(2)}, u32[]{:S(2)}) collective-permute-start(bf16[128,2816]{1,0:T(8,128)(2,1)S(1)} %get-tuple-element.46), channel_id=1, source_target_pairs={{0,8},{2,10},{4,12},{6,14},{8,16},{10,18},{12,20},{14,22},{1,9},{3... | collective-permute-start | bytes 2162696 | tf_op jit(solution)/shard_map/ppermute | solution.py:40
  109.7 5.4 %convolution_convert_fusion.1 = bf16[512,2688]{1,0:T(8,128)(2,1)S(1)} fusion(bf16[2688,512]{1,0:T(8,128)(2,1)} %collective-permute-done.14, bf16[2688,256]{1,0:T(8,128)(2,1)S(1)} %copy-done.18, bf16[2688,256]{1,0:T(8,128)(2,1)} %slice.78, bf16[128,1024]{1,0:T(8,128)(2,1)S(1)} %bitcast.24, bf16[384,1024]{1,0:T(8,128)(2,1)S(1)} %bitcast.17), kind=kOutput, calls=%fused_computation.6 | convolution fusion | flops 2838560768 | bytes 9306112 | tf_op jit(solution)/shard_map/dot_general | solution.py:109
  116.5 8.4 %collective-permute-done.15 = bf16[128,2816]{1,0:T(8,128)(2,1)S(1)} collective-permute-done((bf16[128,2816]{1,0:T(8,128)(2,1)S(1)}, bf16[128,2816]{1,0:T(8,128)(2,1)S(1)}, u32[]{:S(2)}, u32[]{:S(2)}) %collective-permute-start.15) | collective-permute-done | bytes 720928 | tf_op jit(solution)/shard_map/ppermute | solution.py:40
  124.9 3.3 %collective-permute-done.16 = bf16[128,2816]{1,0:T(8,128)(2,1)S(1)} collective-permute-done((bf16[128,2816]{1,0:T(8,128)(2,1)S(1)}, bf16[128,2816]{1,0:T(8,128)(2,1)S(1)}, u32[]{:S(2)}, u32[]{:S(2)}) %collective-permute-start.16) | collective-permute-done | bytes 720928 | tf_op jit(solution)/shard_map/ppermute | solution.py:40
  128.6 1.9 collective-permute-start.19
  130.5 3.9 %collective-permute-start.18 = (bf16[128,2816]{1,0:T(8,128)(2,1)S(1)}, bf16[128,2816]{1,0:T(8,128)(2,1)S(1)}, u32[]{:S(2)}, u32[]{:S(2)}) collective-permute-start(bf16[128,2816]{1,0:T(8,128)(2,1)S(1)} %get-tuple-element.77), channel_id=1, source_target_pairs={{0,8},{2,10},{4,12},{6,14},{8,16},{10,18},{12,20},{14,22},{16,24},... | collective-permute-start | bytes 2162696 | tf_op jit(solution)/shard_map/ppermute | solution.py:40
  134.4 5.2 %collective-permute-done.17 = bf16[128,2688]{1,0:T(8,128)(2,1)S(1)} collective-permute-done((bf16[128,2688]{1,0:T(8,128)(2,1)S(1)}, bf16[128,2688]{1,0:T(8,128)(2,1)S(1)}, u32[]{:S(2)}, u32[]{:S(2)}) %collective-permute-start.17) | collective-permute-done | bytes 688160 | tf_op jit(solution)/shard_map/ppermute | solution.py:40
  139.6 1.8 broadcast_select_fusion.1
  141.4 2.6 %broadcast_select_fusion.2 = (bf16[128,5504]{1,0:T(8,128)(2,1)S(1)}, bf16[128,5504]{1,0:T(8,128)(2,1)S(1)}) fusion(bf16[128,5504]{1,0:T(8,128)(2,1)} %collective-permute-done, bf16[128,5504]{1,0:T(8,128)(2,1)S(1)} %collective-permute-done.13, pred[]{:T(512)S(6)} %lt.176, bf16[128,5504]{1,0:T(8,128)(2,1)} %collective-permute-done.1, pred[]{:T(512)S(6)} %lt.178), kind=kLoop, calls=%fused_computation.52 | loop fusion | flops 1409024 | bytes 7045122 | tf_op jit(solution)/shard_map/jit(_where)/select_n | solution.py:174
  144.0 6.8 %convolution_convert_fusion = bf16[5504,512]{1,0:T(8,128)(2,1)} fusion(bf16[384,1024]{1,0:T(8,128)(2,1)S(1)} %bitcast.18, bf16[128,1024]{1,0:T(8,128)(2,1)S(1)} %bitcast.25, bf16[128,5504]{1,0:T(8,128)(2,1)S(1)} %get-tuple-element.81, bf16[128,5504]{1,0:T(8,128)(2,1)S(1)} %broadcast_select_fusion.1, bf16[128,5504]{1,0:T(8,128)(2,1)S(1)} %get-tuple-element.80, ...), kind=kOutput, calls=%fused_computation | convolution fusion | flops 2912092160 | bytes 12320768 | tf_op jit(solution)/shard_map/dot_general | solution.py:179
  151.7 2.6 %collective-permute-done.18 = bf16[128,2816]{1,0:T(8,128)(2,1)S(1)} collective-permute-done((bf16[128,2816]{1,0:T(8,128)(2,1)S(1)}, bf16[128,2816]{1,0:T(8,128)(2,1)S(1)}, u32[]{:S(2)}, u32[]{:S(2)}) %collective-permute-start.18) | collective-permute-done | bytes 720928 | tf_op jit(solution)/shard_map/ppermute | solution.py:40
  155.2 1.7 fusion.22
  157.0 6.8 %collective-permute-start.21 = (bf16[128,2688]{1,0:T(8,128)(2,1)S(1)}, bf16[128,2688]{1,0:T(8,128)(2,1)S(1)}, u32[]{:S(2)}, u32[]{:S(2)}) collective-permute-start(bf16[128,2688]{1,0:T(8,128)(2,1)S(1)} %get-tuple-element.57), channel_id=1, source_target_pairs={{0,8},{2,10},{4,12},{6,14},{8,16},{10,18},{12,20},{14,22},{1,9},{3... | collective-permute-start | bytes 2064392 | tf_op jit(solution)/shard_map/ppermute | solution.py:40
  163.8 1.5 collective-permute-start.22
  165.3 3.2 %pad_maximum_fusion.1 = bf16[512,5504]{1,0:T(8,128)(2,1)S(1)} fusion(bf16[128,5504]{1,0:T(8,128)(2,1)} %copy-done.11, bf16[128,5504]{1,0:T(8,128)(2,1)S(1)} %copy-done.8, bf16[128,5504]{1,0:T(8,128)(2,1)} %copy-done.9, bf16[128,5504]{1,0:T(8,128)(2,1)} %fusion.6), kind=kLoop, calls=%fused_computation.2 | loop fusion | flops 22544384 | bytes 11272192 | tf_op jit(solution)/shard_map/concatenate | solution.py:175
  168.6 5.0 %add_convert_fusion = bf16[5504,256]{1,0:T(8,128)(2,1)} fusion(bf16[5504,512]{1,0:T(8,128)(2,1)} %collective-permute-done.20, bf16[384,1024]{1,0:T(8,128)(2,1)S(1)} %bitcast.19, bf16[128,1024]{1,0:T(8,128)(2,1)S(1)} %bitcast.26, bf16[128,5504]{1,0:T(8,128)(2,1)S(1)} %copy-done.12, bf16[128,5504]{1,0:T(8,128)(2,1)S(1)} %copy-done.8, ...), kind=kOutput, calls=%fused_computation.4 | convolution fusion | flops 1470136320 | bytes 12320768 | tf_op jit(solution)/shard_map/dot_general | solution.py:179
  174.9 5.4 %fusion = f32[512,1024]{1,0:T(8,128)S(1)} fusion(bf16[512,5504]{1,0:T(8,128)(2,1)S(1)} %pad_maximum_fusion.1, bf16[2816,512]{1,0:T(8,128)(2,1)} %collective-permute-done.11, bf16[2816,256]{1,0:T(8,128)(2,1)} %collective-permute-done.6, bf16[2816,256]{1,0:T(8,128)(2,1)S(1)} %copy-done.4), kind=kOutput, calls=%fused_computation.11 | convolution fusion | flops 2970091520 | bytes 10747904 | tf_op jit(solution)/shard_map/dot_general | solution.py:190
  180.4 5.4 %add_convert_fusion.1 = bf16[512,1024]{1,0:T(8,128)(2,1)S(1)} fusion(f32[512,1024]{1,0:T(8,128)S(1)} %fusion, bf16[2688,512]{1,0:T(8,128)(2,1)} %collective-permute-done.14, bf16[2688,256]{1,0:T(8,128)(2,1)S(1)} %copy-done.19, bf16[2688,256]{1,0:T(8,128)(2,1)} %slice.78, bf16[512,5504]{1,0:T(8,128)(2,1)S(1)} %pad_maximum_fusion.1), kind=kOutput, calls=%fused_computation.24 | convolution fusion | flops 2836135936 | bytes 11403264 | tf_op jit(solution)/shard_map/dot_general | solution.py:190
  185.8 4.2 %fusion.34 = f32[5504,256]{1,0:T(8,128)} fusion(bf16[512,5504]{1,0:T(8,128)(2,1)S(1)} %pad_maximum_fusion.1, bf16[384,1024]{1,0:T(8,128)(2,1)S(1)} %bitcast.20, bf16[128,1024]{1,0:T(8,128)(2,1)S(1)} %bitcast.27), kind=kOutput, calls=%fused_computation.82 | convolution fusion | flops 1443364864 | bytes 12320768 | tf_op jit(solution)/shard_map/dot_general | solution.py:179
  190.1 1.6 collective-permute-start.24
  193.2 3.3 %collective-permute-start.28 = (bf16[128,2688]{1,0:T(8,128)(2,1)S(1)}, bf16[128,2688]{1,0:T(8,128)(2,1)S(1)}, u32[]{:S(2)}, u32[]{:S(2)}) collective-permute-start(bf16[128,2688]{1,0:T(8,128)(2,1)S(1)} %get-tuple-element.66), channel_id=1, source_target_pairs={{24,16},{26,18},{28,20},{30,22},{16,8},{18,10},{20,12},{22,14},{8,... | collective-permute-start | bytes 2064392 | tf_op jit(solution)/shard_map/ppermute | solution.py:40
  196.5 2.5 collective-permute-start.27
  199.0 10.6 %collective-permute-done.23 = bf16[128,1024]{1,0:T(8,128)(2,1)S(1)} collective-permute-done((bf16[128,1024]{1,0:T(8,128)(2,1)S(1)}, bf16[128,1024]{1,0:T(8,128)(2,1)S(1)}, u32[]{:S(2)}, u32[]{:S(2)}) %collective-permute-start.23) | collective-permute-done | bytes 262176 | tf_op jit(solution)/shard_map/ppermute | solution.py:36
  210.6 19.9 %collective-permute-done.25 = bf16[128,1024]{1,0:T(8,128)(2,1)S(1)} collective-permute-done((bf16[128,1024]{1,0:T(8,128)(2,1)S(1)}, bf16[128,1024]{1,0:T(8,128)(2,1)S(1)}, u32[]{:S(2)}, u32[]{:S(2)}) %collective-permute-start.25) | collective-permute-done | bytes 262176 | tf_op jit(solution)/shard_map/ppermute | solution.py:36
  233.1 1.7 pad_maximum_fusion.12
  234.8 9.7 %collective-permute-done.26 = bf16[128,2048]{1,0:T(8,128)(2,1)S(1)} collective-permute-done((bf16[128,2048]{1,0:T(8,128)(2,1)S(1)}, bf16[128,2048]{1,0:T(8,128)(2,1)S(1)}, u32[]{:S(2)}, u32[]{:S(2)}) %collective-permute-start.26) | collective-permute-done | bytes 524320 | tf_op jit(solution)/shard_map/ppermute | solution.py:49
  248.5 7.5 %convert_add_fusion = f32[5504,256]{1,0:T(8,128)} fusion(bf16[5504,256]{1,0:T(8,128)(2,1)} %collective-permute-done.29, f32[5504,256]{1,0:T(8,128)} %fusion.34, bf16[5504,512]{1,0:T(8,128)(2,1)} %collective-permute-done.20), kind=kLoop, calls=%fused_computation.3 | loop fusion | flops 5636096 | bytes 16908288 | tf_op jit(solution)/shard_map/add | solution.py:187
  (119 shorter events, 24.0 us)
Async XLA Ops:
  0.6 14.1 %collective-permute-start.2 = (bf16[128,2048]{1,0:T(8,128)(2,1)}, bf16[128,2048]{1,0:T(8,128)(2,1)S(1)}, u32[]{:S(2)}, u32[]{:S(2)}) collective-permute-start(bf16[128,2048]{1,0:T(8,128)(2,1)} %param.6), channel_id=1, source_target_pairs={{0,1},{1,0},{2,3},{3,2},{4,5},{5,4},{6,7},{7,6},{8,9},{9,8},{10,11... | collective-permute-start | bytes 1572872 | tf_op jit(solution)/shard_map/ppermute | solution.py:49
  5.9 8.9 %copy-start.27 = (bf16[128,2048]{1,0:T(8,128)(2,1)S(1)}, bf16[128,2048]{1,0:T(8,128)(2,1)}, u32[]{:S(2)}) copy-start(bf16[128,2048]{1,0:T(8,128)(2,1)} %param.6) | copy-start | bytes 1572868
  6.0 47.4 %copy-start.2 = (bf16[2816,256]{1,0:T(8,128)(2,1)}, bf16[2816,256]{1,0:T(8,128)(2,1)S(1)}, u32[]{:S(2)}) copy-start(bf16[2816,256]{1,0:T(8,128)(2,1)S(1)} %slice.77) | copy-start | bytes 4325380
  6.0 47.4 %collective-permute-start.6 = (bf16[2816,256]{1,0:T(8,128)(2,1)S(1)}, bf16[2816,256]{1,0:T(8,128)(2,1)}, u32[]{:S(2)}, u32[]{:S(2)}) collective-permute-start(bf16[2816,256]{1,0:T(8,128)(2,1)S(1)} %slice.77), channel_id=1, source_target_pairs={{0,4},{2,6},{4,0},{6,2},{8,12},{10,14},{12,8},{14,10},{16,20},{18,... | collective-permute-start | bytes 4325384 | tf_op jit(solution)/shard_map/ppermute | solution.py:32
  7.6 50.8 %collective-permute-start.1 = (bf16[128,5504]{1,0:T(8,128)(2,1)}, bf16[128,5504]{1,0:T(8,128)(2,1)}, u32[]{:S(2)}, u32[]{:S(2)}) collective-permute-start(bf16[128,5504]{1,0:T(8,128)(2,1)} %fusion.6), channel_id=1, source_target_pairs={{0,8},{2,10},{4,12},{6,14},{8,16},{10,18},{12,20},{14,22},{16,24},... | collective-permute-start | bytes 4227080 | tf_op jit(solution)/shard_map/ppermute | solution.py:40
  11.1 47.3 %collective-permute-start = (bf16[128,5504]{1,0:T(8,128)(2,1)}, bf16[128,5504]{1,0:T(8,128)(2,1)}, u32[]{:S(2)}, u32[]{:S(2)}) collective-permute-start(bf16[128,5504]{1,0:T(8,128)(2,1)} %fusion.6), channel_id=1, source_target_pairs={{24,16},{26,18},{28,20},{30,22},{16,8},{18,10},{20,12},{22,14},{8,... | collective-permute-start | bytes 4227080 | tf_op jit(solution)/shard_map/ppermute | solution.py:40
  21.6 31.7 %collective-permute-start.3 = (bf16[64,1024]{1,0:T(8,128)(2,1)S(1)}, bf16[64,1024]{1,0:T(8,128)(2,1)S(1)}, u32[]{:S(2)}, u32[]{:S(2)}) collective-permute-start(bf16[64,1024]{1,0:T(8,128)(2,1)S(1)} %bitcast.30), channel_id=1, source_target_pairs={{0,24},{2,26},{4,28},{6,30},{8,0},{10,2},{12,4},{14,6},{16,8},{18,... | collective-permute-start | bytes 393224 | tf_op jit(solution)/shard_map/ppermute | solution.py:36
  24.3 32.2 %collective-permute-start.4 = (bf16[64,1024]{1,0:T(8,128)(2,1)S(1)}, bf16[64,1024]{1,0:T(8,128)(2,1)S(1)}, u32[]{:S(2)}, u32[]{:S(2)}) collective-permute-start(bf16[64,1024]{1,0:T(8,128)(2,1)S(1)} %bitcast.29), channel_id=1, source_target_pairs={{0,16},{2,18},{4,20},{6,22},{8,24},{10,26},{12,28},{14,30},{16,0},... | collective-permute-start | bytes 393224 | tf_op jit(solution)/shard_map/ppermute | solution.py:36
  53.4 5.0 %collective-permute-start.5 = (bf16[64,1024]{1,0:T(8,128)(2,1)S(1)}, bf16[64,1024]{1,0:T(8,128)(2,1)S(1)}, u32[]{:S(2)}, u32[]{:S(2)}) collective-permute-start(bf16[64,1024]{1,0:T(8,128)(2,1)S(1)} %bitcast.28), channel_id=1, source_target_pairs={{0,8},{2,10},{4,12},{6,14},{8,16},{10,18},{12,20},{14,22},{16,24},... | collective-permute-start | bytes 393224 | tf_op jit(solution)/shard_map/ppermute | solution.py:36
  58.4 11.8 %collective-permute-start.11 = (bf16[2816,512]{1,0:T(8,128)(2,1)}, bf16[2816,512]{1,0:T(8,128)(2,1)}, u32[]{:S(2)}, u32[]{:S(2)}) collective-permute-start(bf16[2816,512]{1,0:T(8,128)(2,1)} %pad_maximum_fusion.3), channel_id=1, source_target_pairs={{0,2},{2,0},{4,6},{6,4},{8,10},{10,8},{12,14},{14,12},{16,18},{18,... | collective-permute-start | bytes 8650760 | tf_op jit(solution)/shard_map/ppermute | solution.py:32
  58.4 11.6 %collective-permute-start.10 = (bf16[192,1024]{1,0:T(8,128)(2,1)S(1)}, bf16[192,1024]{1,0:T(8,128)(2,1)S(1)}, u32[]{:S(2)}, u32[]{:S(2)}) collective-permute-start(bf16[192,1024]{1,0:T(8,128)(2,1)S(1)} %constant_dynamic-update-slice_fusion), channel_id=1, source_target_pairs={{0,1},{1,0},{2,3},{3,2},{4,5},{5,4},{6,7},{7,6},{8,9},{9,8},{10,11... | collective-permute-start | bytes 1179656 | tf_op jit(solution)/shard_map/ppermute | solution.py:49
  59.7 10.4 %copy-start.3 = (bf16[2816,256]{1,0:T(8,128)(2,1)S(1)}, bf16[2816,256]{1,0:T(8,128)(2,1)}, u32[]{:S(2)}) copy-start(bf16[2816,256]{1,0:T(8,128)(2,1)} %copy-done.2) | copy-start | bytes 4325380
  59.8 32.6 %collective-permute-start.9 = (bf16[2688,256]{1,0:T(8,128)(2,1)}, bf16[2688,256]{1,0:T(8,128)(2,1)S(1)}, u32[]{:S(2)}, u32[]{:S(2)}) collective-permute-start(bf16[2688,256]{1,0:T(8,128)(2,1)} %slice.78), channel_id=1, source_target_pairs={{0,4},{2,6},{4,0},{6,2},{8,12},{10,14},{12,8},{14,10},{16,20},{18,... | collective-permute-start | bytes 4128776 | tf_op jit(solution)/shard_map/ppermute | solution.py:32
  60.4 35.6 %collective-permute-start.7 = (bf16[128,5504]{1,0:T(8,128)(2,1)}, bf16[128,5504]{1,0:T(8,128)(2,1)}, u32[]{:S(2)}, u32[]{:S(2)}) collective-permute-start(bf16[128,5504]{1,0:T(8,128)(2,1)} %collective-permute-done), channel_id=1, source_target_pairs={{16,8},{18,10},{20,12},{22,14},{8,0},{10,2},{12,4},{14,6},{17,9},{... | collective-permute-start | bytes 4227080 | tf_op jit(solution)/shard_map/ppermute | solution.py:40
  62.6 35.1 %collective-permute-start.8 = (bf16[128,5504]{1,0:T(8,128)(2,1)}, bf16[128,5504]{1,0:T(8,128)(2,1)}, u32[]{:S(2)}, u32[]{:S(2)}) collective-permute-start(bf16[128,5504]{1,0:T(8,128)(2,1)} %collective-permute-done.1), channel_id=1, source_target_pairs={{8,16},{10,18},{12,20},{14,22},{16,24},{18,26},{20,28},{22,30},{9,... | collective-permute-start | bytes 4227080 | tf_op jit(solution)/shard_map/ppermute | solution.py:40
  76.0 21.8 %collective-permute-start.12 = (bf16[128,2816]{1,0:T(8,128)(2,1)S(1)}, bf16[128,2816]{1,0:T(8,128)(2,1)S(1)}, u32[]{:S(2)}, u32[]{:S(2)}) collective-permute-start(bf16[128,2816]{1,0:T(8,128)(2,1)S(1)} %broadcast_select_fusion.4), channel_id=1, source_target_pairs={{0,8},{2,10},{4,12},{6,14},{24,16},{26,18},{28,20},{30,22},{1,9},{... | collective-permute-start | bytes 2162696 | tf_op jit(solution)/shard_map/ppermute | solution.py:40
  98.6 5.4 %collective-permute-start.14 = (bf16[2688,512]{1,0:T(8,128)(2,1)}, bf16[2688,512]{1,0:T(8,128)(2,1)}, u32[]{:S(2)}, u32[]{:S(2)}) collective-permute-start(bf16[2688,512]{1,0:T(8,128)(2,1)} %pad_maximum_fusion.4), channel_id=1, source_target_pairs={{0,2},{2,0},{4,6},{6,4},{8,10},{10,8},{12,14},{14,12},{16,18},{18,... | collective-permute-start | bytes 8257544 | tf_op jit(solution)/shard_map/ppermute | solution.py:32
  100.2 9.5 %copy-start.14 = (bf16[3,128,1024]{2,1,0:T(8,128)(2,1)S(1)}, bf16[3,128,1024]{2,1,0:T(8,128)(2,1)}, u32[]{:S(2)}) copy-start(bf16[3,128,1024]{2,1,0:T(8,128)(2,1)} %copy-done.13) | copy-start | bytes 2359300
  100.2 9.5 %copy-start.18 = (bf16[2688,256]{1,0:T(8,128)(2,1)S(1)}, bf16[2688,256]{1,0:T(8,128)(2,1)}, u32[]{:S(2)}) copy-start(bf16[2688,256]{1,0:T(8,128)(2,1)} %copy-done.17) | copy-start | bytes 4128772
  100.2 34.2 %collective-permute-start.13 = (bf16[128,5504]{1,0:T(8,128)(2,1)S(1)}, bf16[128,5504]{1,0:T(8,128)(2,1)S(1)}, u32[]{:S(2)}, u32[]{:S(2)}) collective-permute-start(bf16[128,5504]{1,0:T(8,128)(2,1)S(1)} %broadcast_select_fusion.3), channel_id=1, source_target_pairs={{16,24},{18,26},{20,28},{22,30},{8,0},{10,2},{12,4},{14,6},{17,25}... | collective-permute-start | bytes 4227080 | tf_op jit(solution)/shard_map/ppermute | solution.py:40
  104.0 20.9 %collective-permute-start.15 = (bf16[128,2816]{1,0:T(8,128)(2,1)S(1)}, bf16[128,2816]{1,0:T(8,128)(2,1)S(1)}, u32[]{:S(2)}, u32[]{:S(2)}) collective-permute-start(bf16[128,2816]{1,0:T(8,128)(2,1)S(1)} %get-tuple-element.46), channel_id=1, source_target_pairs={{0,8},{2,10},{4,12},{6,14},{8,16},{10,18},{12,20},{14,22},{1,9},{3... | collective-permute-start | bytes 2162696 | tf_op jit(solution)/shard_map/ppermute | solution.py:40
  108.4 19.8 %collective-permute-start.16 = (bf16[128,2816]{1,0:T(8,128)(2,1)S(1)}, bf16[128,2816]{1,0:T(8,128)(2,1)S(1)}, u32[]{:S(2)}, u32[]{:S(2)}) collective-permute-start(bf16[128,2816]{1,0:T(8,128)(2,1)S(1)} %get-tuple-element.47), channel_id=1, source_target_pairs={{24,16},{26,18},{28,20},{30,22},{16,8},{18,10},{20,12},{22,14},{25... | collective-permute-start | bytes 2162696 | tf_op jit(solution)/shard_map/ppermute | solution.py:40
  115.1 13.4 %copy-start = (bf16[512,2688]{1,0:T(8,128)(2,1)}, bf16[512,2688]{1,0:T(8,128)(2,1)S(1)}, u32[]{:S(2)}) copy-start(bf16[512,2688]{1,0:T(8,128)(2,1)S(1)} %convolution_convert_fusion.1) | copy-start | bytes 8257540
  115.2 24.4 %collective-permute-start.17 = (bf16[128,2688]{1,0:T(8,128)(2,1)S(1)}, bf16[128,2688]{1,0:T(8,128)(2,1)S(1)}, u32[]{:S(2)}, u32[]{:S(2)}) collective-permute-start(bf16[128,2688]{1,0:T(8,128)(2,1)S(1)} %broadcast_select_fusion.5), channel_id=1, source_target_pairs={{0,8},{2,10},{4,12},{6,14},{24,16},{26,18},{28,20},{30,22},{1,9},{... | collective-permute-start | bytes 2064392 | tf_op jit(solution)/shard_map/ppermute | solution.py:40
  128.6 22.2 %collective-permute-start.19 = (bf16[128,2816]{1,0:T(8,128)(2,1)S(1)}, bf16[128,2816]{1,0:T(8,128)(2,1)S(1)}, u32[]{:S(2)}, u32[]{:S(2)}) collective-permute-start(bf16[128,2816]{1,0:T(8,128)(2,1)S(1)} %get-tuple-element.76), channel_id=1, source_target_pairs={{24,16},{26,18},{28,20},{30,22},{16,8},{18,10},{20,12},{22,14},{8,... | collective-permute-start | bytes 2162696 | tf_op jit(solution)/shard_map/ppermute | solution.py:40
  130.5 23.8 %collective-permute-start.18 = (bf16[128,2816]{1,0:T(8,128)(2,1)S(1)}, bf16[128,2816]{1,0:T(8,128)(2,1)S(1)}, u32[]{:S(2)}, u32[]{:S(2)}) collective-permute-start(bf16[128,2816]{1,0:T(8,128)(2,1)S(1)} %get-tuple-element.77), channel_id=1, source_target_pairs={{0,8},{2,10},{4,12},{6,14},{8,16},{10,18},{12,20},{14,22},{16,24},... | collective-permute-start | bytes 2162696 | tf_op jit(solution)/shard_map/ppermute | solution.py:40
  144.0 6.8 %copy-start.9 = (bf16[128,5504]{1,0:T(8,128)(2,1)}, bf16[128,5504]{1,0:T(8,128)(2,1)S(1)}, u32[]{:S(2)}) copy-start(bf16[128,5504]{1,0:T(8,128)(2,1)S(1)} %get-tuple-element.80) | copy-start | bytes 4227076
  144.0 6.8 %copy-start.11 = (bf16[128,5504]{1,0:T(8,128)(2,1)}, bf16[128,5504]{1,0:T(8,128)(2,1)S(1)}, u32[]{:S(2)}) copy-start(bf16[128,5504]{1,0:T(8,128)(2,1)S(1)} %get-tuple-element.81) | copy-start | bytes 4227076
  155.2 13.3 %collective-permute-start.20 = (bf16[5504,512]{1,0:T(8,128)(2,1)}, bf16[5504,512]{1,0:T(8,128)(2,1)}, u32[]{:S(2)}, u32[]{:S(2)}) collective-permute-start(bf16[5504,512]{1,0:T(8,128)(2,1)} %convolution_convert_fusion), channel_id=1, source_target_pairs={{0,2},{2,0},{4,6},{6,4},{8,10},{10,8},{12,14},{14,12},{16,18},{18,... | collective-permute-start | bytes 16908296 | tf_op jit(solution)/shard_map/ppermute | solution.py:32
  155.2 10.1 %copy-start.8 = (bf16[128,5504]{1,0:T(8,128)(2,1)S(1)}, bf16[128,5504]{1,0:T(8,128)(2,1)}, u32[]{:S(2)}) copy-start(bf16[128,5504]{1,0:T(8,128)(2,1)} %copy-done.7) | copy-start | bytes 4227076
  156.9 11.6 %copy-start.10 = (bf16[128,5504]{1,0:T(8,128)(2,1)S(1)}, bf16[128,5504]{1,0:T(8,128)(2,1)}, u32[]{:S(2)}) copy-start(bf16[128,5504]{1,0:T(8,128)(2,1)} %copy-done.9) | copy-start | bytes 4227076
  156.9 11.6 %copy-start.12 = (bf16[128,5504]{1,0:T(8,128)(2,1)S(1)}, bf16[128,5504]{1,0:T(8,128)(2,1)}, u32[]{:S(2)}) copy-start(bf16[128,5504]{1,0:T(8,128)(2,1)} %copy-done.11) | copy-start | bytes 4227076
  156.9 11.6 %copy-start.15 = (bf16[3,128,1024]{2,1,0:T(8,128)(2,1)S(1)}, bf16[3,128,1024]{2,1,0:T(8,128)(2,1)}, u32[]{:S(2)}) copy-start(bf16[3,128,1024]{2,1,0:T(8,128)(2,1)} %copy-done.13) | copy-start | bytes 2359300
  157.0 33.0 %collective-permute-start.21 = (bf16[128,2688]{1,0:T(8,128)(2,1)S(1)}, bf16[128,2688]{1,0:T(8,128)(2,1)S(1)}, u32[]{:S(2)}, u32[]{:S(2)}) collective-permute-start(bf16[128,2688]{1,0:T(8,128)(2,1)S(1)} %get-tuple-element.57), channel_id=1, source_target_pairs={{0,8},{2,10},{4,12},{6,14},{8,16},{10,18},{12,20},{14,22},{1,9},{3... | collective-permute-start | bytes 2064392 | tf_op jit(solution)/shard_map/ppermute | solution.py:40
  163.8 26.1 %collective-permute-start.22 = (bf16[128,2688]{1,0:T(8,128)(2,1)S(1)}, bf16[128,2688]{1,0:T(8,128)(2,1)S(1)}, u32[]{:S(2)}, u32[]{:S(2)}) collective-permute-start(bf16[128,2688]{1,0:T(8,128)(2,1)S(1)} %get-tuple-element.58), channel_id=1, source_target_pairs={{24,16},{26,18},{28,20},{30,22},{16,8},{18,10},{20,12},{22,14},{25... | collective-permute-start | bytes 2064392 | tf_op jit(solution)/shard_map/ppermute | solution.py:40
  173.5 6.8 %copy-start.19 = (bf16[2688,256]{1,0:T(8,128)(2,1)S(1)}, bf16[2688,256]{1,0:T(8,128)(2,1)}, u32[]{:S(2)}) copy-start(bf16[2688,256]{1,0:T(8,128)(2,1)} %copy-done.17) | copy-start | bytes 4128772
  173.5 75.0 %collective-permute-start.29 = (bf16[5504,256]{1,0:T(8,128)(2,1)}, bf16[5504,256]{1,0:T(8,128)(2,1)}, u32[]{:S(2)}, u32[]{:S(2)}) collective-permute-start(bf16[5504,256]{1,0:T(8,128)(2,1)} %add_convert_fusion), channel_id=1, source_target_pairs={{0,4},{2,6},{4,0},{6,2},{8,12},{10,14},{12,8},{14,10},{16,20},{18,... | collective-permute-start | bytes 8454152 | tf_op jit(solution)/shard_map/ppermute | solution.py:32
  185.7 7.1 %copy-start.1 = (bf16[512,2688]{1,0:T(8,128)(2,1)S(1)}, bf16[512,2688]{1,0:T(8,128)(2,1)}, u32[]{:S(2)}) copy-start(bf16[512,2688]{1,0:T(8,128)(2,1)} %copy-done) | copy-start | bytes 8257540
  189.9 19.7 %copy-start.23 = (bf16[128,2816]{1,0:T(8,128)(2,1)S(1)}, bf16[128,2816]{1,0:T(8,128)(2,1)}, u32[]{:S(2)}) copy-start(bf16[128,2816]{1,0:T(8,128)(2,1)} %copy-done.22) | copy-start | bytes 2162692
  190.0 19.6 %copy-start.5 = (bf16[128,5504]{1,0:T(8,128)(2,1)S(1)}, bf16[128,5504]{1,0:T(8,128)(2,1)}, u32[]{:S(2)}) copy-start(bf16[128,5504]{1,0:T(8,128)(2,1)} %param.5) | copy-start | bytes 4227076
  190.0 19.6 %copy-start.6 = (bf16[128,5504]{1,0:T(8,128)(2,1)S(1)}, bf16[128,5504]{1,0:T(8,128)(2,1)}, u32[]{:S(2)}) copy-start(bf16[128,5504]{1,0:T(8,128)(2,1)} %param.4) | copy-start | bytes 4227076
  190.1 19.6 %copy-start.21 = (bf16[128,2816]{1,0:T(8,128)(2,1)S(1)}, bf16[128,2816]{1,0:T(8,128)(2,1)}, u32[]{:S(2)}) copy-start(bf16[128,2816]{1,0:T(8,128)(2,1)} %copy-done.20) | copy-start | bytes 2162692
  190.1 20.5 %collective-permute-start.24 = (bf16[128,1024]{1,0:T(8,128)(2,1)S(1)}, bf16[128,1024]{1,0:T(8,128)(2,1)S(1)}, u32[]{:S(2)}, u32[]{:S(2)}) collective-permute-start(bf16[128,1024]{1,0:T(8,128)(2,1)S(1)} %get-tuple-element.88), channel_id=1, source_target_pairs={{0,16},{2,18},{4,20},{6,22},{8,24},{10,26},{12,28},{14,30},{16,0},... | collective-permute-start | bytes 786440 | tf_op jit(solution)/shard_map/ppermute | solution.py:36
  191.6 18.0 %collective-permute-start.23 = (bf16[128,1024]{1,0:T(8,128)(2,1)S(1)}, bf16[128,1024]{1,0:T(8,128)(2,1)S(1)}, u32[]{:S(2)}, u32[]{:S(2)}) collective-permute-start(bf16[128,1024]{1,0:T(8,128)(2,1)S(1)} %get-tuple-element.89), channel_id=1, source_target_pairs={{0,8},{2,10},{4,12},{6,14},{8,16},{10,18},{12,20},{14,22},{16,24},... | collective-permute-start | bytes 786440 | tf_op jit(solution)/shard_map/ppermute | solution.py:36
  193.2 39.0 %collective-permute-start.28 = (bf16[128,2688]{1,0:T(8,128)(2,1)S(1)}, bf16[128,2688]{1,0:T(8,128)(2,1)S(1)}, u32[]{:S(2)}, u32[]{:S(2)}) collective-permute-start(bf16[128,2688]{1,0:T(8,128)(2,1)S(1)} %get-tuple-element.66), channel_id=1, source_target_pairs={{24,16},{26,18},{28,20},{30,22},{16,8},{18,10},{20,12},{22,14},{8,... | collective-permute-start | bytes 2064392 | tf_op jit(solution)/shard_map/ppermute | solution.py:40
  196.5 35.7 %collective-permute-start.27 = (bf16[128,2688]{1,0:T(8,128)(2,1)S(1)}, bf16[128,2688]{1,0:T(8,128)(2,1)S(1)}, u32[]{:S(2)}, u32[]{:S(2)}) collective-permute-start(bf16[128,2688]{1,0:T(8,128)(2,1)S(1)} %get-tuple-element.64), channel_id=1, source_target_pairs={{0,8},{2,10},{4,12},{6,14},{8,16},{10,18},{12,20},{14,22},{16,24},... | collective-permute-start | bytes 2064392 | tf_op jit(solution)/shard_map/ppermute | solution.py:40
  209.6 20.9 %collective-permute-start.25 = (bf16[128,1024]{1,0:T(8,128)(2,1)S(1)}, bf16[128,1024]{1,0:T(8,128)(2,1)S(1)}, u32[]{:S(2)}, u32[]{:S(2)}) collective-permute-start(bf16[128,1024]{1,0:T(8,128)(2,1)S(1)} %get-tuple-element.60), channel_id=1, source_target_pairs={{0,24},{2,26},{4,28},{6,30},{8,0},{10,2},{12,4},{14,6},{16,8},{18,... | collective-permute-start | bytes 786440 | tf_op jit(solution)/shard_map/ppermute | solution.py:36
  230.8 13.7 %collective-permute-start.26 = (bf16[128,2048]{1,0:T(8,128)(2,1)S(1)}, bf16[128,2048]{1,0:T(8,128)(2,1)S(1)}, u32[]{:S(2)}, u32[]{:S(2)}) collective-permute-start(bf16[128,2048]{1,0:T(8,128)(2,1)S(1)} %pad_maximum_fusion.20), channel_id=1, source_target_pairs={{0,1},{1,0},{2,3},{3,2},{4,5},{5,4},{6,7},{7,6},{8,9},{9,8},{10,11... | collective-permute-start | bytes 1572872 | tf_op jit(solution)/shard_map/ppermute | solution.py:49
  (10 other events, 31.1 us)

commit v6 on v5

--- a/solution.py
+++ b/solution.py
@@ -227,7 +227,7 @@
         sides = [local_shift(half_of(step), step) for step in range(1, n_local)]
         output = half_of(0).astype(jnp.float32)
         for side in sides:
-            output = output + side.astype(jnp.float32)
+            output = output + after(side, down_grad).astype(jnp.float32)
         output = output.astype(jnp.bfloat16).reshape(tokens, per_half, QUAD, width)
         return (
             picked(output, slot_of(near), 2).reshape(tokens, half),

time: 257 us -> 246 us (0.957)
  starting transfers between devices: 57.7 us -> 54.3 us
  waiting for transfers between devices: 108 us -> 105 us
    ppermute x3, waiting for transfers between devices: 11.2 us -> 3.83 us  [local_shift(): lax.ppermute(value, 'local', [(i, (i + step) % n_local) for i in range(n_...]
    ppermute x6, waiting for transfers between devices: 17.1 us -> 21.3 us  [swap(): return lax.ppermute(value, 'hst', [(h, h ^ bit) for h in range(n_hst)])]
    ppermute x15, waiting for transfers between devices: 21.3 us -> 25.3 us  [far_permute(): return lax.ppermute(value, 'hst', pairs)]
    ppermute x6, waiting for transfers between devices: 58.5 us -> 54.7 us  [shift(): return lax.ppermute(value, 'hst', pairs)]
    ppermute x15, starting transfers between devices: 44.8 us -> 41.5 us  [far_permute(): return lax.ppermute(value, 'hst', pairs)]
  transfers between devices with their start and end apart: 30 -> 30, of which waited for: 13 -> 16; matrix products, arithmetic and copies ran while one was open for 31% -> 31% of each run, Pallas kernels for 0% -> 0%
where the time goes in v6:
time: 246 us; the launch traced here: 245 us
  waiting for transfers between devices  105 us (43%)
  starting transfers between devices  54.3 us (22%)
  matrix products  35.4 us (14%)
  other arithmetic  35.1 us (14%)
  local copies, waits for them, and re-layouts  13.2 us (5%)
    ppermute x6, waiting for transfers between devices, shift(): return lax.ppermute(value, 'hst', pairs)  54.7 us
    ppermute x15, starting transfers between devices, far_permute(): return lax.ppermute(value, 'hst', pairs)  41.5 us
    ppermute x15, waiting for transfers between devices, far_permute(): return lax.ppermute(value, 'hst', pairs)  25.3 us
    ppermute x6, waiting for transfers between devices, swap(): return lax.ppermute(value, 'hst', [(h, h ^ bit) for h in range(n_hst)])  21.3 us
    dot_general x3, matrix products, grad_terms(): lax.dot_general(rows, part, SUM_ROWS, preferred_element_type=jnp.float32)  13.4 us
    dot_general x2, matrix products, reduce_terms(): lax.dot_general(cot_rows, weights[f], KEEP_COLS, preferred_element_type=j...  11 us
    dot_general x2, matrix products, on_device(): jnp.dot(rows[:, lo:hi], weights[f], preferred_element_type=jnp.float32)  11 us
    concatenate x2, other arithmetic, weight_columns(): pair = jnp.concatenate([down_weight[lo:hi], other], axis=1)  6.74 us
  transfers between devices with their start and end apart: 30, of which 16 were waited for; matrix products, arithmetic and copies ran while one was open for 31% of the time, Pallas kernels for 0%

profile of v6, /device:TPU:8, one launch (start us, length us, event | category | flops | bytes accessed | tf_op | source)
XLA Modules:
  0.0 244.7 jit_solution(3897098823551756865)
XLA Ops:
  0.6 1.6 collective-permute-start.2
  2.2 3.7 %fusion.6 = bf16[128,5504]{1,0:T(8,128)(2,1)} fusion(bf16[128,5504]{1,0:T(8,128)(2,1)} %param.5, bf16[128,5504]{1,0:T(8,128)(2,1)} %param.4), kind=kLoop, calls=%fused_computation.17 | loop fusion | flops 5636096 | bytes 4227072 | tf_op jit(solution)/shard_map/convert_element_type | solution.py:69
  6.0 1.6 collective-permute-start.6
  7.6 2.3 collective-permute-start
  10.0 3.5 %collective-permute-start.1 = (bf16[128,5504]{1,0:T(8,128)(2,1)}, bf16[128,5504]{1,0:T(8,128)(2,1)}, u32[]{:S(2)}, u32[]{:S(2)}) collective-permute-start(bf16[128,5504]{1,0:T(8,128)(2,1)} %fusion.6), channel_id=1, source_target_pairs={{0,8},{2,10},{4,12},{6,14},{8,16},{10,18},{12,20},{14,22},{16,24},... | collective-permute-start | bytes 4227080 | tf_op jit(solution)/shard_map/ppermute | solution.py:40
  15.5 2.2 constant_dynamic-slice_fusion.15
  17.7 2.4 pad_maximum_fusion.15
  21.9 2.5 %slice.78 = bf16[2688,256]{1,0:T(8,128)(2,1)} slice(bf16[5504,256]{1,0:T(8,128)(2,1)} %param.7), slice={[2816:5504], [0:256]} | slice | bytes 2752512 | tf_op jit(solution)/shard_map/slice | solution.py:134
  24.4 2.9 %collective-permute-start.4 = (bf16[64,1024]{1,0:T(8,128)(2,1)S(1)}, bf16[64,1024]{1,0:T(8,128)(2,1)S(1)}, u32[]{:S(2)}, u32[]{:S(2)}) collective-permute-start(bf16[64,1024]{1,0:T(8,128)(2,1)S(1)} %bitcast.28), channel_id=1, source_target_pairs={{0,16},{2,18},{4,20},{6,22},{8,24},{10,26},{12,28},{14,30},{16,0},... | collective-permute-start | bytes 393224 | tf_op jit(solution)/shard_map/ppermute | solution.py:36
  27.4 22.7 %collective-permute-done.3 = bf16[64,1024]{1,0:T(8,128)(2,1)S(1)} collective-permute-done((bf16[64,1024]{1,0:T(8,128)(2,1)S(1)}, bf16[64,1024]{1,0:T(8,128)(2,1)S(1)}, u32[]{:S(2)}, u32[]{:S(2)}) %collective-permute-start.3) | collective-permute-done | bytes 131104 | tf_op jit(solution)/shard_map/ppermute | solution.py:36
  50.2 3.1 %pad_maximum_fusion.3 = bf16[2816,512]{1,0:T(8,128)(2,1)} fusion(bf16[2816,256]{1,0:T(8,128)(2,1)} %collective-permute-done.6, bf16[2816,256]{1,0:T(8,128)(2,1)S(1)} %slice.77), kind=kLoop, calls=%fused_computation.10 | loop fusion | flops 5767168 | bytes 5767168 | tf_op jit(solution)/shard_map/concatenate | solution.py:104
  53.3 1.8 collective-permute-done.5
  57.2 4.6 %collective-permute-start.8 = (bf16[128,5504]{1,0:T(8,128)(2,1)}, bf16[128,5504]{1,0:T(8,128)(2,1)}, u32[]{:S(2)}, u32[]{:S(2)}) collective-permute-start(bf16[128,5504]{1,0:T(8,128)(2,1)} %collective-permute-done.1), channel_id=1, source_target_pairs={{8,16},{10,18},{12,20},{14,22},{16,24},{18,26},{20,28},{22,30},{9,... | collective-permute-start | bytes 4227080 | tf_op jit(solution)/shard_map/ppermute | solution.py:40
  61.8 2.1 collective-permute-start.7
  63.9 2.9 %collective-permute-done.10 = bf16[192,1024]{1,0:T(8,128)(2,1)S(1)} collective-permute-done((bf16[192,1024]{1,0:T(8,128)(2,1)S(1)}, bf16[192,1024]{1,0:T(8,128)(2,1)S(1)}, u32[]{:S(2)}, u32[]{:S(2)}) %collective-permute-start.10) | collective-permute-done | bytes 393248 | tf_op jit(solution)/shard_map/ppermute | solution.py:49
  67.0 5.7 %convolution_convert_fusion.2 = bf16[512,2816]{1,0:T(8,128)(2,1)S(1)} fusion(bf16[2816,512]{1,0:T(8,128)(2,1)} %collective-permute-done.11, bf16[2816,256]{1,0:T(8,128)(2,1)} %collective-permute-done.6, bf16[2816,256]{1,0:T(8,128)(2,1)S(1)} %copy-done.3, bf16[128,1024]{1,0:T(8,128)(2,1)S(1)} %bitcast.23, bf16[384,1024]{1,0:T(8,128)(2,1)S(1)} %bitcast.16), kind=kOutput, calls=%fused_computation.7 | convolution fusion | flops 2973630464 | bytes 9699328 | tf_op jit(solution)/shard_map/dot_general | solution.py:109
  74.0 15.2 %collective-permute-done.9 = bf16[2688,256]{1,0:T(8,128)(2,1)S(1)} collective-permute-done((bf16[2688,256]{1,0:T(8,128)(2,1)}, bf16[2688,256]{1,0:T(8,128)(2,1)S(1)}, u32[]{:S(2)}, u32[]{:S(2)}) %collective-permute-start.9) | collective-permute-done | bytes 1376288 | tf_op jit(solution)/shard_map/ppermute | solution.py:32
  89.2 3.6 %pad_maximum_fusion.4 = bf16[2688,512]{1,0:T(8,128)(2,1)} fusion(bf16[2688,256]{1,0:T(8,128)(2,1)S(1)} %collective-permute-done.9, bf16[2688,256]{1,0:T(8,128)(2,1)} %slice.78), kind=kLoop, calls=%fused_computation.18 | loop fusion | flops 5505024 | bytes 5505024 | tf_op jit(solution)/shard_map/concatenate | solution.py:104
  92.8 3.7 %collective-permute-done.7 = bf16[128,5504]{1,0:T(8,128)(2,1)} collective-permute-done((bf16[128,5504]{1,0:T(8,128)(2,1)}, bf16[128,5504]{1,0:T(8,128)(2,1)}, u32[]{:S(2)}, u32[]{:S(2)}) %collective-permute-start.7) | collective-permute-done | bytes 1409056 | tf_op jit(solution)/shard_map/ppermute | solution.py:40
  97.4 1.6 broadcast_select_fusion.3
  99.0 2.4 collective-permute-start.13
  104.1 4.6 %collective-permute-start.15 = (bf16[128,2816]{1,0:T(8,128)(2,1)S(1)}, bf16[128,2816]{1,0:T(8,128)(2,1)S(1)}, u32[]{:S(2)}, u32[]{:S(2)}) collective-permute-start(bf16[128,2816]{1,0:T(8,128)(2,1)S(1)} %get-tuple-element.47), channel_id=1, source_target_pairs={{0,8},{2,10},{4,12},{6,14},{8,16},{10,18},{12,20},{14,22},{1,9},{3... | collective-permute-start | bytes 2162696 | tf_op jit(solution)/shard_map/ppermute | solution.py:40
  108.7 5.4 %convolution_convert_fusion.1 = bf16[512,2688]{1,0:T(8,128)(2,1)S(1)} fusion(bf16[2688,512]{1,0:T(8,128)(2,1)} %collective-permute-done.14, bf16[2688,256]{1,0:T(8,128)(2,1)S(1)} %copy-done.18, bf16[2688,256]{1,0:T(8,128)(2,1)} %slice.78, bf16[128,1024]{1,0:T(8,128)(2,1)S(1)} %bitcast.24, bf16[384,1024]{1,0:T(8,128)(2,1)S(1)} %bitcast.17), kind=kOutput, calls=%fused_computation.6 | convolution fusion | flops 2838560768 | bytes 9306112 | tf_op jit(solution)/shard_map/dot_general | solution.py:109
  115.5 7.4 %collective-permute-done.16 = bf16[128,2816]{1,0:T(8,128)(2,1)S(1)} collective-permute-done((bf16[128,2816]{1,0:T(8,128)(2,1)S(1)}, bf16[128,2816]{1,0:T(8,128)(2,1)S(1)}, u32[]{:S(2)}, u32[]{:S(2)}) %collective-permute-start.16) | collective-permute-done | bytes 720928 | tf_op jit(solution)/shard_map/ppermute | solution.py:40
  122.9 2.1 collective-permute-done.15
  125.3 3.5 %collective-permute-start.18 = (bf16[128,2816]{1,0:T(8,128)(2,1)S(1)}, bf16[128,2816]{1,0:T(8,128)(2,1)S(1)}, u32[]{:S(2)}, u32[]{:S(2)}) collective-permute-start(bf16[128,2816]{1,0:T(8,128)(2,1)S(1)} %get-tuple-element.79), channel_id=1, source_target_pairs={{0,8},{2,10},{4,12},{6,14},{8,16},{10,18},{12,20},{14,22},{16,24},... | collective-permute-start | bytes 2162696 | tf_op jit(solution)/shard_map/ppermute | solution.py:40
  128.8 2.4 collective-permute-start.19
  132.5 7.2 %collective-permute-done.17 = bf16[128,2688]{1,0:T(8,128)(2,1)S(1)} collective-permute-done((bf16[128,2688]{1,0:T(8,128)(2,1)S(1)}, bf16[128,2688]{1,0:T(8,128)(2,1)S(1)}, u32[]{:S(2)}, u32[]{:S(2)}) %collective-permute-start.17) | collective-permute-done | bytes 688160 | tf_op jit(solution)/shard_map/ppermute | solution.py:40
  139.8 1.8 broadcast_select_fusion.1
  141.5 2.6 %broadcast_select_fusion.2 = (bf16[128,5504]{1,0:T(8,128)(2,1)S(1)}, bf16[128,5504]{1,0:T(8,128)(2,1)S(1)}) fusion(bf16[128,5504]{1,0:T(8,128)(2,1)} %collective-permute-done, bf16[128,5504]{1,0:T(8,128)(2,1)S(1)} %collective-permute-done.13, pred[]{:T(512)S(6)} %lt.176, bf16[128,5504]{1,0:T(8,128)(2,1)} %collective-permute-done.1, pred[]{:T(512)S(6)} %lt.178), kind=kLoop, calls=%fused_computation.52 | loop fusion | flops 1409024 | bytes 7045122 | tf_op jit(solution)/shard_map/jit(_where)/select_n | solution.py:174
  144.1 6.8 %convolution_convert_fusion = bf16[5504,512]{1,0:T(8,128)(2,1)} fusion(bf16[384,1024]{1,0:T(8,128)(2,1)S(1)} %bitcast.18, bf16[128,1024]{1,0:T(8,128)(2,1)S(1)} %bitcast.25, bf16[128,5504]{1,0:T(8,128)(2,1)S(1)} %get-tuple-element.83, bf16[128,5504]{1,0:T(8,128)(2,1)S(1)} %broadcast_select_fusion.1, bf16[128,5504]{1,0:T(8,128)(2,1)S(1)} %get-tuple-element.82, ...), kind=kOutput, calls=%fused_computation | convolution fusion | flops 2912092160 | bytes 12320768 | tf_op jit(solution)/shard_map/dot_general | solution.py:179
  150.9 3.5 %collective-permute-done.18 = bf16[128,2816]{1,0:T(8,128)(2,1)S(1)} collective-permute-done((bf16[128,2816]{1,0:T(8,128)(2,1)S(1)}, bf16[128,2816]{1,0:T(8,128)(2,1)S(1)}, u32[]{:S(2)}, u32[]{:S(2)}) %collective-permute-start.18) | collective-permute-done | bytes 720928 | tf_op jit(solution)/shard_map/ppermute | solution.py:40
  156.2 1.7 fusion.22
  159.3 5.0 %collective-permute-start.21 = (bf16[128,2688]{1,0:T(8,128)(2,1)S(1)}, bf16[128,2688]{1,0:T(8,128)(2,1)S(1)}, u32[]{:S(2)}, u32[]{:S(2)}) collective-permute-start(bf16[128,2688]{1,0:T(8,128)(2,1)S(1)} %get-tuple-element.58), channel_id=1, source_target_pairs={{0,8},{2,10},{4,12},{6,14},{8,16},{10,18},{12,20},{14,22},{1,9},{3... | collective-permute-start | bytes 2064392 | tf_op jit(solution)/shard_map/ppermute | solution.py:40
  164.3 3.2 %pad_maximum_fusion.1 = bf16[512,5504]{1,0:T(8,128)(2,1)S(1)} fusion(bf16[128,5504]{1,0:T(8,128)(2,1)} %copy-done.11, bf16[128,5504]{1,0:T(8,128)(2,1)S(1)} %copy-done.8, bf16[128,5504]{1,0:T(8,128)(2,1)} %copy-done.9, bf16[128,5504]{1,0:T(8,128)(2,1)} %fusion.6), kind=kLoop, calls=%fused_computation.2 | loop fusion | flops 22544384 | bytes 11272192 | tf_op jit(solution)/shard_map/concatenate | solution.py:175
  167.6 5.0 %add_convert_fusion = bf16[5504,256]{1,0:T(8,128)(2,1)} fusion(bf16[5504,512]{1,0:T(8,128)(2,1)} %collective-permute-done.20, bf16[384,1024]{1,0:T(8,128)(2,1)S(1)} %bitcast.19, bf16[128,1024]{1,0:T(8,128)(2,1)S(1)} %bitcast.26, bf16[128,5504]{1,0:T(8,128)(2,1)S(1)} %copy-done.12, bf16[128,5504]{1,0:T(8,128)(2,1)S(1)} %copy-done.8, ...), kind=kOutput, calls=%fused_computation.4 | convolution fusion | flops 1470136320 | bytes 12320768 | tf_op jit(solution)/shard_map/dot_general | solution.py:179
  172.5 1.4 collective-permute-start.27
  173.9 5.4 %fusion = f32[512,1024]{1,0:T(8,128)S(1)} fusion(bf16[512,5504]{1,0:T(8,128)(2,1)S(1)} %pad_maximum_fusion.1, bf16[2816,512]{1,0:T(8,128)(2,1)} %collective-permute-done.11, bf16[2816,256]{1,0:T(8,128)(2,1)} %collective-permute-done.6, bf16[2816,256]{1,0:T(8,128)(2,1)S(1)} %copy-done.4), kind=kOutput, calls=%fused_computation.11 | convolution fusion | flops 2970091520 | bytes 10747904 | tf_op jit(solution)/shard_map/dot_general | solution.py:190
  179.3 1.7 fusion.34
  181.1 5.5 %add_convert_fusion.1 = bf16[512,1024]{1,0:T(8,128)(2,1)S(1)} fusion(f32[512,1024]{1,0:T(8,128)S(1)} %fusion, bf16[2688,512]{1,0:T(8,128)(2,1)} %collective-permute-done.14, bf16[2688,256]{1,0:T(8,128)(2,1)S(1)} %copy-done.19, bf16[2688,256]{1,0:T(8,128)(2,1)} %slice.78, bf16[512,5504]{1,0:T(8,128)(2,1)S(1)} %pad_maximum_fusion.1), kind=kOutput, calls=%fused_computation.24 | convolution fusion | flops 2836135936 | bytes 11403264 | tf_op jit(solution)/shard_map/dot_general | solution.py:190
  187.7 2.1 collective-permute-start.28
  189.8 4.0 %collective-permute-start.29 = (bf16[128,2688]{1,0:T(8,128)(2,1)S(1)}, bf16[128,2688]{1,0:T(8,128)(2,1)S(1)}, u32[]{:S(2)}, u32[]{:S(2)}) collective-permute-start(bf16[128,2688]{1,0:T(8,128)(2,1)S(1)} %get-tuple-element.69), channel_id=1, source_target_pairs={{24,16},{26,18},{28,20},{30,22},{16,8},{18,10},{20,12},{22,14},{8,... | collective-permute-start | bytes 2064392 | tf_op jit(solution)/shard_map/ppermute | solution.py:40
  197.3 26.8 %collective-permute-done.24 = bf16[128,1024]{1,0:T(8,128)(2,1)S(1)} collective-permute-done((bf16[128,1024]{1,0:T(8,128)(2,1)S(1)}, bf16[128,1024]{1,0:T(8,128)(2,1)S(1)}, u32[]{:S(2)}, u32[]{:S(2)}) %collective-permute-start.24) | collective-permute-done | bytes 262176 | tf_op jit(solution)/shard_map/ppermute | solution.py:36
  224.1 2.2 collective-permute-done.25
  226.5 1.4 collective-permute-start.26
  228.8 1.7 pad_maximum_fusion.12
  230.6 5.1 %collective-permute-done.27 = bf16[5504,256]{1,0:T(8,128)(2,1)S(1)} collective-permute-done((bf16[5504,256]{1,0:T(8,128)(2,1)}, bf16[5504,256]{1,0:T(8,128)(2,1)S(1)}, u32[]{:S(2)}, u32[]{:S(2)}) %collective-permute-start.27) | collective-permute-done | bytes 2818080 | tf_op jit(solution)/shard_map/ppermute | solution.py:32
  235.7 5.0 %convert_add_fusion = f32[5504,256]{1,0:T(8,128)} fusion(bf16[5504,256]{1,0:T(8,128)(2,1)S(1)} %collective-permute-done.27, f32[5504,256]{1,0:T(8,128)S(1)} %fusion.34, bf16[5504,512]{1,0:T(8,128)(2,1)} %collective-permute-done.20), kind=kLoop, calls=%fused_computation.3 | loop fusion | flops 5636096 | bytes 16908288 | tf_op jit(solution)/shard_map/add | solution.py:187
  (119 shorter events, 26.6 us)
Async XLA Ops:
  0.6 13.9 %collective-permute-start.2 = (bf16[128,2048]{1,0:T(8,128)(2,1)}, bf16[128,2048]{1,0:T(8,128)(2,1)S(1)}, u32[]{:S(2)}, u32[]{:S(2)}) collective-permute-start(bf16[128,2048]{1,0:T(8,128)(2,1)} %param.6), channel_id=1, source_target_pairs={{0,1},{1,0},{2,3},{3,2},{4,5},{5,4},{6,7},{7,6},{8,9},{9,8},{10,11... | collective-permute-start | bytes 1572872 | tf_op jit(solution)/shard_map/ppermute | solution.py:49
  5.9 8.7 %copy-start.27 = (bf16[128,2048]{1,0:T(8,128)(2,1)S(1)}, bf16[128,2048]{1,0:T(8,128)(2,1)}, u32[]{:S(2)}) copy-start(bf16[128,2048]{1,0:T(8,128)(2,1)} %param.6) | copy-start | bytes 1572868
  6.0 44.2 %copy-start.2 = (bf16[2816,256]{1,0:T(8,128)(2,1)}, bf16[2816,256]{1,0:T(8,128)(2,1)S(1)}, u32[]{:S(2)}) copy-start(bf16[2816,256]{1,0:T(8,128)(2,1)S(1)} %slice.77) | copy-start | bytes 4325380
  6.0 44.2 %collective-permute-start.6 = (bf16[2816,256]{1,0:T(8,128)(2,1)S(1)}, bf16[2816,256]{1,0:T(8,128)(2,1)}, u32[]{:S(2)}, u32[]{:S(2)}) collective-permute-start(bf16[2816,256]{1,0:T(8,128)(2,1)S(1)} %slice.77), channel_id=1, source_target_pairs={{0,4},{2,6},{4,0},{6,2},{8,12},{10,14},{12,8},{14,10},{16,20},{18,... | collective-permute-start | bytes 4325384 | tf_op jit(solution)/shard_map/ppermute | solution.py:32
  7.6 47.6 %collective-permute-start = (bf16[128,5504]{1,0:T(8,128)(2,1)}, bf16[128,5504]{1,0:T(8,128)(2,1)}, u32[]{:S(2)}, u32[]{:S(2)}) collective-permute-start(bf16[128,5504]{1,0:T(8,128)(2,1)} %fusion.6), channel_id=1, source_target_pairs={{24,16},{26,18},{28,20},{30,22},{16,8},{18,10},{20,12},{22,14},{8,... | collective-permute-start | bytes 4227080 | tf_op jit(solution)/shard_map/ppermute | solution.py:40
  10.0 45.2 %collective-permute-start.1 = (bf16[128,5504]{1,0:T(8,128)(2,1)}, bf16[128,5504]{1,0:T(8,128)(2,1)}, u32[]{:S(2)}, u32[]{:S(2)}) collective-permute-start(bf16[128,5504]{1,0:T(8,128)(2,1)} %fusion.6), channel_id=1, source_target_pairs={{0,8},{2,10},{4,12},{6,14},{8,16},{10,18},{12,20},{14,22},{16,24},... | collective-permute-start | bytes 4227080 | tf_op jit(solution)/shard_map/ppermute | solution.py:40
  21.4 28.7 %collective-permute-start.3 = (bf16[64,1024]{1,0:T(8,128)(2,1)S(1)}, bf16[64,1024]{1,0:T(8,128)(2,1)S(1)}, u32[]{:S(2)}, u32[]{:S(2)}) collective-permute-start(bf16[64,1024]{1,0:T(8,128)(2,1)S(1)} %bitcast.30), channel_id=1, source_target_pairs={{0,24},{2,26},{4,28},{6,30},{8,0},{10,2},{12,4},{14,6},{16,8},{18,... | collective-permute-start | bytes 393224 | tf_op jit(solution)/shard_map/ppermute | solution.py:36
  24.4 28.9 %collective-permute-start.4 = (bf16[64,1024]{1,0:T(8,128)(2,1)S(1)}, bf16[64,1024]{1,0:T(8,128)(2,1)S(1)}, u32[]{:S(2)}, u32[]{:S(2)}) collective-permute-start(bf16[64,1024]{1,0:T(8,128)(2,1)S(1)} %bitcast.28), channel_id=1, source_target_pairs={{0,16},{2,18},{4,20},{6,22},{8,24},{10,26},{12,28},{14,30},{16,0},... | collective-permute-start | bytes 393224 | tf_op jit(solution)/shard_map/ppermute | solution.py:36
  50.2 5.0 %collective-permute-start.5 = (bf16[64,1024]{1,0:T(8,128)(2,1)S(1)}, bf16[64,1024]{1,0:T(8,128)(2,1)S(1)}, u32[]{:S(2)}, u32[]{:S(2)}) collective-permute-start(bf16[64,1024]{1,0:T(8,128)(2,1)S(1)} %bitcast.29), channel_id=1, source_target_pairs={{0,8},{2,10},{4,12},{6,14},{8,16},{10,18},{12,20},{14,22},{16,24},... | collective-permute-start | bytes 393224 | tf_op jit(solution)/shard_map/ppermute | solution.py:36
  55.2 11.8 %collective-permute-start.11 = (bf16[2816,512]{1,0:T(8,128)(2,1)}, bf16[2816,512]{1,0:T(8,128)(2,1)}, u32[]{:S(2)}, u32[]{:S(2)}) collective-permute-start(bf16[2816,512]{1,0:T(8,128)(2,1)} %pad_maximum_fusion.3), channel_id=1, source_target_pairs={{0,2},{2,0},{4,6},{6,4},{8,10},{10,8},{12,14},{14,12},{16,18},{18,... | collective-permute-start | bytes 8650760 | tf_op jit(solution)/shard_map/ppermute | solution.py:32
  55.2 11.6 %collective-permute-start.10 = (bf16[192,1024]{1,0:T(8,128)(2,1)S(1)}, bf16[192,1024]{1,0:T(8,128)(2,1)S(1)}, u32[]{:S(2)}, u32[]{:S(2)}) collective-permute-start(bf16[192,1024]{1,0:T(8,128)(2,1)S(1)} %constant_dynamic-update-slice_fusion), channel_id=1, source_target_pairs={{0,1},{1,0},{2,3},{3,2},{4,5},{5,4},{6,7},{7,6},{8,9},{9,8},{10,11... | collective-permute-start | bytes 1179656 | tf_op jit(solution)/shard_map/ppermute | solution.py:49
  56.5 10.4 %copy-start.3 = (bf16[2816,256]{1,0:T(8,128)(2,1)S(1)}, bf16[2816,256]{1,0:T(8,128)(2,1)}, u32[]{:S(2)}) copy-start(bf16[2816,256]{1,0:T(8,128)(2,1)} %copy-done.2) | copy-start | bytes 4325380
  56.6 32.6 %collective-permute-start.9 = (bf16[2688,256]{1,0:T(8,128)(2,1)}, bf16[2688,256]{1,0:T(8,128)(2,1)S(1)}, u32[]{:S(2)}, u32[]{:S(2)}) collective-permute-start(bf16[2688,256]{1,0:T(8,128)(2,1)} %slice.78), channel_id=1, source_target_pairs={{0,4},{2,6},{4,0},{6,2},{8,12},{10,14},{12,8},{14,10},{16,20},{18,... | collective-permute-start | bytes 4128776 | tf_op jit(solution)/shard_map/ppermute | solution.py:32
  57.2 35.6 %collective-permute-start.8 = (bf16[128,5504]{1,0:T(8,128)(2,1)}, bf16[128,5504]{1,0:T(8,128)(2,1)}, u32[]{:S(2)}, u32[]{:S(2)}) collective-permute-start(bf16[128,5504]{1,0:T(8,128)(2,1)} %collective-permute-done.1), channel_id=1, source_target_pairs={{8,16},{10,18},{12,20},{14,22},{16,24},{18,26},{20,28},{22,30},{9,... | collective-permute-start | bytes 4227080 | tf_op jit(solution)/shard_map/ppermute | solution.py:40
  61.8 34.8 %collective-permute-start.7 = (bf16[128,5504]{1,0:T(8,128)(2,1)}, bf16[128,5504]{1,0:T(8,128)(2,1)}, u32[]{:S(2)}, u32[]{:S(2)}) collective-permute-start(bf16[128,5504]{1,0:T(8,128)(2,1)} %collective-permute-done), channel_id=1, source_target_pairs={{16,8},{18,10},{20,12},{22,14},{8,0},{10,2},{12,4},{14,6},{17,9},{... | collective-permute-start | bytes 4227080 | tf_op jit(solution)/shard_map/ppermute | solution.py:40
  72.7 23.8 %collective-permute-start.12 = (bf16[128,2816]{1,0:T(8,128)(2,1)S(1)}, bf16[128,2816]{1,0:T(8,128)(2,1)S(1)}, u32[]{:S(2)}, u32[]{:S(2)}) collective-permute-start(bf16[128,2816]{1,0:T(8,128)(2,1)S(1)} %broadcast_select_fusion.4), channel_id=1, source_target_pairs={{0,8},{2,10},{4,12},{6,14},{24,16},{26,18},{28,20},{30,22},{1,9},{... | collective-permute-start | bytes 2162696 | tf_op jit(solution)/shard_map/ppermute | solution.py:40
  97.4 5.4 %collective-permute-start.14 = (bf16[2688,512]{1,0:T(8,128)(2,1)}, bf16[2688,512]{1,0:T(8,128)(2,1)}, u32[]{:S(2)}, u32[]{:S(2)}) collective-permute-start(bf16[2688,512]{1,0:T(8,128)(2,1)} %pad_maximum_fusion.4), channel_id=1, source_target_pairs={{0,2},{2,0},{4,6},{6,4},{8,10},{10,8},{12,14},{14,12},{16,18},{18,... | collective-permute-start | bytes 8257544 | tf_op jit(solution)/shard_map/ppermute | solution.py:32
  99.0 9.7 %copy-start.14 = (bf16[3,128,1024]{2,1,0:T(8,128)(2,1)S(1)}, bf16[3,128,1024]{2,1,0:T(8,128)(2,1)}, u32[]{:S(2)}) copy-start(bf16[3,128,1024]{2,1,0:T(8,128)(2,1)} %copy-done.13) | copy-start | bytes 2359300
  99.0 9.7 %copy-start.18 = (bf16[2688,256]{1,0:T(8,128)(2,1)S(1)}, bf16[2688,256]{1,0:T(8,128)(2,1)}, u32[]{:S(2)}) copy-start(bf16[2688,256]{1,0:T(8,128)(2,1)} %copy-done.17) | copy-start | bytes 4128772
  99.0 33.5 %collective-permute-start.13 = (bf16[128,5504]{1,0:T(8,128)(2,1)S(1)}, bf16[128,5504]{1,0:T(8,128)(2,1)S(1)}, u32[]{:S(2)}, u32[]{:S(2)}) collective-permute-start(bf16[128,5504]{1,0:T(8,128)(2,1)S(1)} %broadcast_select_fusion.3), channel_id=1, source_target_pairs={{16,24},{18,26},{20,28},{22,30},{8,0},{10,2},{12,4},{14,6},{17,25}... | collective-permute-start | bytes 4227080 | tf_op jit(solution)/shard_map/ppermute | solution.py:40
  102.8 20.1 %collective-permute-start.16 = (bf16[128,2816]{1,0:T(8,128)(2,1)S(1)}, bf16[128,2816]{1,0:T(8,128)(2,1)S(1)}, u32[]{:S(2)}, u32[]{:S(2)}) collective-permute-start(bf16[128,2816]{1,0:T(8,128)(2,1)S(1)} %get-tuple-element.48), channel_id=1, source_target_pairs={{24,16},{26,18},{28,20},{30,22},{16,8},{18,10},{20,12},{22,14},{25... | collective-permute-start | bytes 2162696 | tf_op jit(solution)/shard_map/ppermute | solution.py:40
  104.1 20.9 %collective-permute-start.15 = (bf16[128,2816]{1,0:T(8,128)(2,1)S(1)}, bf16[128,2816]{1,0:T(8,128)(2,1)S(1)}, u32[]{:S(2)}, u32[]{:S(2)}) collective-permute-start(bf16[128,2816]{1,0:T(8,128)(2,1)S(1)} %get-tuple-element.47), channel_id=1, source_target_pairs={{0,8},{2,10},{4,12},{6,14},{8,16},{10,18},{12,20},{14,22},{1,9},{3... | collective-permute-start | bytes 2162696 | tf_op jit(solution)/shard_map/ppermute | solution.py:40
  114.1 11.3 %copy-start = (bf16[512,2688]{1,0:T(8,128)(2,1)}, bf16[512,2688]{1,0:T(8,128)(2,1)S(1)}, u32[]{:S(2)}) copy-start(bf16[512,2688]{1,0:T(8,128)(2,1)S(1)} %convolution_convert_fusion.1) | copy-start | bytes 8257540
  114.2 25.6 %collective-permute-start.17 = (bf16[128,2688]{1,0:T(8,128)(2,1)S(1)}, bf16[128,2688]{1,0:T(8,128)(2,1)S(1)}, u32[]{:S(2)}, u32[]{:S(2)}) collective-permute-start(bf16[128,2688]{1,0:T(8,128)(2,1)S(1)} %broadcast_select_fusion.5), channel_id=1, source_target_pairs={{0,8},{2,10},{4,12},{6,14},{24,16},{26,18},{28,20},{30,22},{1,9},{... | collective-permute-start | bytes 2064392 | tf_op jit(solution)/shard_map/ppermute | solution.py:40
  125.3 29.1 %collective-permute-start.18 = (bf16[128,2816]{1,0:T(8,128)(2,1)S(1)}, bf16[128,2816]{1,0:T(8,128)(2,1)S(1)}, u32[]{:S(2)}, u32[]{:S(2)}) collective-permute-start(bf16[128,2816]{1,0:T(8,128)(2,1)S(1)} %get-tuple-element.79), channel_id=1, source_target_pairs={{0,8},{2,10},{4,12},{6,14},{8,16},{10,18},{12,20},{14,22},{16,24},... | collective-permute-start | bytes 2162696 | tf_op jit(solution)/shard_map/ppermute | solution.py:40
  128.8 26.4 %collective-permute-start.19 = (bf16[128,2816]{1,0:T(8,128)(2,1)S(1)}, bf16[128,2816]{1,0:T(8,128)(2,1)S(1)}, u32[]{:S(2)}, u32[]{:S(2)}) collective-permute-start(bf16[128,2816]{1,0:T(8,128)(2,1)S(1)} %get-tuple-element.78), channel_id=1, source_target_pairs={{24,16},{26,18},{28,20},{30,22},{16,8},{18,10},{20,12},{22,14},{8,... | collective-permute-start | bytes 2162696 | tf_op jit(solution)/shard_map/ppermute | solution.py:40
  144.1 6.8 %copy-start.9 = (bf16[128,5504]{1,0:T(8,128)(2,1)}, bf16[128,5504]{1,0:T(8,128)(2,1)S(1)}, u32[]{:S(2)}) copy-start(bf16[128,5504]{1,0:T(8,128)(2,1)S(1)} %get-tuple-element.82) | copy-start | bytes 4227076
  144.1 6.8 %copy-start.11 = (bf16[128,5504]{1,0:T(8,128)(2,1)}, bf16[128,5504]{1,0:T(8,128)(2,1)S(1)}, u32[]{:S(2)}) copy-start(bf16[128,5504]{1,0:T(8,128)(2,1)S(1)} %get-tuple-element.83) | copy-start | bytes 4227076
  156.2 11.3 %collective-permute-start.20 = (bf16[5504,512]{1,0:T(8,128)(2,1)}, bf16[5504,512]{1,0:T(8,128)(2,1)}, u32[]{:S(2)}, u32[]{:S(2)}) collective-permute-start(bf16[5504,512]{1,0:T(8,128)(2,1)} %convolution_convert_fusion), channel_id=1, source_target_pairs={{0,2},{2,0},{4,6},{6,4},{8,10},{10,8},{12,14},{14,12},{16,18},{18,... | collective-permute-start | bytes 16908296 | tf_op jit(solution)/shard_map/ppermute | solution.py:32
  156.2 8.1 %copy-start.8 = (bf16[128,5504]{1,0:T(8,128)(2,1)S(1)}, bf16[128,5504]{1,0:T(8,128)(2,1)}, u32[]{:S(2)}) copy-start(bf16[128,5504]{1,0:T(8,128)(2,1)} %copy-done.7) | copy-start | bytes 4227076
  157.9 21.4 %collective-permute-start.22 = (bf16[128,2688]{1,0:T(8,128)(2,1)S(1)}, bf16[128,2688]{1,0:T(8,128)(2,1)S(1)}, u32[]{:S(2)}, u32[]{:S(2)}) collective-permute-start(bf16[128,2688]{1,0:T(8,128)(2,1)S(1)} %get-tuple-element.59), channel_id=1, source_target_pairs={{24,16},{26,18},{28,20},{30,22},{16,8},{18,10},{20,12},{22,14},{25... | collective-permute-start | bytes 2064392 | tf_op jit(solution)/shard_map/ppermute | solution.py:40
  159.2 8.3 %copy-start.10 = (bf16[128,5504]{1,0:T(8,128)(2,1)S(1)}, bf16[128,5504]{1,0:T(8,128)(2,1)}, u32[]{:S(2)}) copy-start(bf16[128,5504]{1,0:T(8,128)(2,1)} %copy-done.9) | copy-start | bytes 4227076
  159.2 8.3 %copy-start.12 = (bf16[128,5504]{1,0:T(8,128)(2,1)S(1)}, bf16[128,5504]{1,0:T(8,128)(2,1)}, u32[]{:S(2)}) copy-start(bf16[128,5504]{1,0:T(8,128)(2,1)} %copy-done.11) | copy-start | bytes 4227076
  159.2 8.3 %copy-start.15 = (bf16[3,128,1024]{2,1,0:T(8,128)(2,1)S(1)}, bf16[3,128,1024]{2,1,0:T(8,128)(2,1)}, u32[]{:S(2)}) copy-start(bf16[3,128,1024]{2,1,0:T(8,128)(2,1)} %copy-done.13) | copy-start | bytes 2359300
  159.3 21.8 %collective-permute-start.21 = (bf16[128,2688]{1,0:T(8,128)(2,1)S(1)}, bf16[128,2688]{1,0:T(8,128)(2,1)S(1)}, u32[]{:S(2)}, u32[]{:S(2)}) collective-permute-start(bf16[128,2688]{1,0:T(8,128)(2,1)S(1)} %get-tuple-element.58), channel_id=1, source_target_pairs={{0,8},{2,10},{4,12},{6,14},{8,16},{10,18},{12,20},{14,22},{1,9},{3... | collective-permute-start | bytes 2064392 | tf_op jit(solution)/shard_map/ppermute | solution.py:40
  167.5 6.4 %copy-start.4 = (bf16[2816,256]{1,0:T(8,128)(2,1)S(1)}, bf16[2816,256]{1,0:T(8,128)(2,1)}, u32[]{:S(2)}) copy-start(bf16[2816,256]{1,0:T(8,128)(2,1)} %copy-done.2) | copy-start | bytes 4325380
  172.5 63.1 %collective-permute-start.27 = (bf16[5504,256]{1,0:T(8,128)(2,1)}, bf16[5504,256]{1,0:T(8,128)(2,1)S(1)}, u32[]{:S(2)}, u32[]{:S(2)}) collective-permute-start(bf16[5504,256]{1,0:T(8,128)(2,1)} %add_convert_fusion), channel_id=1, source_target_pairs={{0,4},{2,6},{4,0},{6,2},{8,12},{10,14},{12,8},{14,10},{16,20},{18,... | collective-permute-start | bytes 8454152 | tf_op jit(solution)/shard_map/ppermute | solution.py:32
  181.1 6.3 %copy-start.1 = (bf16[512,2688]{1,0:T(8,128)(2,1)S(1)}, bf16[512,2688]{1,0:T(8,128)(2,1)}, u32[]{:S(2)}) copy-start(bf16[512,2688]{1,0:T(8,128)(2,1)} %copy-done) | copy-start | bytes 8257540
  186.6 9.7 %copy-start.23 = (bf16[128,2816]{1,0:T(8,128)(2,1)S(1)}, bf16[128,2816]{1,0:T(8,128)(2,1)}, u32[]{:S(2)}) copy-start(bf16[128,2816]{1,0:T(8,128)(2,1)} %copy-done.22) | copy-start | bytes 2162692
  186.7 9.6 %copy-start.5 = (bf16[128,5504]{1,0:T(8,128)(2,1)S(1)}, bf16[128,5504]{1,0:T(8,128)(2,1)}, u32[]{:S(2)}) copy-start(bf16[128,5504]{1,0:T(8,128)(2,1)} %param.5) | copy-start | bytes 4227076
  186.7 9.6 %copy-start.6 = (bf16[128,5504]{1,0:T(8,128)(2,1)S(1)}, bf16[128,5504]{1,0:T(8,128)(2,1)}, u32[]{:S(2)}) copy-start(bf16[128,5504]{1,0:T(8,128)(2,1)} %param.4) | copy-start | bytes 4227076
  186.7 9.6 %copy-start.21 = (bf16[128,2816]{1,0:T(8,128)(2,1)S(1)}, bf16[128,2816]{1,0:T(8,128)(2,1)}, u32[]{:S(2)}) copy-start(bf16[128,2816]{1,0:T(8,128)(2,1)} %copy-done.20) | copy-start | bytes 2162692
  186.7 9.3 %collective-permute-start.23 = (bf16[128,1024]{1,0:T(8,128)(2,1)S(1)}, bf16[128,1024]{1,0:T(8,128)(2,1)S(1)}, u32[]{:S(2)}, u32[]{:S(2)}) collective-permute-start(bf16[128,1024]{1,0:T(8,128)(2,1)S(1)} %get-tuple-element.91), channel_id=1, source_target_pairs={{0,8},{2,10},{4,12},{6,14},{8,16},{10,18},{12,20},{14,22},{16,24},... | collective-permute-start | bytes 786440 | tf_op jit(solution)/shard_map/ppermute | solution.py:36
  187.7 40.2 %collective-permute-start.28 = (bf16[128,2688]{1,0:T(8,128)(2,1)S(1)}, bf16[128,2688]{1,0:T(8,128)(2,1)S(1)}, u32[]{:S(2)}, u32[]{:S(2)}) collective-permute-start(bf16[128,2688]{1,0:T(8,128)(2,1)S(1)} %get-tuple-element.67), channel_id=1, source_target_pairs={{0,8},{2,10},{4,12},{6,14},{8,16},{10,18},{12,20},{14,22},{16,24},... | collective-permute-start | bytes 2064392 | tf_op jit(solution)/shard_map/ppermute | solution.py:40
  189.8 38.2 %collective-permute-start.29 = (bf16[128,2688]{1,0:T(8,128)(2,1)S(1)}, bf16[128,2688]{1,0:T(8,128)(2,1)S(1)}, u32[]{:S(2)}, u32[]{:S(2)}) collective-permute-start(bf16[128,2688]{1,0:T(8,128)(2,1)S(1)} %get-tuple-element.69), channel_id=1, source_target_pairs={{24,16},{26,18},{28,20},{30,22},{16,8},{18,10},{20,12},{22,14},{8,... | collective-permute-start | bytes 2064392 | tf_op jit(solution)/shard_map/ppermute | solution.py:40
  193.7 30.4 %collective-permute-start.24 = (bf16[128,1024]{1,0:T(8,128)(2,1)S(1)}, bf16[128,1024]{1,0:T(8,128)(2,1)S(1)}, u32[]{:S(2)}, u32[]{:S(2)}) collective-permute-start(bf16[128,1024]{1,0:T(8,128)(2,1)S(1)} %get-tuple-element.90), channel_id=1, source_target_pairs={{0,16},{2,18},{4,20},{6,22},{8,24},{10,26},{12,28},{14,30},{16,0},... | collective-permute-start | bytes 786440 | tf_op jit(solution)/shard_map/ppermute | solution.py:36
  196.0 30.3 %collective-permute-start.25 = (bf16[128,1024]{1,0:T(8,128)(2,1)S(1)}, bf16[128,1024]{1,0:T(8,128)(2,1)S(1)}, u32[]{:S(2)}, u32[]{:S(2)}) collective-permute-start(bf16[128,1024]{1,0:T(8,128)(2,1)S(1)} %get-tuple-element.61), channel_id=1, source_target_pairs={{0,24},{2,26},{4,28},{6,30},{8,0},{10,2},{12,4},{14,6},{16,8},{18,... | collective-permute-start | bytes 786440 | tf_op jit(solution)/shard_map/ppermute | solution.py:36
  226.5 14.2 %collective-permute-start.26 = (bf16[128,2048]{1,0:T(8,128)(2,1)S(1)}, bf16[128,2048]{1,0:T(8,128)(2,1)S(1)}, u32[]{:S(2)}, u32[]{:S(2)}) collective-permute-start(bf16[128,2048]{1,0:T(8,128)(2,1)S(1)} %pad_maximum_fusion.20), channel_id=1, source_target_pairs={{0,1},{1,0},{2,3},{3,2},{4,5},{5,4},{6,7},{7,6},{8,9},{9,8},{10,11... | collective-permute-start | bytes 1572872 | tf_op jit(solution)/shard_map/ppermute | solution.py:49
  (10 other events, 27.4 us)

commit v7 on v6

--- a/solution.py
+++ b/solution.py
@@ -57,7 +57,7 @@
         columns = QUAD * width
         hidden_units = gate_act.shape[1]
         per_half = half // columns
-        middle = 128 * ((hidden_units // 128 + 1) // 2)
+        middle = 128 * (hidden_units // 128 * 15 // 32)
         bounds = [(0, middle), (middle, hidden_units)]
 
         fence = []

time: 246 us -> 249 us (1.012)
  local copies, waits for them, and re-layouts: 13.2 us -> 18.6 us
    slice x1, local copies, waits for them, and re-layouts: 0.09 us -> 2.98 us  [on_device(): weight_side = swap(after(down_weight[:middle], hidden), 2)]
  transfers between devices with their start and end apart: 30 -> 30, of which waited for: 16 -> 16; matrix products, arithmetic and copies ran while one was open for 31% -> 33% of each run, Pallas kernels for 0% -> 0%
where the time goes in v7:
time: 249 us; the launch traced here: 247 us
  waiting for transfers between devices  103 us (41%)
  starting transfers between devices  54.1 us (22%)
  other arithmetic  35.8 us (14%)
  matrix products  34.5 us (14%)
  local copies, waits for them, and re-layouts  18.6 us (7%)
    ppermute x6, waiting for transfers between devices, shift(): return lax.ppermute(value, 'hst', pairs)  55.6 us
    ppermute x15, starting transfers between devices, far_permute(): return lax.ppermute(value, 'hst', pairs)  40.5 us
    ppermute x15, waiting for transfers between devices, far_permute(): return lax.ppermute(value, 'hst', pairs)  22.9 us
    ppermute x6, waiting for transfers between devices, swap(): return lax.ppermute(value, 'hst', [(h, h ^ bit) for h in range(n_hst)])  21 us
    dot_general x3, matrix products, grad_terms(): lax.dot_general(rows, part, SUM_ROWS, preferred_element_type=jnp.float32)  12.7 us
    dot_general x2, matrix products, reduce_terms(): lax.dot_general(cot_rows, weights[f], KEEP_COLS, preferred_element_type=j...  11 us
    dot_general x2, matrix products, on_device(): jnp.dot(rows[:, lo:hi], weights[f], preferred_element_type=jnp.float32)  10.8 us
    ppermute x6, starting transfers between devices, shift(): return lax.ppermute(value, 'hst', pairs)  6.36 us
  transfers between devices with their start and end apart: 30, of which 16 were waited for; matrix products, arithmetic and copies ran while one was open for 33% of the time, Pallas kernels for 0%

profile of v7, /device:TPU:8, one launch (start us, length us, event | category | flops | bytes accessed | tf_op | source)
XLA Modules:
  0.0 247.4 jit_solution(31953587996224065)
XLA Ops:
  0.6 1.6 collective-permute-start.2
  2.2 2.6 %fusion.6 = bf16[128,5504]{1,0:T(8,128)(2,1)S(1)} fusion(bf16[128,5504]{1,0:T(8,128)(2,1)} %param.5, bf16[128,5504]{1,0:T(8,128)(2,1)} %param.4), kind=kLoop, calls=%fused_computation.17 | loop fusion | flops 5636096 | bytes 4227072 | tf_op jit(solution)/shard_map/convert_element_type | solution.py:69
  4.8 3.0 %slice.77 = bf16[2560,256]{1,0:T(8,128)(2,1)} slice(bf16[5504,256]{1,0:T(8,128)(2,1)} %param.7), slice={[0:2560], [0:256]} | slice | bytes 2621440 | tf_op jit(solution)/shard_map/slice | solution.py:117
  9.3 2.3 collective-permute-start
  11.7 3.5 %collective-permute-start.1 = (bf16[128,5504]{1,0:T(8,128)(2,1)S(1)}, bf16[128,5504]{1,0:T(8,128)(2,1)}, u32[]{:S(2)}, u32[]{:S(2)}) collective-permute-start(bf16[128,5504]{1,0:T(8,128)(2,1)S(1)} %fusion.6), channel_id=1, source_target_pairs={{0,8},{2,10},{4,12},{6,14},{8,16},{10,18},{12,20},{14,22},{16,24},... | collective-permute-start | bytes 4227080 | tf_op jit(solution)/shard_map/ppermute | solution.py:40
  16.4 2.2 constant_dynamic-slice_fusion.15
  18.5 2.4 pad_maximum_fusion.15
  25.2 2.9 %collective-permute-start.4 = (bf16[64,1024]{1,0:T(8,128)(2,1)S(1)}, bf16[64,1024]{1,0:T(8,128)(2,1)S(1)}, u32[]{:S(2)}, u32[]{:S(2)}) collective-permute-start(bf16[64,1024]{1,0:T(8,128)(2,1)S(1)} %bitcast.28), channel_id=1, source_target_pairs={{0,16},{2,18},{4,20},{6,22},{8,24},{10,26},{12,28},{14,30},{16,0},... | collective-permute-start | bytes 393224 | tf_op jit(solution)/shard_map/ppermute | solution.py:36
  28.2 23.5 %collective-permute-done.3 = bf16[64,1024]{1,0:T(8,128)(2,1)S(1)} collective-permute-done((bf16[64,1024]{1,0:T(8,128)(2,1)S(1)}, bf16[64,1024]{1,0:T(8,128)(2,1)S(1)}, u32[]{:S(2)}, u32[]{:S(2)}) %collective-permute-start.3) | collective-permute-done | bytes 131104 | tf_op jit(solution)/shard_map/ppermute | solution.py:36
  51.7 3.4 %pad_maximum_fusion.4 = bf16[2560,512]{1,0:T(8,128)(2,1)} fusion(bf16[2560,256]{1,0:T(8,128)(2,1)} %collective-permute-done.6, bf16[2560,256]{1,0:T(8,128)(2,1)} %slice.77), kind=kLoop, calls=%fused_computation.18 | loop fusion | flops 5242880 | bytes 5242880 | tf_op jit(solution)/shard_map/concatenate | solution.py:104
  55.1 1.6 collective-permute-done.5
  59.2 1.8 constant_dynamic-slice_fusion.8
  61.6 3.5 %collective-permute-start.8 = (bf16[128,5504]{1,0:T(8,128)(2,1)}, bf16[128,5504]{1,0:T(8,128)(2,1)S(1)}, u32[]{:S(2)}, u32[]{:S(2)}) collective-permute-start(bf16[128,5504]{1,0:T(8,128)(2,1)} %collective-permute-done.1), channel_id=1, source_target_pairs={{8,16},{10,18},{12,20},{14,22},{16,24},{18,26},{20,28},{22,30},{9,... | collective-permute-start | bytes 4227080 | tf_op jit(solution)/shard_map/ppermute | solution.py:40
  65.1 2.1 collective-permute-start.7
  67.2 3.3 %collective-permute-done.10 = bf16[192,1024]{1,0:T(8,128)(2,1)} collective-permute-done((bf16[192,1024]{1,0:T(8,128)(2,1)}, bf16[192,1024]{1,0:T(8,128)(2,1)}, u32[]{:S(2)}, u32[]{:S(2)}) %collective-permute-start.10) | collective-permute-done | bytes 393248 | tf_op jit(solution)/shard_map/ppermute | solution.py:49
  71.8 5.7 %convolution_convert_fusion.1 = bf16[512,2560]{1,0:T(8,128)(2,1)S(1)} fusion(bf16[2560,512]{1,0:T(8,128)(2,1)} %collective-permute-done.11, bf16[2560,256]{1,0:T(8,128)(2,1)} %collective-permute-done.6, bf16[2560,256]{1,0:T(8,128)(2,1)} %slice.77, bf16[128,1024]{1,0:T(8,128)(2,1)S(1)} %bitcast.23, bf16[384,1024]{1,0:T(8,128)(2,1)S(1)} %bitcast.16), kind=kOutput, calls=%fused_computation.6 | convolution fusion | flops 2703491072 | bytes 8912896 | tf_op jit(solution)/shard_map/dot_general | solution.py:109
  78.9 17.4 %collective-permute-done.9 = bf16[2944,256]{1,0:T(8,128)(2,1)S(1)} collective-permute-done((bf16[2944,256]{1,0:T(8,128)(2,1)S(1)}, bf16[2944,256]{1,0:T(8,128)(2,1)S(1)}, u32[]{:S(2)}, u32[]{:S(2)}) %collective-permute-start.9) | collective-permute-done | bytes 1507360 | tf_op jit(solution)/shard_map/ppermute | solution.py:32
  96.3 2.0 pad_maximum_fusion.3
  100.6 1.7 broadcast_select_fusion.3
  102.3 2.4 collective-permute-start.13
  107.7 4.6 %collective-permute-start.15 = (bf16[128,2560]{1,0:T(8,128)(2,1)S(1)}, bf16[128,2560]{1,0:T(8,128)(2,1)S(1)}, u32[]{:S(2)}, u32[]{:S(2)}) collective-permute-start(bf16[128,2560]{1,0:T(8,128)(2,1)S(1)} %get-tuple-element.47), channel_id=1, source_target_pairs={{0,8},{2,10},{4,12},{6,14},{8,16},{10,18},{12,20},{14,22},{1,9},{3... | collective-permute-start | bytes 1966088 | tf_op jit(solution)/shard_map/ppermute | solution.py:40
  112.3 5.3 %convolution_convert_fusion.2 = bf16[512,2944]{1,0:T(8,128)(2,1)S(1)} fusion(bf16[2944,512]{1,0:T(8,128)(2,1)} %collective-permute-done.14, bf16[2944,256]{1,0:T(8,128)(2,1)S(1)} %copy-done.23, bf16[2944,256]{1,0:T(8,128)(2,1)S(1)} %copy-done.1, bf16[128,1024]{1,0:T(8,128)(2,1)S(1)} %bitcast.24, bf16[384,1024]{1,0:T(8,128)(2,1)S(1)} %bitcast.17), kind=kOutput, calls=%fused_computation.7 | convolution fusion | flops 3108700160 | bytes 10092544 | tf_op jit(solution)/shard_map/dot_general | solution.py:109
  119.2 5.9 %collective-permute-done.16 = bf16[128,2560]{1,0:T(8,128)(2,1)S(1)} collective-permute-done((bf16[128,2560]{1,0:T(8,128)(2,1)S(1)}, bf16[128,2560]{1,0:T(8,128)(2,1)S(1)}, u32[]{:S(2)}, u32[]{:S(2)}) %collective-permute-start.16) | collective-permute-done | bytes 655392 | tf_op jit(solution)/shard_map/ppermute | solution.py:40
  125.1 2.1 collective-permute-done.15
  127.5 3.5 %collective-permute-start.18 = (bf16[128,2560]{1,0:T(8,128)(2,1)S(1)}, bf16[128,2560]{1,0:T(8,128)(2,1)S(1)}, u32[]{:S(2)}, u32[]{:S(2)}) collective-permute-start(bf16[128,2560]{1,0:T(8,128)(2,1)S(1)} %get-tuple-element.81), channel_id=1, source_target_pairs={{0,8},{2,10},{4,12},{6,14},{8,16},{10,18},{12,20},{14,22},{16,24},... | collective-permute-start | bytes 1966088 | tf_op jit(solution)/shard_map/ppermute | solution.py:40
  131.0 2.4 collective-permute-start.19
  133.4 2.4 collective-permute-done.13
  135.8 7.5 %collective-permute-done.17 = bf16[128,2944]{1,0:T(8,128)(2,1)S(1)} collective-permute-done((bf16[128,2944]{1,0:T(8,128)(2,1)S(1)}, bf16[128,2944]{1,0:T(8,128)(2,1)S(1)}, u32[]{:S(2)}, u32[]{:S(2)}) %collective-permute-start.17) | collective-permute-done | bytes 753696 | tf_op jit(solution)/shard_map/ppermute | solution.py:40
  143.4 1.8 broadcast_select_fusion.1
  145.2 2.7 %broadcast_select_fusion.2 = (bf16[128,5504]{1,0:T(8,128)(2,1)S(1)}, bf16[128,5504]{1,0:T(8,128)(2,1)S(1)}) fusion(bf16[128,5504]{1,0:T(8,128)(2,1)} %collective-permute-done, bf16[128,5504]{1,0:T(8,128)(2,1)S(1)} %collective-permute-done.13, pred[]{:T(512)S(6)} %lt.176, bf16[128,5504]{1,0:T(8,128)(2,1)} %collective-permute-done.1, pred[]{:T(512)S(6)} %lt.178), kind=kLoop, calls=%fused_computation.52 | loop fusion | flops 1409024 | bytes 7045122 | tf_op jit(solution)/shard_map/jit(_where)/select_n | solution.py:174
  147.9 5.2 %convolution_convert_fusion = bf16[5504,512]{1,0:T(8,128)(2,1)} fusion(bf16[384,1024]{1,0:T(8,128)(2,1)S(1)} %bitcast.18, bf16[128,1024]{1,0:T(8,128)(2,1)S(1)} %bitcast.25, bf16[128,5504]{1,0:T(8,128)(2,1)S(1)} %get-tuple-element.83, bf16[128,5504]{1,0:T(8,128)(2,1)S(1)} %broadcast_select_fusion.1, bf16[128,5504]{1,0:T(8,128)(2,1)S(1)} %get-tuple-element.82, ...), kind=kOutput, calls=%fused_computation | convolution fusion | flops 2912092160 | bytes 12320768 | tf_op jit(solution)/shard_map/dot_general | solution.py:179
  153.1 3.5 %collective-permute-done.18 = bf16[128,2560]{1,0:T(8,128)(2,1)S(1)} collective-permute-done((bf16[128,2560]{1,0:T(8,128)(2,1)S(1)}, bf16[128,2560]{1,0:T(8,128)(2,1)S(1)}, u32[]{:S(2)}, u32[]{:S(2)}) %collective-permute-start.18) | collective-permute-done | bytes 655392 | tf_op jit(solution)/shard_map/ppermute | solution.py:40
  158.4 1.6 fusion.12
  161.4 5.0 %collective-permute-start.21 = (bf16[128,2944]{1,0:T(8,128)(2,1)S(1)}, bf16[128,2944]{1,0:T(8,128)(2,1)S(1)}, u32[]{:S(2)}, u32[]{:S(2)}) collective-permute-start(bf16[128,2944]{1,0:T(8,128)(2,1)S(1)} %get-tuple-element.58), channel_id=1, source_target_pairs={{0,8},{2,10},{4,12},{6,14},{8,16},{10,18},{12,20},{14,22},{1,9},{3... | collective-permute-start | bytes 2261000 | tf_op jit(solution)/shard_map/ppermute | solution.py:40
  166.4 2.9 %pad_maximum_fusion.1 = bf16[512,5504]{1,0:T(8,128)(2,1)S(1)} fusion(bf16[128,5504]{1,0:T(8,128)(2,1)} %copy-done.16, bf16[128,5504]{1,0:T(8,128)(2,1)S(1)} %copy-done.13, bf16[128,5504]{1,0:T(8,128)(2,1)} %copy-done.14, bf16[128,5504]{1,0:T(8,128)(2,1)S(1)} %copy-done.11), kind=kLoop, calls=%fused_computation.2 | loop fusion | flops 22544384 | bytes 11272192 | tf_op jit(solution)/shard_map/concatenate | solution.py:175
  169.4 5.8 %add_convert_fusion = bf16[5504,256]{1,0:T(8,128)(2,1)} fusion(bf16[5504,512]{1,0:T(8,128)(2,1)} %collective-permute-done.20, bf16[384,1024]{1,0:T(8,128)(2,1)S(1)} %bitcast.19, bf16[128,1024]{1,0:T(8,128)(2,1)S(1)} %bitcast.26, bf16[128,5504]{1,0:T(8,128)(2,1)S(1)} %copy-done.17, bf16[128,5504]{1,0:T(8,128)(2,1)S(1)} %copy-done.13, ...), kind=kOutput, calls=%fused_computation.4 | convolution fusion | flops 1470136320 | bytes 12320768 | tf_op jit(solution)/shard_map/dot_general | solution.py:179
  176.7 5.4 %fusion.7 = f32[512,1024]{1,0:T(8,128)S(1)} fusion(bf16[512,5504]{1,0:T(8,128)(2,1)S(1)} %pad_maximum_fusion.1, bf16[2560,512]{1,0:T(8,128)(2,1)} %collective-permute-done.11, bf16[2560,256]{1,0:T(8,128)(2,1)} %collective-permute-done.6, bf16[2560,256]{1,0:T(8,128)(2,1)} %slice.77), kind=kOutput, calls=%fused_computation.19 | convolution fusion | flops 2700083200 | bytes 9961472 | tf_op jit(solution)/shard_map/dot_general | solution.py:190
  182.1 1.7 fusion.34
  183.9 5.4 %add_convert_fusion.1 = bf16[512,1024]{1,0:T(8,128)(2,1)S(1)} fusion(f32[512,1024]{1,0:T(8,128)S(1)} %fusion.7, bf16[2944,512]{1,0:T(8,128)(2,1)} %collective-permute-done.14, bf16[2944,256]{1,0:T(8,128)(2,1)S(1)} %copy-done.24, bf16[2944,256]{1,0:T(8,128)(2,1)S(1)} %copy-done.2, bf16[512,5504]{1,0:T(8,128)(2,1)S(1)} %pad_maximum_fusion.1), kind=kOutput, calls=%fused_computation.24 | convolution fusion | flops 3106144256 | bytes 12189696 | tf_op jit(solution)/shard_map/dot_general | solution.py:190
  191.1 2.1 collective-permute-start.28
  193.1 3.8 %collective-permute-start.29 = (bf16[128,2944]{1,0:T(8,128)(2,1)S(1)}, bf16[128,2944]{1,0:T(8,128)(2,1)S(1)}, u32[]{:S(2)}, u32[]{:S(2)}) collective-permute-start(bf16[128,2944]{1,0:T(8,128)(2,1)S(1)} %get-tuple-element.69), channel_id=1, source_target_pairs={{24,16},{26,18},{28,20},{30,22},{16,8},{18,10},{20,12},{22,14},{8,... | collective-permute-start | bytes 2261000 | tf_op jit(solution)/shard_map/ppermute | solution.py:40
  199.0 1.9 fusion.30
  200.9 27.9 %collective-permute-done.24 = bf16[128,1024]{1,0:T(8,128)(2,1)S(1)} collective-permute-done((bf16[128,1024]{1,0:T(8,128)(2,1)S(1)}, bf16[128,1024]{1,0:T(8,128)(2,1)S(1)}, u32[]{:S(2)}, u32[]{:S(2)}) %collective-permute-start.24) | collective-permute-done | bytes 262176 | tf_op jit(solution)/shard_map/ppermute | solution.py:36
  228.8 1.6 collective-permute-done.25
  230.6 1.6 collective-permute-start.26
  233.2 1.7 pad_maximum_fusion.12
  234.9 3.4 %collective-permute-done.27 = bf16[5504,256]{1,0:T(8,128)(2,1)S(1)} collective-permute-done((bf16[5504,256]{1,0:T(8,128)(2,1)}, bf16[5504,256]{1,0:T(8,128)(2,1)S(1)}, u32[]{:S(2)}, u32[]{:S(2)}) %collective-permute-start.27) | collective-permute-done | bytes 2818080 | tf_op jit(solution)/shard_map/ppermute | solution.py:32
  238.3 5.0 %convert_add_fusion = f32[5504,256]{1,0:T(8,128)} fusion(bf16[5504,256]{1,0:T(8,128)(2,1)S(1)} %collective-permute-done.27, f32[5504,256]{1,0:T(8,128)S(1)} %fusion.34, bf16[5504,512]{1,0:T(8,128)(2,1)} %collective-permute-done.20), kind=kLoop, calls=%fused_computation.3 | loop fusion | flops 5636096 | bytes 16908288 | tf_op jit(solution)/shard_map/add | solution.py:187
  (127 shorter events, 33.4 us)
Async XLA Ops:
  0.6 14.8 %collective-permute-start.2 = (bf16[128,2048]{1,0:T(8,128)(2,1)}, bf16[128,2048]{1,0:T(8,128)(2,1)S(1)}, u32[]{:S(2)}, u32[]{:S(2)}) collective-permute-start(bf16[128,2048]{1,0:T(8,128)(2,1)} %param.6), channel_id=1, source_target_pairs={{0,1},{1,0},{2,3},{3,2},{4,5},{5,4},{6,7},{7,6},{8,9},{9,8},{10,11... | collective-permute-start | bytes 1572872 | tf_op jit(solution)/shard_map/ppermute | solution.py:49
  4.8 10.7 %copy-start.9 = (bf16[128,5504]{1,0:T(8,128)(2,1)}, bf16[128,5504]{1,0:T(8,128)(2,1)S(1)}, u32[]{:S(2)}) copy-start(bf16[128,5504]{1,0:T(8,128)(2,1)S(1)} %fusion.6) | copy-start | bytes 4227076
  4.8 10.6 %copy-start.31 = (bf16[128,2048]{1,0:T(8,128)(2,1)S(1)}, bf16[128,2048]{1,0:T(8,128)(2,1)}, u32[]{:S(2)}) copy-start(bf16[128,2048]{1,0:T(8,128)(2,1)} %param.6) | copy-start | bytes 1572868
  7.8 43.9 %collective-permute-start.6 = (bf16[2560,256]{1,0:T(8,128)(2,1)}, bf16[2560,256]{1,0:T(8,128)(2,1)}, u32[]{:S(2)}, u32[]{:S(2)}) collective-permute-start(bf16[2560,256]{1,0:T(8,128)(2,1)} %slice.77), channel_id=1, source_target_pairs={{0,4},{2,6},{4,0},{6,2},{8,12},{10,14},{12,8},{14,10},{16,20},{18,... | collective-permute-start | bytes 3932168 | tf_op jit(solution)/shard_map/ppermute | solution.py:32
  9.3 47.3 %collective-permute-start = (bf16[128,5504]{1,0:T(8,128)(2,1)S(1)}, bf16[128,5504]{1,0:T(8,128)(2,1)}, u32[]{:S(2)}, u32[]{:S(2)}) collective-permute-start(bf16[128,5504]{1,0:T(8,128)(2,1)S(1)} %fusion.6), channel_id=1, source_target_pairs={{24,16},{26,18},{28,20},{30,22},{16,8},{18,10},{20,12},{22,14},{8,... | collective-permute-start | bytes 4227080 | tf_op jit(solution)/shard_map/ppermute | solution.py:40
  11.7 45.0 %collective-permute-start.1 = (bf16[128,5504]{1,0:T(8,128)(2,1)S(1)}, bf16[128,5504]{1,0:T(8,128)(2,1)}, u32[]{:S(2)}, u32[]{:S(2)}) collective-permute-start(bf16[128,5504]{1,0:T(8,128)(2,1)S(1)} %fusion.6), channel_id=1, source_target_pairs={{0,8},{2,10},{4,12},{6,14},{8,16},{10,18},{12,20},{14,22},{16,24},... | collective-permute-start | bytes 4227080 | tf_op jit(solution)/shard_map/ppermute | solution.py:40
  22.4 29.3 %collective-permute-start.3 = (bf16[64,1024]{1,0:T(8,128)(2,1)S(1)}, bf16[64,1024]{1,0:T(8,128)(2,1)S(1)}, u32[]{:S(2)}, u32[]{:S(2)}) collective-permute-start(bf16[64,1024]{1,0:T(8,128)(2,1)S(1)} %bitcast.30), channel_id=1, source_target_pairs={{0,24},{2,26},{4,28},{6,30},{8,0},{10,2},{12,4},{14,6},{16,8},{18,... | collective-permute-start | bytes 393224 | tf_op jit(solution)/shard_map/ppermute | solution.py:36
  25.2 71.1 %copy-start = (bf16[2944,256]{1,0:T(8,128)(2,1)}, bf16[2944,256]{1,0:T(8,128)(2,1)S(1)}, u32[]{:S(2)}) copy-start(bf16[2944,256]{1,0:T(8,128)(2,1)S(1)} %slice.78) | copy-start | bytes 4521988
  25.2 29.9 %collective-permute-start.4 = (bf16[64,1024]{1,0:T(8,128)(2,1)S(1)}, bf16[64,1024]{1,0:T(8,128)(2,1)S(1)}, u32[]{:S(2)}, u32[]{:S(2)}) collective-permute-start(bf16[64,1024]{1,0:T(8,128)(2,1)S(1)} %bitcast.28), channel_id=1, source_target_pairs={{0,16},{2,18},{4,20},{6,22},{8,24},{10,26},{12,28},{14,30},{16,0},... | collective-permute-start | bytes 393224 | tf_op jit(solution)/shard_map/ppermute | solution.py:36
  51.7 5.0 %collective-permute-start.5 = (bf16[64,1024]{1,0:T(8,128)(2,1)S(1)}, bf16[64,1024]{1,0:T(8,128)(2,1)S(1)}, u32[]{:S(2)}, u32[]{:S(2)}) collective-permute-start(bf16[64,1024]{1,0:T(8,128)(2,1)S(1)} %bitcast.29), channel_id=1, source_target_pairs={{0,8},{2,10},{4,12},{6,14},{8,16},{10,18},{12,20},{14,22},{16,24},... | collective-permute-start | bytes 393224 | tf_op jit(solution)/shard_map/ppermute | solution.py:36
  56.7 15.1 %collective-permute-start.11 = (bf16[2560,512]{1,0:T(8,128)(2,1)}, bf16[2560,512]{1,0:T(8,128)(2,1)}, u32[]{:S(2)}, u32[]{:S(2)}) collective-permute-start(bf16[2560,512]{1,0:T(8,128)(2,1)} %pad_maximum_fusion.4), channel_id=1, source_target_pairs={{0,2},{2,0},{4,6},{6,4},{8,10},{10,8},{12,14},{14,12},{16,18},{18,... | collective-permute-start | bytes 7864328 | tf_op jit(solution)/shard_map/ppermute | solution.py:32
  58.7 11.8 %collective-permute-start.10 = (bf16[192,1024]{1,0:T(8,128)(2,1)}, bf16[192,1024]{1,0:T(8,128)(2,1)}, u32[]{:S(2)}, u32[]{:S(2)}) collective-permute-start(bf16[192,1024]{1,0:T(8,128)(2,1)} %constant_dynamic-update-slice_fusion), channel_id=1, source_target_pairs={{0,1},{1,0},{2,3},{3,2},{4,5},{5,4},{6,7},{7,6},{8,9},{9,8},{10,11... | collective-permute-start | bytes 1179656 | tf_op jit(solution)/shard_map/ppermute | solution.py:49
  61.1 35.2 %collective-permute-start.9 = (bf16[2944,256]{1,0:T(8,128)(2,1)S(1)}, bf16[2944,256]{1,0:T(8,128)(2,1)S(1)}, u32[]{:S(2)}, u32[]{:S(2)}) collective-permute-start(bf16[2944,256]{1,0:T(8,128)(2,1)S(1)} %slice.78), channel_id=1, source_target_pairs={{0,4},{2,6},{4,0},{6,2},{8,12},{10,14},{12,8},{14,10},{16,20},{18,... | collective-permute-start | bytes 4521992 | tf_op jit(solution)/shard_map/ppermute | solution.py:32
  61.6 36.8 %collective-permute-start.8 = (bf16[128,5504]{1,0:T(8,128)(2,1)}, bf16[128,5504]{1,0:T(8,128)(2,1)S(1)}, u32[]{:S(2)}, u32[]{:S(2)}) collective-permute-start(bf16[128,5504]{1,0:T(8,128)(2,1)} %collective-permute-done.1), channel_id=1, source_target_pairs={{8,16},{10,18},{12,20},{14,22},{16,24},{18,26},{20,28},{22,30},{9,... | collective-permute-start | bytes 4227080 | tf_op jit(solution)/shard_map/ppermute | solution.py:40
  65.1 34.7 %collective-permute-start.7 = (bf16[128,5504]{1,0:T(8,128)(2,1)}, bf16[128,5504]{1,0:T(8,128)(2,1)}, u32[]{:S(2)}, u32[]{:S(2)}) collective-permute-start(bf16[128,5504]{1,0:T(8,128)(2,1)} %collective-permute-done), channel_id=1, source_target_pairs={{16,8},{18,10},{20,12},{22,14},{8,0},{10,2},{12,4},{14,6},{17,9},{... | collective-permute-start | bytes 4227080 | tf_op jit(solution)/shard_map/ppermute | solution.py:40
  71.7 5.7 %copy-start.19 = (bf16[3,128,1024]{2,1,0:T(8,128)(2,1)}, bf16[3,128,1024]{2,1,0:T(8,128)(2,1)S(1)}, u32[]{:S(2)}) copy-start(bf16[3,128,1024]{2,1,0:T(8,128)(2,1)S(1)} %pad_maximum_fusion.17) | copy-start | bytes 2359300
  77.5 20.8 %copy-start.3 = (bf16[512,2560]{1,0:T(8,128)(2,1)}, bf16[512,2560]{1,0:T(8,128)(2,1)S(1)}, u32[]{:S(2)}) copy-start(bf16[512,2560]{1,0:T(8,128)(2,1)S(1)} %convolution_convert_fusion.1) | copy-start | bytes 7864324
  77.6 22.2 %collective-permute-start.12 = (bf16[128,2560]{1,0:T(8,128)(2,1)S(1)}, bf16[128,2560]{1,0:T(8,128)(2,1)S(1)}, u32[]{:S(2)}, u32[]{:S(2)}) collective-permute-start(bf16[128,2560]{1,0:T(8,128)(2,1)S(1)} %broadcast_select_fusion.5), channel_id=1, source_target_pairs={{0,8},{2,10},{4,12},{6,14},{24,16},{26,18},{28,20},{30,22},{1,9},{... | collective-permute-start | bytes 1966088 | tf_op jit(solution)/shard_map/ppermute | solution.py:40
  100.6 5.8 %collective-permute-start.14 = (bf16[2944,512]{1,0:T(8,128)(2,1)}, bf16[2944,512]{1,0:T(8,128)(2,1)}, u32[]{:S(2)}, u32[]{:S(2)}) collective-permute-start(bf16[2944,512]{1,0:T(8,128)(2,1)} %pad_maximum_fusion.3), channel_id=1, source_target_pairs={{0,2},{2,0},{4,6},{6,4},{8,10},{10,8},{12,14},{14,12},{16,18},{18,... | collective-permute-start | bytes 9043976 | tf_op jit(solution)/shard_map/ppermute | solution.py:32
  100.6 11.7 %copy-start.23 = (bf16[2944,256]{1,0:T(8,128)(2,1)S(1)}, bf16[2944,256]{1,0:T(8,128)(2,1)}, u32[]{:S(2)}) copy-start(bf16[2944,256]{1,0:T(8,128)(2,1)} %copy-done.22) | copy-start | bytes 4521988
  102.3 10.0 %copy-start.1 = (bf16[2944,256]{1,0:T(8,128)(2,1)S(1)}, bf16[2944,256]{1,0:T(8,128)(2,1)}, u32[]{:S(2)}) copy-start(bf16[2944,256]{1,0:T(8,128)(2,1)} %copy-done) | copy-start | bytes 4521988
  102.3 10.0 %copy-start.20 = (bf16[3,128,1024]{2,1,0:T(8,128)(2,1)S(1)}, bf16[3,128,1024]{2,1,0:T(8,128)(2,1)}, u32[]{:S(2)}) copy-start(bf16[3,128,1024]{2,1,0:T(8,128)(2,1)} %copy-done.19) | copy-start | bytes 2359300
  102.3 33.5 %collective-permute-start.13 = (bf16[128,5504]{1,0:T(8,128)(2,1)S(1)}, bf16[128,5504]{1,0:T(8,128)(2,1)S(1)}, u32[]{:S(2)}, u32[]{:S(2)}) collective-permute-start(bf16[128,5504]{1,0:T(8,128)(2,1)S(1)} %broadcast_select_fusion.3), channel_id=1, source_target_pairs={{16,24},{18,26},{20,28},{22,30},{8,0},{10,2},{12,4},{14,6},{17,25}... | collective-permute-start | bytes 4227080 | tf_op jit(solution)/shard_map/ppermute | solution.py:40
  106.5 18.7 %collective-permute-start.16 = (bf16[128,2560]{1,0:T(8,128)(2,1)S(1)}, bf16[128,2560]{1,0:T(8,128)(2,1)S(1)}, u32[]{:S(2)}, u32[]{:S(2)}) collective-permute-start(bf16[128,2560]{1,0:T(8,128)(2,1)S(1)} %get-tuple-element.48), channel_id=1, source_target_pairs={{24,16},{26,18},{28,20},{30,22},{16,8},{18,10},{20,12},{22,14},{25... | collective-permute-start | bytes 1966088 | tf_op jit(solution)/shard_map/ppermute | solution.py:40
  107.7 19.5 %collective-permute-start.15 = (bf16[128,2560]{1,0:T(8,128)(2,1)S(1)}, bf16[128,2560]{1,0:T(8,128)(2,1)S(1)}, u32[]{:S(2)}, u32[]{:S(2)}) collective-permute-start(bf16[128,2560]{1,0:T(8,128)(2,1)S(1)} %get-tuple-element.47), channel_id=1, source_target_pairs={{0,8},{2,10},{4,12},{6,14},{8,16},{10,18},{12,20},{14,22},{1,9},{3... | collective-permute-start | bytes 1966088 | tf_op jit(solution)/shard_map/ppermute | solution.py:40
  117.7 25.6 %copy-start.8 = (bf16[128,5504]{1,0:T(8,128)(2,1)S(1)}, bf16[128,5504]{1,0:T(8,128)(2,1)}, u32[]{:S(2)}) copy-start(bf16[128,5504]{1,0:T(8,128)(2,1)} %copy-done.7) | copy-start | bytes 4227076
  117.7 25.6 %collective-permute-start.17 = (bf16[128,2944]{1,0:T(8,128)(2,1)S(1)}, bf16[128,2944]{1,0:T(8,128)(2,1)S(1)}, u32[]{:S(2)}, u32[]{:S(2)}) collective-permute-start(bf16[128,2944]{1,0:T(8,128)(2,1)S(1)} %broadcast_select_fusion.4), channel_id=1, source_target_pairs={{0,8},{2,10},{4,12},{6,14},{24,16},{26,18},{28,20},{30,22},{1,9},{... | collective-permute-start | bytes 2261000 | tf_op jit(solution)/shard_map/ppermute | solution.py:40
  127.5 29.1 %collective-permute-start.18 = (bf16[128,2560]{1,0:T(8,128)(2,1)S(1)}, bf16[128,2560]{1,0:T(8,128)(2,1)S(1)}, u32[]{:S(2)}, u32[]{:S(2)}) collective-permute-start(bf16[128,2560]{1,0:T(8,128)(2,1)S(1)} %get-tuple-element.81), channel_id=1, source_target_pairs={{0,8},{2,10},{4,12},{6,14},{8,16},{10,18},{12,20},{14,22},{16,24},... | collective-permute-start | bytes 1966088 | tf_op jit(solution)/shard_map/ppermute | solution.py:40
  131.0 26.5 %collective-permute-start.19 = (bf16[128,2560]{1,0:T(8,128)(2,1)S(1)}, bf16[128,2560]{1,0:T(8,128)(2,1)S(1)}, u32[]{:S(2)}, u32[]{:S(2)}) collective-permute-start(bf16[128,2560]{1,0:T(8,128)(2,1)S(1)} %get-tuple-element.80), channel_id=1, source_target_pairs={{24,16},{26,18},{28,20},{30,22},{16,8},{18,10},{20,12},{22,14},{8,... | collective-permute-start | bytes 1966088 | tf_op jit(solution)/shard_map/ppermute | solution.py:40
  158.4 10.9 %collective-permute-start.20 = (bf16[5504,512]{1,0:T(8,128)(2,1)}, bf16[5504,512]{1,0:T(8,128)(2,1)}, u32[]{:S(2)}, u32[]{:S(2)}) collective-permute-start(bf16[5504,512]{1,0:T(8,128)(2,1)} %convolution_convert_fusion), channel_id=1, source_target_pairs={{0,2},{2,0},{4,6},{6,4},{8,10},{10,8},{12,14},{14,12},{16,18},{18,... | collective-permute-start | bytes 16908296 | tf_op jit(solution)/shard_map/ppermute | solution.py:32
  158.4 8.0 %copy-start.11 = (bf16[128,5504]{1,0:T(8,128)(2,1)S(1)}, bf16[128,5504]{1,0:T(8,128)(2,1)}, u32[]{:S(2)}) copy-start(bf16[128,5504]{1,0:T(8,128)(2,1)} %copy-done.9) | copy-start | bytes 4227076
  158.4 8.0 %copy-start.13 = (bf16[128,5504]{1,0:T(8,128)(2,1)S(1)}, bf16[128,5504]{1,0:T(8,128)(2,1)}, u32[]{:S(2)}) copy-start(bf16[128,5504]{1,0:T(8,128)(2,1)} %copy-done.12) | copy-start | bytes 4227076
  160.0 22.1 %collective-permute-start.22 = (bf16[128,2944]{1,0:T(8,128)(2,1)S(1)}, bf16[128,2944]{1,0:T(8,128)(2,1)S(1)}, u32[]{:S(2)}, u32[]{:S(2)}) collective-permute-start(bf16[128,2944]{1,0:T(8,128)(2,1)S(1)} %get-tuple-element.59), channel_id=1, source_target_pairs={{24,16},{26,18},{28,20},{30,22},{16,8},{18,10},{20,12},{22,14},{25... | collective-permute-start | bytes 2261000 | tf_op jit(solution)/shard_map/ppermute | solution.py:40
  161.3 8.0 %copy-start.15 = (bf16[128,5504]{1,0:T(8,128)(2,1)S(1)}, bf16[128,5504]{1,0:T(8,128)(2,1)}, u32[]{:S(2)}) copy-start(bf16[128,5504]{1,0:T(8,128)(2,1)} %copy-done.14) | copy-start | bytes 4227076
  161.3 8.0 %copy-start.17 = (bf16[128,5504]{1,0:T(8,128)(2,1)S(1)}, bf16[128,5504]{1,0:T(8,128)(2,1)}, u32[]{:S(2)}) copy-start(bf16[128,5504]{1,0:T(8,128)(2,1)} %copy-done.16) | copy-start | bytes 4227076
  161.4 8.0 %copy-start.21 = (bf16[3,128,1024]{2,1,0:T(8,128)(2,1)S(1)}, bf16[3,128,1024]{2,1,0:T(8,128)(2,1)}, u32[]{:S(2)}) copy-start(bf16[3,128,1024]{2,1,0:T(8,128)(2,1)} %copy-done.19) | copy-start | bytes 2359300
  161.4 22.5 %collective-permute-start.21 = (bf16[128,2944]{1,0:T(8,128)(2,1)S(1)}, bf16[128,2944]{1,0:T(8,128)(2,1)S(1)}, u32[]{:S(2)}, u32[]{:S(2)}) collective-permute-start(bf16[128,2944]{1,0:T(8,128)(2,1)S(1)} %get-tuple-element.58), channel_id=1, source_target_pairs={{0,8},{2,10},{4,12},{6,14},{8,16},{10,18},{12,20},{14,22},{1,9},{3... | collective-permute-start | bytes 2261000 | tf_op jit(solution)/shard_map/ppermute | solution.py:40
  175.1 63.1 %collective-permute-start.27 = (bf16[5504,256]{1,0:T(8,128)(2,1)}, bf16[5504,256]{1,0:T(8,128)(2,1)S(1)}, u32[]{:S(2)}, u32[]{:S(2)}) collective-permute-start(bf16[5504,256]{1,0:T(8,128)(2,1)} %add_convert_fusion), channel_id=1, source_target_pairs={{0,4},{2,6},{4,0},{6,2},{8,12},{10,14},{12,8},{14,10},{16,20},{18,... | collective-permute-start | bytes 8454152 | tf_op jit(solution)/shard_map/ppermute | solution.py:32
  189.4 9.5 %copy-start.5 = (bf16[128,5504]{1,0:T(8,128)(2,1)S(1)}, bf16[128,5504]{1,0:T(8,128)(2,1)}, u32[]{:S(2)}) copy-start(bf16[128,5504]{1,0:T(8,128)(2,1)} %param.5) | copy-start | bytes 4227076
  189.4 9.5 %copy-start.6 = (bf16[128,5504]{1,0:T(8,128)(2,1)S(1)}, bf16[128,5504]{1,0:T(8,128)(2,1)}, u32[]{:S(2)}) copy-start(bf16[128,5504]{1,0:T(8,128)(2,1)} %param.4) | copy-start | bytes 4227076
  189.4 9.5 %copy-start.27 = (bf16[128,2560]{1,0:T(8,128)(2,1)S(1)}, bf16[128,2560]{1,0:T(8,128)(2,1)}, u32[]{:S(2)}) copy-start(bf16[128,2560]{1,0:T(8,128)(2,1)} %copy-done.26) | copy-start | bytes 1966084
  189.4 9.5 %copy-start.29 = (bf16[128,2560]{1,0:T(8,128)(2,1)S(1)}, bf16[128,2560]{1,0:T(8,128)(2,1)}, u32[]{:S(2)}) copy-start(bf16[128,2560]{1,0:T(8,128)(2,1)} %copy-done.28) | copy-start | bytes 1966084
  189.4 9.3 %collective-permute-start.23 = (bf16[128,1024]{1,0:T(8,128)(2,1)S(1)}, bf16[128,1024]{1,0:T(8,128)(2,1)S(1)}, u32[]{:S(2)}, u32[]{:S(2)}) collective-permute-start(bf16[128,1024]{1,0:T(8,128)(2,1)S(1)} %get-tuple-element.91), channel_id=1, source_target_pairs={{0,8},{2,10},{4,12},{6,14},{8,16},{10,18},{12,20},{14,22},{16,24},... | collective-permute-start | bytes 786440 | tf_op jit(solution)/shard_map/ppermute | solution.py:36
  191.1 41.1 %collective-permute-start.28 = (bf16[128,2944]{1,0:T(8,128)(2,1)S(1)}, bf16[128,2944]{1,0:T(8,128)(2,1)S(1)}, u32[]{:S(2)}, u32[]{:S(2)}) collective-permute-start(bf16[128,2944]{1,0:T(8,128)(2,1)S(1)} %get-tuple-element.67), channel_id=1, source_target_pairs={{0,8},{2,10},{4,12},{6,14},{8,16},{10,18},{12,20},{14,22},{16,24},... | collective-permute-start | bytes 2261000 | tf_op jit(solution)/shard_map/ppermute | solution.py:40
  193.1 39.1 %collective-permute-start.29 = (bf16[128,2944]{1,0:T(8,128)(2,1)S(1)}, bf16[128,2944]{1,0:T(8,128)(2,1)S(1)}, u32[]{:S(2)}, u32[]{:S(2)}) collective-permute-start(bf16[128,2944]{1,0:T(8,128)(2,1)S(1)} %get-tuple-element.69), channel_id=1, source_target_pairs={{24,16},{26,18},{28,20},{30,22},{16,8},{18,10},{20,12},{22,14},{8,... | collective-permute-start | bytes 2261000 | tf_op jit(solution)/shard_map/ppermute | solution.py:40
  197.0 31.9 %collective-permute-start.24 = (bf16[128,1024]{1,0:T(8,128)(2,1)S(1)}, bf16[128,1024]{1,0:T(8,128)(2,1)S(1)}, u32[]{:S(2)}, u32[]{:S(2)}) collective-permute-start(bf16[128,1024]{1,0:T(8,128)(2,1)S(1)} %get-tuple-element.90), channel_id=1, source_target_pairs={{0,16},{2,18},{4,20},{6,22},{8,24},{10,26},{12,28},{14,30},{16,0},... | collective-permute-start | bytes 786440 | tf_op jit(solution)/shard_map/ppermute | solution.py:36
  198.7 31.7 %collective-permute-start.25 = (bf16[128,1024]{1,0:T(8,128)(2,1)S(1)}, bf16[128,1024]{1,0:T(8,128)(2,1)S(1)}, u32[]{:S(2)}, u32[]{:S(2)}) collective-permute-start(bf16[128,1024]{1,0:T(8,128)(2,1)S(1)} %get-tuple-element.61), channel_id=1, source_target_pairs={{0,24},{2,26},{4,28},{6,30},{8,0},{10,2},{12,4},{14,6},{16,8},{18,... | collective-permute-start | bytes 786440 | tf_op jit(solution)/shard_map/ppermute | solution.py:36
  230.6 12.7 %collective-permute-start.26 = (bf16[128,2048]{1,0:T(8,128)(2,1)S(1)}, bf16[128,2048]{1,0:T(8,128)(2,1)S(1)}, u32[]{:S(2)}, u32[]{:S(2)}) collective-permute-start(bf16[128,2048]{1,0:T(8,128)(2,1)S(1)} %pad_maximum_fusion.20), channel_id=1, source_target_pairs={{0,1},{1,0},{2,3},{3,2},{4,5},{5,4},{6,7},{7,6},{8,9},{9,8},{10,11... | collective-permute-start | bytes 1572872 | tf_op jit(solution)/shard_map/ppermute | solution.py:49
  (14 other events, 35.0 us)
